TPU v7x, 32 devices: a whole 2x2x4 slice. The times are simulated.
32 devices in a mesh: dp: 8 (over z, x), mp: 4 (over y, core).
Axes of the slice: x: 2, y: 2, z: 4, core: 2. Of those that a mesh axis runs over, the one named last changes fastest.
Arguments:
- latent: bfloat16 [262144, 256], P(('dp', 'mp')), may hold values from -6 to 6
- chance_code: int32 [262144], P(('dp', 'mp')), may hold values from 0 to 31
- importance: int32 [262144], P(('dp', 'mp')), may hold values from 21 to 2835
- value_bin: int32 [262144], P(('dp', 'mp')), may hold values from 0 to 600
- reward_bin: int32 [262144], P(('dp', 'mp')), may hold values from 0 to 600
- action_taken: int32 [262144], P(('dp', 'mp')), may hold values from 0 to 3
- code_target: int32 [262144], P(('dp', 'mp')), may hold values from 0 to 31
- stem_weight: float32 [256, 256], P('mp', 'dp'), may hold values from -0.375 to 0.375
- stem_moment: float32 [256, 256], P('mp', 'dp'), may hold values from -2.5 to 2.5
- stem_square: float32 [256, 256], P('mp', 'dp'), may hold values from 0.026 to 0.104
- up_weight: float32 [4, 256, 256], P(None, 'dp', 'mp'), may hold values from -0.5 to 0.5
- up_moment: float32 [4, 256, 256], P(None, 'dp', 'mp'), may hold values from -2.5 to 2.5
- up_square: float32 [4, 256, 256], P(None, 'dp', 'mp'), may hold values from 0.026 to 0.104
- down_weight: float32 [4, 256, 256], P(None, 'mp', 'dp'), may hold values from -0.5 to 0.5
- down_moment: float32 [4, 256, 256], P(None, 'mp', 'dp'), may hold values from -2.5 to 2.5
- down_square: float32 [4, 256, 256], P(None, 'mp', 'dp'), may hold values from 0.026 to 0.104
- head_weight: float32 [256, 1238], P(('dp', 'mp')), may hold values from -0.75 to 0.75
- head_moment: float32 [256, 1238], P(('dp', 'mp')), may hold values from -2.5 to 2.5
- head_square: float32 [256, 1238], P(('dp', 'mp')), may hold values from 0.026 to 0.104
- chance_table: float32 [32, 256], P(None, ('dp', 'mp')), may hold values from -1.8 to 1.8
- table_moment: float32 [32, 256], P(None, ('dp', 'mp')), may hold values from -2.5 to 2.5
- table_square: float32 [32, 256], P(None, ('dp', 'mp')), may hold values from 0.026 to 0.104
- norm_params: float32 [5, 2, 256], P(None, None, ('dp', 'mp')), may hold values from -1.5 to 2.5
- norm_moment: float32 [5, 2, 256], P(None, None, ('dp', 'mp')), may hold values from -4 to 4
- norm_square: float32 [5, 2, 256], P(None, None, ('dp', 'mp')), may hold values from 0.23428571 to 0.9342857
Outputs:
- grad_norm: float32 [], replicated
- latent_grad: float32 [262144, 256], P(('dp', 'mp'))
- new_stem: float32 [256, 256], P('mp', 'dp')
- stem_first: float32 [256, 256], P('mp', 'dp')
- stem_second: float32 [256, 256], P('mp', 'dp')
- stem_copy: bfloat16 [256, 256], P('mp', 'dp')
- new_up: float32 [4, 256, 256], P(None, 'dp', 'mp')
- up_first: float32 [4, 256, 256], P(None, 'dp', 'mp')
- up_second: float32 [4, 256, 256], P(None, 'dp', 'mp')
- up_copy: bfloat16 [4, 256, 256], P(None, 'dp', 'mp')
- new_down: float32 [4, 256, 256], P(None, 'mp', 'dp')
- down_first: float32 [4, 256, 256], P(None, 'mp', 'dp')
- down_second: float32 [4, 256, 256], P(None, 'mp', 'dp')
- down_copy: bfloat16 [4, 256, 256], P(None, 'mp', 'dp')
- new_head: float32 [256, 1238], P(('dp', 'mp'))
- head_first: float32 [256, 1238], P(('dp', 'mp'))
- head_second: float32 [256, 1238], P(('dp', 'mp'))
- head_copy: bfloat16 [256, 1238], P(('dp', 'mp'))
- new_table: float32 [32, 256], P(None, ('dp', 'mp'))
- table_first: float32 [32, 256], P(None, ('dp', 'mp'))
- table_second: float32 [32, 256], P(None, ('dp', 'mp'))
- table_copy: bfloat16 [32, 256], P(None, ('dp', 'mp'))
- new_norms: float32 [5, 2, 256], P(None, None, ('dp', 'mp'))
- norms_first: float32 [5, 2, 256], P(None, None, ('dp', 'mp'))
- norms_second: float32 [5, 2, 256], P(None, None, ('dp', 'mp'))
All inputs are finite; a program needn't handle non-finite values.
Results may differ from a plain program's by a relative error of at most 0.0055.
The roundings to bfloat16 on the way count: a program that leaves them out, or rounds other values in their place, can miss the bound.
Values may be sent and summed in bfloat16 or wider, within the bound.
A program may use at most 256 MiB of HBM per device.

v0:
```python
import math

import jax
import jax.numpy as jnp
from jax import lax
from jax.sharding import PartitionSpec as P

D = 256
BINS = 601
ACTIONS = 4
CODES = 32
LAYERS = 4
STEP = 10


beta_one = 0.9
beta_two = 0.99
eps_adam = 1e-08
eps_norm = 1e-05
matrix_rate = 0.2
vector_rate = 0.6
decay_rate = 0.1
clip_scale = 3.0


def layer_norm(stream, gain, shift):
    centered = stream - jnp.mean(stream, axis=-1, keepdims=True)
    spread = jnp.mean(centered * centered, axis=-1, keepdims=True)
    return centered * lax.rsqrt(spread + eps_norm) * gain + shift


def normed(stream, gain, shift):
    return jax.nn.gelu(layer_norm(stream, gain, shift))


def contract_rows(left, right):
    return lax.dot_general(
        left, right, (((0,), (0,)), ((), ())), preferred_element_type=jnp.float32
    )


def contract_cols(left, right):
    return lax.dot_general(
        left, right, (((1,), (1,)), ((), ())), preferred_element_type=jnp.float32
    )


def adamw(weight, moment, square, grad, rate, decay):
    first = beta_one * moment + (1.0 - beta_one) * grad
    second = beta_two * square + (1.0 - beta_two) * grad * grad
    first_hat = first / (1.0 - beta_one**STEP)
    second_hat = second / (1.0 - beta_two**STEP)
    updated = weight - rate * (first_hat / (jnp.sqrt(second_hat) + eps_adam) + decay * weight)
    return (updated, first, second)


def logit_grads(logits, coef_rows, value_rows, reward_rows, action_rows, target_rows):
    col_bounds = (
        (0, BINS),
        (BINS, 2 * BINS),
        (2 * BINS, 2 * BINS + ACTIONS),
        (2 * BINS + ACTIONS, 2 * BINS + ACTIONS + CODES),
    )
    targets_all = (value_rows, reward_rows, action_rows, target_rows)
    pieces_out = []
    for bound_pair, target in zip(col_bounds, targets_all):
        section = logits[:, bound_pair[0] : bound_pair[1]]
        softened = jax.nn.softmax(section, axis=1)
        target_hot = (
            target[:, None] == jnp.arange(bound_pair[1] - bound_pair[0], dtype=jnp.int32)[None, :]
        ).astype(jnp.float32)
        pieces_out.append((softened - target_hot) * coef_rows[:, None])
    return jnp.concatenate(pieces_out, axis=1)


def square_sum(arrays):
    return jnp.sum(jnp.stack([jnp.sum(member * member) for member in arrays]))


def body(
    latent,
    chance_code,
    importance,
    value_bin,
    reward_bin,
    action_taken,
    code_target,
    stem_weight,
    stem_moment,
    stem_square,
    up_weight,
    up_moment,
    up_square,
    down_weight,
    down_moment,
    down_square,
    head_weight,
    head_moment,
    head_square,
    chance_table,
    table_moment,
    table_square,
    norm_params,
    norm_moment,
    norm_square,
):
    own_rows = chance_code.shape[0]
    total_rows = own_rows * lax.axis_size(("dp", "mp"))
    weight_values = importance.astype(jnp.float32)
    weight_total = lax.psum(jnp.sum(weight_values), ("dp", "mp"))
    coef = weight_values * (total_rows / weight_total)
    stem_rows, up_rows, down_rows = (
        lax.all_gather(stem_weight.astype(jnp.bfloat16), "dp", axis=1, tiled=True),
        lax.all_gather(up_weight.astype(jnp.bfloat16), "dp", axis=1, tiled=True),
        lax.all_gather(down_weight.astype(jnp.bfloat16), "dp", axis=2, tiled=True),
    )
    stem_full, up_full, down_full = (
        lax.all_gather(stem_rows, "mp", axis=0, tiled=True),
        lax.all_gather(up_rows, "mp", axis=2, tiled=True),
        lax.all_gather(down_rows, "mp", axis=1, tiled=True),
    )
    head_full, table_full, norm_full = (
        lax.all_gather(head_weight.astype(jnp.bfloat16), ("dp", "mp"), axis=0, tiled=True),
        lax.all_gather(chance_table.astype(jnp.bfloat16), ("dp", "mp"), axis=1, tiled=True),
        lax.all_gather(norm_params.astype(jnp.bfloat16), ("dp", "mp"), axis=2, tiled=True),
    )
    norm_values = norm_full.astype(jnp.float32)
    code_hot = chance_code[:, None] == jnp.arange(CODES, dtype=jnp.int32)[None, :]
    pre_stem = jnp.dot(latent, stem_full, preferred_element_type=jnp.float32)
    pre_stem = pre_stem + jnp.dot(
        code_hot.astype(jnp.bfloat16), table_full, preferred_element_type=jnp.float32
    )
    stream = normed(pre_stem, norm_values[0, 0], norm_values[0, 1])
    saved = [stream]
    for layer_idx in range(LAYERS):
        active = normed(
            stream, norm_values[layer_idx + 1, 0], norm_values[layer_idx + 1, 1]
        ).astype(jnp.bfloat16)
        inner = jnp.dot(active, up_full[layer_idx], preferred_element_type=jnp.float32)
        gated = jax.nn.gelu(inner).astype(jnp.bfloat16)
        stream = stream + jnp.dot(gated, down_full[layer_idx], preferred_element_type=jnp.float32)
        saved.append(stream)
    top = stream.astype(jnp.bfloat16)
    block_rows = math.gcd(own_rows, 2048)
    block_count = own_rows // block_rows

    def head_step(head_grad, pieces):
        top_rows, coef_rows, value_rows, reward_rows, action_rows, target_rows = pieces
        logits = jnp.dot(top_rows, head_full, preferred_element_type=jnp.float32)
        logit_low = logit_grads(
            logits, coef_rows, value_rows, reward_rows, action_rows, target_rows
        ).astype(jnp.bfloat16)
        head_grad = head_grad + contract_rows(top_rows, logit_low)
        return (head_grad, contract_cols(logit_low, head_full))

    pieces_all = tuple(
        (
            member.reshape((block_count, block_rows) + member.shape[1:])
            for member in (top, coef, value_bin, reward_bin, action_taken, code_target)
        )
    )
    head_grad, top_grads = lax.scan(head_step, jnp.zeros(head_full.shape, jnp.float32), pieces_all)
    grad_stream = top_grads.reshape(own_rows, D)
    up_list = [None] * LAYERS
    down_list = [None] * LAYERS
    norm_list = [None] * (LAYERS + 1)
    for layer_idx in reversed(range(LAYERS)):
        active_f, norm_back = jax.vjp(
            normed, saved[layer_idx], norm_values[layer_idx + 1, 0], norm_values[layer_idx + 1, 1]
        )
        active = active_f.astype(jnp.bfloat16)
        inner = jnp.dot(active, up_full[layer_idx], preferred_element_type=jnp.float32)
        gated_f, gelu_back = jax.vjp(jax.nn.gelu, inner)
        gated = gated_f.astype(jnp.bfloat16)
        branch_grad = grad_stream.astype(jnp.bfloat16)
        down_list[layer_idx] = contract_rows(gated, branch_grad)
        gated_grad = contract_cols(branch_grad, down_full[layer_idx])
        inner_grad = gelu_back(gated_grad)[0].astype(jnp.bfloat16)
        up_list[layer_idx] = contract_rows(active, inner_grad)
        active_grad = contract_cols(inner_grad, up_full[layer_idx])
        stream_part, gain_grad, shift_grad = norm_back(active_grad)
        grad_stream = grad_stream + stream_part
        norm_list[layer_idx + 1] = jnp.stack([gain_grad, shift_grad], axis=0)
    unused, stem_back = jax.vjp(normed, pre_stem, norm_values[0, 0], norm_values[0, 1])
    pre_grad, gain_grad, shift_grad = stem_back(grad_stream)
    norm_list[0] = jnp.stack([gain_grad, shift_grad], axis=0)
    table_grad = lax.dot_general(
        code_hot.astype(jnp.float32),
        pre_grad,
        (((0,), (0,)), ((), ())),
        precision=lax.Precision.HIGHEST,
        preferred_element_type=jnp.float32,
    )
    pre_low = pre_grad.astype(jnp.bfloat16)
    stem_grad = contract_rows(latent, pre_low)
    latent_grad = contract_cols(pre_low, stem_full)
    up_grad = jnp.stack(up_list, axis=0)
    down_grad = jnp.stack(down_list, axis=0)
    norm_grad = jnp.stack(norm_list, axis=0)
    data_index = lax.axis_index("dp")
    model_index = lax.axis_index("mp")
    all_index = lax.axis_index(("dp", "mp"))
    summed = lax.psum(
        (stem_grad, up_grad, down_grad, head_grad, table_grad, norm_grad), ("dp", "mp")
    )
    grad_norm = jnp.sqrt(square_sum(summed))
    stem_own = lax.dynamic_slice(
        summed[0],
        (model_index * stem_weight.shape[0], data_index * stem_weight.shape[1]),
        stem_weight.shape,
    )
    up_own = lax.dynamic_slice_in_dim(
        lax.dynamic_slice_in_dim(summed[1], data_index * up_weight.shape[1], up_weight.shape[1], 1),
        model_index * up_weight.shape[2],
        up_weight.shape[2],
        2,
    )
    down_own = lax.dynamic_slice_in_dim(
        lax.dynamic_slice_in_dim(
            summed[2], model_index * down_weight.shape[1], down_weight.shape[1], 1
        ),
        data_index * down_weight.shape[2],
        down_weight.shape[2],
        2,
    )
    head_own = lax.dynamic_slice_in_dim(
        summed[3], all_index * head_weight.shape[0], head_weight.shape[0], 0
    )
    table_own = lax.dynamic_slice_in_dim(
        summed[4], all_index * chance_table.shape[1], chance_table.shape[1], 1
    )
    norm_own = lax.dynamic_slice_in_dim(
        summed[5], all_index * norm_params.shape[2], norm_params.shape[2], 2
    )
    ratio = jnp.minimum(1.0, clip_scale * math.sqrt(total_rows) / grad_norm)
    stem_new, stem_first, stem_second = adamw(
        stem_weight, stem_moment, stem_square, stem_own * ratio, matrix_rate, decay_rate
    )
    up_new, up_first, up_second = adamw(
        up_weight, up_moment, up_square, up_own * ratio, matrix_rate, decay_rate
    )
    down_new, down_first, down_second = adamw(
        down_weight, down_moment, down_square, down_own * ratio, matrix_rate, decay_rate
    )
    head_new, head_first, head_second = adamw(
        head_weight, head_moment, head_square, head_own * ratio, matrix_rate, decay_rate
    )
    table_new, table_first, table_second = adamw(
        chance_table, table_moment, table_square, table_own * ratio, matrix_rate, decay_rate
    )
    norms_new, norms_first, norms_second = adamw(
        norm_params, norm_moment, norm_square, norm_own * ratio, vector_rate, 0.0
    )
    return (
        grad_norm,
        latent_grad,
        stem_new,
        stem_first,
        stem_second,
        stem_new.astype(jnp.bfloat16),
        up_new,
        up_first,
        up_second,
        up_new.astype(jnp.bfloat16),
        down_new,
        down_first,
        down_second,
        down_new.astype(jnp.bfloat16),
        head_new,
        head_first,
        head_second,
        head_new.astype(jnp.bfloat16),
        table_new,
        table_first,
        table_second,
        table_new.astype(jnp.bfloat16),
        norms_new,
        norms_first,
        norms_second,
    )


def solution(mesh):
    in_specs = (
        P(("dp", "mp"), None),
        P(("dp", "mp")),
        P(("dp", "mp")),
        P(("dp", "mp")),
        P(("dp", "mp")),
        P(("dp", "mp")),
        P(("dp", "mp")),
        P("mp", "dp"),
        P("mp", "dp"),
        P("mp", "dp"),
        P(None, "dp", "mp"),
        P(None, "dp", "mp"),
        P(None, "dp", "mp"),
        P(None, "mp", "dp"),
        P(None, "mp", "dp"),
        P(None, "mp", "dp"),
        P(("dp", "mp"), None),
        P(("dp", "mp"), None),
        P(("dp", "mp"), None),
        P(None, ("dp", "mp")),
        P(None, ("dp", "mp")),
        P(None, ("dp", "mp")),
        P(None, None, ("dp", "mp")),
        P(None, None, ("dp", "mp")),
        P(None, None, ("dp", "mp")),
    )
    out_specs = (
        P(),
        P(("dp", "mp"), None),
        P("mp", "dp"),
        P("mp", "dp"),
        P("mp", "dp"),
        P("mp", "dp"),
        P(None, "dp", "mp"),
        P(None, "dp", "mp"),
        P(None, "dp", "mp"),
        P(None, "dp", "mp"),
        P(None, "mp", "dp"),
        P(None, "mp", "dp"),
        P(None, "mp", "dp"),
        P(None, "mp", "dp"),
        P(("dp", "mp"), None),
        P(("dp", "mp"), None),
        P(("dp", "mp"), None),
        P(("dp", "mp"), None),
        P(None, ("dp", "mp")),
        P(None, ("dp", "mp")),
        P(None, ("dp", "mp")),
        P(None, ("dp", "mp")),
        P(None, None, ("dp", "mp")),
        P(None, None, ("dp", "mp")),
        P(None, None, ("dp", "mp")),
    )
    return jax.shard_map(body, mesh=mesh, in_specs=in_specs, out_specs=out_specs, check_vma=False)
```

profile of v0, /device:TPU:0, one launch (start us, length us, event | category | flops | bytes accessed | tf_op | source)
XLA Modules:
  0.0 931.4 jit_solution(15877704444050464051)
XLA Ops:
  8.6 42.2 %psum.49 = f32[]{:T(128)} all-reduce(f32[]{:T(128)} %convert_reduce_fusion), channel_id=1, replica_groups=mesh['dp'=8,'mp'=4] {'dp','mp'}, use_global_device_ids=true, to_apply=%region_11.0 | all-reduce | flops 1 | bytes 8 | tf_op jit(solution)/shard_map/psum | solution.py:110
  60.8 30.5 %all_gather.27 = bf16[64,256]{0,1:T(8,128)(2,1)S(1)} all-gather(bf16[64,32]{0,1:T(8,128)(2,1)S(1)} %convert_element_type.121), channel_id=1, replica_groups=mesh['dp'=8,'mp'=4] {'dp'}, dimensions={1}, use_global_device_ids=true | all-gather | bytes 36864 | tf_op jit(solution)/shard_map/all_gather | solution.py:113
  91.4 40.6 %all_gather.29 = bf16[32,256]{0,1:T(8,128)(2,1)S(1)} all-gather(bf16[32,8]{0,1:T(8,128)(2,1)S(1)} %convert_element_type.122), channel_id=1, replica_groups=mesh['dp'=8,'mp'=4] {'dp','mp'}, dimensions={1}, use_global_device_ids=true | all-gather | bytes 16896 | tf_op jit(solution)/shard_map/all_gather | solution.py:124
  131.9 5.4 all_gather.28
  137.4 37.0 %all_gather.30 = bf16[5,2,256]{0,1,2:T(2,128)(2,1)S(1)} all-gather(bf16[5,2,8]{0,1,2:T(2,128)(2,1)S(1)} %copy.180), channel_id=1, replica_groups=mesh['dp'=8,'mp'=4] {'dp','mp'}, dimensions={2}, use_global_device_ids=true | all-gather | bytes 5280 | tf_op jit(solution)/shard_map/all_gather | solution.py:125
  174.4 9.7 %slice_reduce_fusion.5 = (f32[256]{0:T(256)}, f32[256]{0:T(256)}, f32[256]{0:T(256)S(1)}, f32[256]{0:T(256)S(1)}, f32[256]{0:T(256)S(1)}, /*index=5*/f32[256]{0:...) fusion(f32[5,2,256]{0,1,2:T(2,128)S(1)} %convert_element_type.124), kind=kLoop, calls=%fused_computation.192 | loop fusion | bytes 20480 | tf_op jit(solution)/shard_map/slice | solution.py:137
  184.1 30.7 %all_gather.33 = bf16[4,64,256]{1,0,2:T(4,128)(2,1)S(1)} all-gather(bf16[4,64,32]{1,0,2:T(4,128)(2,1)S(1)} %copy.228), channel_id=1, replica_groups=mesh['dp'=8,'mp'=4] {'dp'}, dimensions={2}, use_global_device_ids=true | all-gather | bytes 147456 | tf_op jit(solution)/shard_map/all_gather | solution.py:115
  215.1 30.7 %all_gather.31 = bf16[4,256,64]{2,0,1:T(4,128)(2,1)S(1)} all-gather(bf16[4,32,64]{2,0,1:T(4,128)(2,1)S(1)} %copy.229), channel_id=1, replica_groups=mesh['dp'=8,'mp'=4] {'dp'}, dimensions={1}, use_global_device_ids=true | all-gather | bytes 147456 | tf_op jit(solution)/shard_map/all_gather | solution.py:114
  246.0 7.4 all_gather.32
  253.4 7.5 all_gather.34
  263.7 39.0 %all_gather.35 = bf16[256,1238]{1,0:T(8,128)(2,1)S(1)} all-gather(bf16[8,1238]{1,0:T(8,128)(2,1)S(1)} %convert_element_type.136), channel_id=1, replica_groups=mesh['dp'=8,'mp'=4] {'dp','mp'}, dimensions={0}, use_global_device_ids=true | all-gather | bytes 653664 | tf_op jit(solution)/shard_map/all_gather | solution.py:123
  310.5 5.2 fusion.159
  331.2 13.1 %multiply_convert_fusion.9 = bf16[8192,256]{1,0:T(8,128)(2,1)S(1)} fusion(f32[8192,256]{1,0:T(8,128)S(1)} %get-tuple-element.348, f32[256]{0:T(256)S(1)} %get-tuple-element.261, f32[256]{0:T(256)S(1)} %get-tuple-element.262, f32[8192]{0:T(1024)S(1)} %fusion.135, f32[8192]{0:T(1024)S(1)} %broadcast_multiply_fusion.2), kind=kLoop, calls=%fused_computation.146 | loop fusion | flops 27262976 | bytes 12650496 | tf_op jit(solution)/shard_map/convert_element_type | solution.py:138
  364.4 5.5 multiply_convert_fusion.5
  373.4 4.6 fusion.12
  378.0 184.3 %while.13 = (s32[]{:T(128)}, f32[256,1238]{0,1:T(8,128)}, f32[4,2048,256]{2,1,0:T(8,128)}, bf16[4,2048,256]{2,1,0:T(8,128)(2,1)}, bf16[256,1238]{1,0:T(8,128)(2,...) while((s32[]{:T(128)}, f32[256,1238]{0,1:T(8,128)}, ...), condition=%wide.region_21.22_spmd.clone, body=%wide.region_12.21_spmd.clone.sunk | while | flops 3920382976 | bytes 94515384 | solution.py:162
  384.6 4.5 multiply_convert_fusion.23
  389.2 26.0 %concatenate.6 = bf16[2048,1238]{0,1:T(8,128)(2,1)} concatenate(bf16[2048,601]{0,1:T(8,128)(2,1)} %get-tuple-element.434, bf16[2048,601]{0,1:T(8,128)(2,1)S(1)} %get-tuple-element.435, bf16[2048,4]{0,1:T(4,128)(2,1)S(1)} %multiply_convert_fusion.24, bf16[2048,32]{0,1:T(8,128)(2,1)S(1)} %multiply_convert_fusion.25), dimensions={1} | concatenate | bytes 10141696 | tf_op jit(solution)/shard_map/while/body/eval_jaxpr/concatenate | solution.py:73
  415.2 5.4 convolution_add_fusion.7
  435.0 26.0 %concatenate.6 = bf16[2048,1238]{0,1:T(8,128)(2,1)} concatenate(bf16[2048,601]{0,1:T(8,128)(2,1)} %get-tuple-element.434, bf16[2048,601]{0,1:T(8,128)(2,1)S(1)} %get-tuple-element.435, bf16[2048,4]{0,1:T(4,128)(2,1)S(1)} %multiply_convert_fusion.24, bf16[2048,32]{0,1:T(8,128)(2,1)S(1)} %multiply_convert_fusion.25), dimensions={1} | concatenate | bytes 10141696 | tf_op jit(solution)/shard_map/while/body/eval_jaxpr/concatenate | solution.py:73
  461.0 5.8 convolution_add_fusion.7
  481.1 26.0 %concatenate.6 = bf16[2048,1238]{0,1:T(8,128)(2,1)} concatenate(bf16[2048,601]{0,1:T(8,128)(2,1)} %get-tuple-element.434, bf16[2048,601]{0,1:T(8,128)(2,1)S(1)} %get-tuple-element.435, bf16[2048,4]{0,1:T(4,128)(2,1)S(1)} %multiply_convert_fusion.24, bf16[2048,32]{0,1:T(8,128)(2,1)S(1)} %multiply_convert_fusion.25), dimensions={1} | concatenate | bytes 10141696 | tf_op jit(solution)/shard_map/while/body/eval_jaxpr/concatenate | solution.py:73
  507.2 5.8 convolution_add_fusion.7
  527.3 26.0 %concatenate.6 = bf16[2048,1238]{0,1:T(8,128)(2,1)} concatenate(bf16[2048,601]{0,1:T(8,128)(2,1)} %get-tuple-element.434, bf16[2048,601]{0,1:T(8,128)(2,1)S(1)} %get-tuple-element.435, bf16[2048,4]{0,1:T(4,128)(2,1)S(1)} %multiply_convert_fusion.24, bf16[2048,32]{0,1:T(8,128)(2,1)S(1)} %multiply_convert_fusion.25), dimensions={1} | concatenate | bytes 10141696 | tf_op jit(solution)/shard_map/while/body/eval_jaxpr/concatenate | solution.py:73
  553.3 5.8 convolution_add_fusion.7
  562.3 10.9 %bitcast_convert_fusion = (bf16[8192,256]{1,0:T(8,128)(2,1)}, bf16[4,2048,256]{2,1,0:T(8,128)(2,1)}) fusion(f32[4,2048,256]{2,1,0:T(8,128)} %get-tuple-element.78), kind=kLoop, calls=%fused_computation.123 | loop fusion | flops 4194304 | bytes 16777216 | tf_op jit(solution)/shard_map/convert_element_type | solution.py:175
  573.2 8.4 fusion.70
  585.7 12.7 %multiply_reduce_fusion = (f32[256]{0:T(256)}, f32[8192]{0:T(1024)S(1)}, f32[256]{0:T(256)}, f32[8192,256]{1,0:T(8,128)S(1)}) fusion(f32[8192,256]{1,0:T(8,128)S(1)} %bitcast.187, f32[8192]{0:T(1024)S(1)} %copy-done.64, f32[8192]{0:T(1024)S(1)} %copy-done.46, f32[256]{0:T(256)} %get-tuple-element.257, f32[256]{0:T(256)} %get-tuple-element.258, ...), kind=kOutput, calls=%fused_computation.125 | convolution fusion | flops 1134550528 | bytes 21204992 | tf_op jit(solution)/shard_map/dot_general | solution.py:43
  598.4 6.8 fusion.158
  617.1 10.2 %fusion.57 = bf16[8192,256]{1,0:T(8,128)(2,1)} fusion(f32[8192,256]{1,0:T(8,128)S(1)} %bitcast.193, f32[8192,256]{1,0:T(8,128)} %copy-done.19, bf16[1,256,256]{2,0,1:T(2,128)(2,1)S(1)} %copy-done.38), kind=kOutput, calls=%fused_computation.109 | convolution fusion | flops 1117782016 | bytes 21102592 | tf_op jit(solution)/shard_map/dot_general | solution.py:43
  631.9 9.5 %multiply_reduce_fusion.1 = (f32[256]{0:T(256)}, f32[8192]{0:T(1024)S(1)}, f32[256]{0:T(256)}, f32[8192,256]{1,0:T(8,128)S(1)}) fusion(f32[8192,256]{1,0:T(8,128)S(1)} %bitcast.181, f32[8192]{0:T(1024)S(1)} %copy-done.62, f32[8192]{0:T(1024)S(1)} %copy-done.44, f32[256]{0:T(256)S(1)} %copy-done.104, f32[256]{0:T(256)S(1)} %copy-done.114, ...), kind=kOutput, calls=%fused_computation.126 | convolution fusion | flops 1134550528 | bytes 21204992 | tf_op jit(solution)/shard_map/dot_general | solution.py:43
  641.4 6.1 fusion.157
  647.6 6.1 add_add_fusion.6
  653.7 6.9 fusion.95
  660.6 8.6 fusion.44
  670.6 9.1 multiply_reduce_fusion.2
  679.7 6.1 fusion.156
  685.8 6.9 add_add_fusion.5
  699.5 8.6 fusion.31
  709.5 11.1 %multiply_reduce_fusion.3 = (f32[256]{0:T(256)S(1)}, f32[8192]{0:T(1024)S(1)}, f32[256]{0:T(256)S(1)}, f32[8192,256]{1,0:T(8,128)}) fusion(f32[8192,256]{1,0:T(8,128)S(1)} %bitcast.183, f32[8192]{0:T(1024)S(1)} %copy-done.58, f32[8192]{0:T(1024)S(1)} %copy-done.40, f32[256]{0:T(256)S(1)} %copy-done.100, f32[256]{0:T(256)S(1)} %copy-done.110, ...), kind=kOutput, calls=%fused_computation.128 | convolution fusion | flops 1134550528 | bytes 21204992 | tf_op jit(solution)/shard_map/dot_general | solution.py:43
  722.1 8.6 convolution_bitcast_fusion.1
  730.8 7.5 fusion.155
  738.4 12.2 %multiply_reduce_fusion.4 = (f32[256]{0:T(256)S(1)}, f32[8192]{0:T(1024)S(1)}, f32[256]{0:T(256)S(1)}, f32[8192,256]{1,0:T(8,128)S(1)}) fusion(f32[8192,256]{1,0:T(8,128)S(1)} %bitcast.185, f32[8192]{0:T(1024)S(1)} %copy-done.56, f32[8192]{0:T(1024)S(1)} %copy-done.32, f32[256]{0:T(256)S(1)} %copy-done.93, f32[256]{0:T(256)S(1)} %copy-done.98, ...), kind=kLoop, calls=%fused_computation.129 | loop fusion | flops 65003008 | bytes 33689600 | tf_op jit(solution)/shard_map/transpose(jvp())/reduce_sum | solution.py:29
  750.7 5.2 fusion.153
  764.9 11.6 %fusion.71 = f32[32,256]{0,1:T(8,128)S(1)} fusion(f32[8192,256]{1,0:T(8,128)} %copy-done.5, f32[8192]{0:T(1024)S(1)} %negate_multiply_fusion, s32[8192]{0:T(1024)S(1)} %copy-done.83), kind=kOutput, calls=%fused_computation.155 | convolution fusion | flops 807665664 | bytes 8486912 | tf_op jit(solution)/shard_map/dot_general | solution.py:187
  776.5 40.1 %all-reduce = (f32[32,256]{0,1:T(8,128)S(1)}, f32[5,2,256]{2,1,0:T(2,128)S(1)}) all-reduce(f32[32,256]{0,1:T(8,128)S(1)} %fusion.71, f32[5,2,256]{2,1,0:T(2,128)S(1)} %constant_dynamic-update-slice_fusion), channel_id=1, replica_groups=mesh['dp'=8,'mp'=4] {'dp','mp'}, use_global_device_ids=true, to_apply=%region_40.41 | all-reduce | flops 10752 | bytes 86016 | tf_op jit(solution)/shard_map/psum | solution.py:203
  818.1 6.5 fusion.141
  824.6 78.8 %all-reduce.4.cloned.1.call-done = (f32[256,256]{0,1:T(8,128)}, f32[4,256,256]{2,1,0:T(8,128)}, f32[4,256,256]{1,2,0:T(8,128)}, f32[256,1238]{1,0:T(8,128)}) async-done(((f32[256,256]{0,1:T(8,128)}, f32[4,256,256]{2,1,0:T(8,128)}, f32[4,256,256]{1,2,0:T(8,128)}, f32[256,1238]{1,0:T(8,128)}), (f32[256,256]{0,1:T(8,128)}, f32[4,256,256]{2,1,0:T(8,128)}, f32[4,256,256]{1,2,0:T(8,128)}, ...) | async-done | bytes 3627024 | tf_op jit(solution)/shard_map/psum | solution.py:203
  (446 shorter events, 170.3 us)
Async XLA Ops:
  7.2 896.1 %all-reduce.4.cloned.1.call-start = ((), (), s32[]{:S(2)}) async-start(), calls=%async_computation | async-start | bytes 7340032 | tf_op jit(solution)/shard_map/psum | solution.py:203
  137.3 168.8 %copy-start.27 = (bf16[256,256]{1,0:T(8,128)(2,1)}, bf16[256,256]{1,0:T(8,128)(2,1)S(1)}, u32[]{:S(2)}) copy-start(bf16[256,256]{1,0:T(8,128)(2,1)S(1)} %all_gather.28) | copy-start | bytes 393220
  184.1 126.4 %copy-start.92 = (f32[256]{0:T(256)}, f32[256]{0:T(256)S(1)}, u32[]{:S(2)}) copy-start(f32[256]{0:T(256)S(1)} %get-tuple-element.266) | copy-start | bytes 3076
  184.1 126.5 %copy-start.97 = (f32[256]{0:T(256)}, f32[256]{0:T(256)S(1)}, u32[]{:S(2)}) copy-start(f32[256]{0:T(256)S(1)} %get-tuple-element.265) | copy-start | bytes 3076
  184.1 134.1 %copy-start.99 = (f32[256]{0:T(256)}, f32[256]{0:T(256)S(1)}, u32[]{:S(2)}) copy-start(f32[256]{0:T(256)S(1)} %get-tuple-element.264) | copy-start | bytes 3076
  184.1 134.1 %copy-start.109 = (f32[256]{0:T(256)}, f32[256]{0:T(256)S(1)}, u32[]{:S(2)}) copy-start(f32[256]{0:T(256)S(1)} %get-tuple-element.263) | copy-start | bytes 3076
  184.1 147.1 %copy-start.101 = (f32[256]{0:T(256)}, f32[256]{0:T(256)S(1)}, u32[]{:S(2)}) copy-start(f32[256]{0:T(256)S(1)} %get-tuple-element.262) | copy-start | bytes 3076
  184.1 147.1 %copy-start.111 = (f32[256]{0:T(256)}, f32[256]{0:T(256)S(1)}, u32[]{:S(2)}) copy-start(f32[256]{0:T(256)S(1)} %get-tuple-element.261) | copy-start | bytes 3076
  184.1 168.1 %copy-start.103 = (f32[256]{0:T(256)}, f32[256]{0:T(256)S(1)}, u32[]{:S(2)}) copy-start(f32[256]{0:T(256)S(1)} %get-tuple-element.260) | copy-start | bytes 3076
  184.1 168.1 %copy-start.113 = (f32[256]{0:T(256)}, f32[256]{0:T(256)S(1)}, u32[]{:S(2)}) copy-start(f32[256]{0:T(256)S(1)} %get-tuple-element.259) | copy-start | bytes 3076
  262.3 63.1 %copy-start.33 = (bf16[1,256,256]{2,0,1:T(2,128)(2,1)}, bf16[1,256,256]{2,0,1:T(2,128)(2,1)S(1)}, u32[]{:S(2)}) copy-start(bf16[1,256,256]{2,0,1:T(2,128)(2,1)S(1)} %get-tuple-element.344) | copy-start | bytes 393220
  262.3 84.1 %copy-start.35 = (bf16[1,256,256]{2,0,1:T(2,128)(2,1)}, bf16[1,256,256]{2,0,1:T(2,128)(2,1)S(1)}, u32[]{:S(2)}) copy-start(bf16[1,256,256]{2,0,1:T(2,128)(2,1)S(1)} %get-tuple-element.343) | copy-start | bytes 393220
  262.3 96.3 %copy-start.37 = (bf16[1,256,256]{2,0,1:T(2,128)(2,1)}, bf16[1,256,256]{2,0,1:T(2,128)(2,1)S(1)}, u32[]{:S(2)}) copy-start(bf16[1,256,256]{2,0,1:T(2,128)(2,1)S(1)} %get-tuple-element.342) | copy-start | bytes 393220
  263.1 43.1 %copy-start.82 = (s32[8192]{0:T(1024)S(1)}, s32[8192]{0:T(1024)}, u32[]{:S(2)}) copy-start(s32[8192]{0:T(1024)} %param.28) | copy-start | bytes 98308
  263.3 106.7 %copy-start.53 = (bf16[1,256,256]{2,1,0:T(8,128)(2,1)}, bf16[1,256,256]{2,1,0:T(8,128)(2,1)S(1)}, u32[]{:S(2)}) copy-start(bf16[1,256,256]{2,1,0:T(8,128)(2,1)S(1)} %copy.210) | copy-start | bytes 393220
  263.4 93.2 %copy-start.51 = (bf16[1,256,256]{2,1,0:T(8,128)(2,1)}, bf16[1,256,256]{2,1,0:T(8,128)(2,1)S(1)}, u32[]{:S(2)}) copy-start(bf16[1,256,256]{2,1,0:T(8,128)(2,1)S(1)} %copy.208) | copy-start | bytes 393220
  263.6 80.8 %copy-start.49 = (bf16[1,256,256]{2,1,0:T(8,128)(2,1)}, bf16[1,256,256]{2,1,0:T(8,128)(2,1)S(1)}, u32[]{:S(2)}) copy-start(bf16[1,256,256]{2,1,0:T(8,128)(2,1)S(1)} %copy.206) | copy-start | bytes 393220
  263.7 59.7 %copy-start.47 = (bf16[1,256,256]{2,1,0:T(8,128)(2,1)}, bf16[1,256,256]{2,1,0:T(8,128)(2,1)S(1)}, u32[]{:S(2)}) copy-start(bf16[1,256,256]{2,1,0:T(8,128)(2,1)S(1)} %copy.204) | copy-start | bytes 393220
  562.3 23.3 %slice-start.8 = ((s8[8388608]{0:T(1024)(128)(4,1)}), s8[4194304]{0:T(1024)(128)(4,1)S(1)}, s32[]{:S(2)}) async-start(s8[8388608]{0:T(1024)(128)(4,1)} %bitcast.186), calls=%async_computation.9 | async-start | bytes 8388608
  583.6 21.6 %slice-start.18 = ((s8[8388608]{0:T(1024)(128)(4,1)}), s8[4194304]{0:T(1024)(128)(4,1)S(1)}, s32[]{:S(2)}) async-start(s8[8388608]{0:T(1024)(128)(4,1)} %bitcast.196), calls=%async_computation.19 | async-start | bytes 8388608
  583.6 29.3 %slice-start.14 = ((s8[8388608]{0:T(1024)(128)(4,1)}), s8[4194304]{0:T(1024)(128)(4,1)S(1)}, s32[]{:S(2)}) async-start(s8[8388608]{0:T(1024)(128)(4,1)} %bitcast.192), calls=%async_computation.15 | async-start | bytes 8388608
  585.6 19.5 %slice-start.19 = ((s8[8388608]{0:T(1024)(128)(4,1)}), s8[4194304]{0:T(1024)(128)(4,1)S(1)}, s32[]{:S(2)}) async-start(s8[8388608]{0:T(1024)(128)(4,1)} %bitcast.196), calls=%async_computation.20 | async-start | bytes 8388608
  585.6 27.2 %slice-start.15 = ((s8[8388608]{0:T(1024)(128)(4,1)}), s8[4194304]{0:T(1024)(128)(4,1)S(1)}, s32[]{:S(2)}) async-start(s8[8388608]{0:T(1024)(128)(4,1)} %bitcast.192), calls=%async_computation.16 | async-start | bytes 8388608
  612.8 18.9 %slice-start.2 = ((s8[8388608]{0:T(1024)(128)(4,1)}), s8[4194304]{0:T(1024)(128)(4,1)S(1)}, s32[]{:S(2)}) async-start(s8[8388608]{0:T(1024)(128)(4,1)} %bitcast.180), calls=%async_computation.3 | async-start | bytes 8388608
  627.4 20.2 %slice-start.20 = ((s8[8388608]{0:T(1024)(128)(4,1)}), s8[4194304]{0:T(1024)(128)(4,1)S(1)}, s32[]{:S(2)}) async-start(s8[8388608]{0:T(1024)(128)(4,1)} %bitcast.198), calls=%async_computation.21 | async-start | bytes 8388608
  627.4 26.2 %slice-start.12 = ((s8[8388608]{0:T(1024)(128)(4,1)}), s8[4194304]{0:T(1024)(128)(4,1)S(1)}, s32[]{:S(2)}) async-start(s8[8388608]{0:T(1024)(128)(4,1)} %bitcast.190), calls=%async_computation.13 | async-start | bytes 8388608
  631.9 21.8 %slice-start.13 = ((s8[8388608]{0:T(1024)(128)(4,1)}), s8[4194304]{0:T(1024)(128)(4,1)S(1)}, s32[]{:S(2)}) async-start(s8[8388608]{0:T(1024)(128)(4,1)} %bitcast.190), calls=%async_computation.14 | async-start | bytes 8388608
  669.2 26.8 %slice-start.10 = ((s8[8388608]{0:T(1024)(128)(4,1)}), s8[4194304]{0:T(1024)(128)(4,1)S(1)}, s32[]{:S(2)}) async-start(s8[8388608]{0:T(1024)(128)(4,1)} %bitcast.188), calls=%async_computation.11 | async-start | bytes 8388608
  670.6 25.4 %slice-start.11 = ((s8[8388608]{0:T(1024)(128)(4,1)}), s8[4194304]{0:T(1024)(128)(4,1)S(1)}, s32[]{:S(2)}) async-start(s8[8388608]{0:T(1024)(128)(4,1)} %bitcast.188), calls=%async_computation.12 | async-start | bytes 8388608
  762.6 55.3 %copy-start.28 = (bf16[256,256]{1,0:T(8,128)(2,1)S(1)}, bf16[256,256]{1,0:T(8,128)(2,1)}, u32[]{:S(2)}) copy-start(bf16[256,256]{1,0:T(8,128)(2,1)} %copy-done.27) | copy-start | bytes 393220
  817.9 97.5 %copy-start.75 = (f32[4,64,32]{1,2,0:T(8,128)S(1)}, f32[4,64,32]{1,2,0:T(8,128)}, u32[]{:S(2)}) copy-start(f32[4,64,32]{1,2,0:T(8,128)} %param.40) | copy-start | bytes 98308
  817.9 97.5 %copy-start.84 = (f32[4,64,32]{1,2,0:T(8,128)S(1)}, f32[4,64,32]{1,2,0:T(8,128)}, u32[]{:S(2)}) copy-start(f32[4,64,32]{1,2,0:T(8,128)} %param.41) | copy-start | bytes 98308
  817.9 97.5 %copy-start.85 = (f32[4,64,32]{1,2,0:T(8,128)S(1)}, f32[4,64,32]{1,2,0:T(8,128)}, u32[]{:S(2)}) copy-start(f32[4,64,32]{1,2,0:T(8,128)} %param.42) | copy-start | bytes 98308
  817.9 99.3 %copy-start.76 = (f32[4,32,64]{2,1,0:T(8,128)S(1)}, f32[4,32,64]{2,1,0:T(8,128)}, u32[]{:S(2)}) copy-start(f32[4,32,64]{2,1,0:T(8,128)} %param.37) | copy-start | bytes 98308
  817.9 99.3 %copy-start.86 = (f32[4,32,64]{2,1,0:T(8,128)S(1)}, f32[4,32,64]{2,1,0:T(8,128)}, u32[]{:S(2)}) copy-start(f32[4,32,64]{2,1,0:T(8,128)} %param.38) | copy-start | bytes 98308
  817.9 99.3 %copy-start.87 = (f32[4,32,64]{2,1,0:T(8,128)S(1)}, f32[4,32,64]{2,1,0:T(8,128)}, u32[]{:S(2)}) copy-start(f32[4,32,64]{2,1,0:T(8,128)} %param.39) | copy-start | bytes 98308
  817.9 101.0 %copy-start.88 = (f32[64,32]{0,1:T(8,128)S(1)}, f32[64,32]{0,1:T(8,128)}, u32[]{:S(2)}) copy-start(f32[64,32]{0,1:T(8,128)} %param.34) | copy-start | bytes 24580
  817.9 101.0 %copy-start.94 = (f32[64,32]{0,1:T(8,128)S(1)}, f32[64,32]{0,1:T(8,128)}, u32[]{:S(2)}) copy-start(f32[64,32]{0,1:T(8,128)} %param.35) | copy-start | bytes 24580
  817.9 101.0 %copy-start.95 = (f32[64,32]{0,1:T(8,128)S(1)}, f32[64,32]{0,1:T(8,128)}, u32[]{:S(2)}) copy-start(f32[64,32]{0,1:T(8,128)} %param.36) | copy-start | bytes 24580
  817.9 102.4 %copy-start.81 = (f32[8,1238]{1,0:T(8,128)S(1)}, f32[8,1238]{1,0:T(8,128)}, u32[]{:S(2)}) copy-start(f32[8,1238]{1,0:T(8,128)} %param.43) | copy-start | bytes 118852
  818.0 102.4 %copy-start.89 = (f32[8,1238]{1,0:T(8,128)S(1)}, f32[8,1238]{1,0:T(8,128)}, u32[]{:S(2)}) copy-start(f32[8,1238]{1,0:T(8,128)} %param.44) | copy-start | bytes 118852
  818.0 102.4 %copy-start.90 = (f32[8,1238]{1,0:T(8,128)S(1)}, f32[8,1238]{1,0:T(8,128)}, u32[]{:S(2)}) copy-start(f32[8,1238]{1,0:T(8,128)} %param.45) | copy-start | bytes 118852
  818.0 103.8 %copy-start.96 = (f32[32,8]{0,1:T(8,128)S(1)}, f32[32,8]{0,1:T(8,128)}, u32[]{:S(2)}) copy-start(f32[32,8]{0,1:T(8,128)} %param.46) | copy-start | bytes 3076
  818.0 103.8 %copy-start.107 = (f32[32,8]{0,1:T(8,128)S(1)}, f32[32,8]{0,1:T(8,128)}, u32[]{:S(2)}) copy-start(f32[32,8]{0,1:T(8,128)} %param.47) | copy-start | bytes 3076
  818.0 103.8 %copy-start.108 = (f32[32,8]{0,1:T(8,128)S(1)}, f32[32,8]{0,1:T(8,128)}, u32[]{:S(2)}) copy-start(f32[32,8]{0,1:T(8,128)} %param.48) | copy-start | bytes 3076
  818.0 104.4 %copy-start.91 = (f32[5,2,8]{2,1,0:T(2,128)S(1)}, f32[5,2,8]{2,1,0:T(2,128)}, u32[]{:S(2)}) copy-start(f32[5,2,8]{2,1,0:T(2,128)} %param.49) | copy-start | bytes 964
  818.0 104.4 %copy-start.105 = (f32[5,2,8]{2,1,0:T(2,128)S(1)}, f32[5,2,8]{2,1,0:T(2,128)}, u32[]{:S(2)}) copy-start(f32[5,2,8]{2,1,0:T(2,128)} %param.50) | copy-start | bytes 964
  818.0 104.4 %copy-start.106 = (f32[5,2,8]{2,1,0:T(2,128)S(1)}, f32[5,2,8]{2,1,0:T(2,128)}, u32[]{:S(2)}) copy-start(f32[5,2,8]{2,1,0:T(2,128)} %param.51) | copy-start | bytes 964
  (97 other events, 665.6 us)
Sparse Core Ops, SparseCore 0:
  764.8 138.4 all-reduce.3
where the time goes:
time: 946 us; the launch traced here: 931 us
  blocking collectives  311 us (33%)
  matrix products  203 us (21%)
  other arithmetic  171 us (18%)
  local copies, waits for them, and re-layouts  145 us (15%)
  waiting for transfers between devices  78.8 us (8%)
  between operations  22.1 us (2%)
    concatenate x4, local copies, waits for them, and re-layouts, logit_grads(): return jnp.concatenate(pieces_out, axis=1)  104 us
    dot_general x13, matrix products, contract_cols(): lax.dot_general(left, right, (((1,), (1,)), ((), ())), preferred_element_...  97.5 us
    psum x1, waiting for transfers between devices, body(): lax.psum((stem_grad, up_grad, down_grad, head_grad, table_grad, norm_grad...  78.8 us
    dot_general x13, matrix products, contract_rows(): lax.dot_general(left, right, (((0,), (0,)), ((), ())), preferred_element_...  58.2 us
    psum x1, blocking collectives, body(): weight_total = lax.psum(jnp.sum(weight_values), ('dp', 'mp'))  42.2 us
    all_gather x1, blocking collectives, body(): lax.all_gather(chance_table.astype(jnp.bfloat16), ('dp', 'mp'), axis=1, t...  40.6 us
    psum x1, blocking collectives, body(): lax.psum((stem_grad, up_grad, down_grad, head_grad, table_grad, norm_grad...  40.1 us
    all_gather x1, blocking collectives, body(): lax.all_gather(head_weight.astype(jnp.bfloat16), ('dp', 'mp'), axis=0, ti...  39 us
  transfers between devices with their start and end apart: 1, of which 1 were waited for; matrix products, arithmetic and copies ran while one was open for 2% of the time, Pallas kernels for 0%

commit v1 on v0

v1 whole, which is shorter than its diff:
```python
import math
import functools

import jax
import jax.numpy as jnp
from jax import lax
from jax.experimental import pallas as pl
from jax.experimental.pallas import tpu as pltpu
from jax.sharding import PartitionSpec as P

D = 256
BINS = 601
ACTIONS = 4
CODES = 32
LAYERS = 4
STEP = 10

VALUE_AT = 0
REWARD_AT = 608
CHANCE_AT = 1216
POLICY_AT = 1248
ROWS = 1264
DEPTH = 1280

beta_one = 0.9
beta_two = 0.99
eps_adam = 1e-08
eps_norm = 1e-05
matrix_rate = 0.2
vector_rate = 0.6
decay_rate = 0.1
clip_scale = 3.0

GELU_A = math.sqrt(2.0 / math.pi)
GELU_B = GELU_A * 0.044715
LOG2E = 1.4426950408889634
LANES = 256
CHAINS = 2
CHUNK = 16
BF = jnp.bfloat16
F32 = jnp.float32
MESH = pl.DeviceIdType.MESH
MATRICES = 1 + 2 * LAYERS
NORM_LANE = 32
SUM_LANE = 64
SUM_ROW = 10


def dot_nn(left, right):
    return lax.dot_general(left, right, (((1,), (0,)), ((), ())), preferred_element_type=F32)


def dot_nt(left, right):
    return lax.dot_general(left, right, (((1,), (1,)), ((), ())), preferred_element_type=F32)


def dot_tn(left, right):
    return lax.dot_general(left, right, (((0,), (0,)), ((), ())), preferred_element_type=F32)


def gelu_pair(v):
    square = v * v
    gate = 1.0 + jnp.tanh(v * (GELU_A + GELU_B * square))
    value = v * gate
    slope = gate + value * (2.0 - gate) * (GELU_A + 3.0 * GELU_B * square)
    return value, slope


def fold_rows(total, part):
    for at in range(0, part.shape[0], 8):
        piece = part[at : at + 8]
        total = piece if total is None else total + piece
    return total


def peak_rows(total, part):
    for at in range(0, part.shape[0], 8):
        piece = part[at : at + 8]
        total = piece if total is None else jnp.maximum(total, piece)
    return total


def orders_of(dp, mp):
    def step(axis, low, size):
        return (axis, low, size) if size > 1 else None

    far_dp, near_dp = step("dp", 2, dp // 2), step("dp", 1, 2)
    far_mp, near_mp = step("mp", 2, mp // 2), step("mp", 1, 2)
    return (
        [member for member in (far_dp, near_dp, far_mp, near_mp) if member],
        [member for member in (far_dp, far_mp, near_dp, near_mp) if member],
    )


def digit_of(step, data, model):
    axis, low, ways = step
    return ((data if axis == "dp" else model) // low) % ways


def slot_of(order, data, model):
    place, weight = 0, 1
    for step in order:
        place = place + digit_of(step, data, model) * weight
        weight *= step[2]
    return place


def partner_of(step, away):
    axis, low, ways = step
    index = lax.axis_index(axis)
    digit = (index // low) % ways
    other = (digit + away) % ways
    return {axis: index + (other - digit) * low}, other - digit


def sizes_of(order):
    sizes = [1]
    for step in order:
        sizes.append(sizes[-1] * step[2])
    return sizes


class Packing:
    def __init__(self, dp, mp):
        self.dp, self.mp, self.count = dp, mp, dp * mp
        self.deep, self.wide, self.own = D // dp, D // mp, D // (dp * mp)
        self.per = 128 // self.wide
        self.groups = -(-MATRICES // self.per)
        self.head_at = self.groups * self.deep
        self.tail_at = -(-(self.head_at + self.own * (DEPTH // 128)) // 8) * 8
        self.rows = -(-(self.tail_at + 16) // 32) * 32
        self.half = self.rows // 2
        self.orders = orders_of(dp, mp)
        self.sizes = [sizes_of(order) for order in self.orders]
        self.most = max(step[2] for step in self.orders[0])

    def split(self, begin, end):
        side = 1 if begin >= self.half else 0
        assert begin >= self.half or end <= self.half
        return side, slice(begin - side * self.half, end - side * self.half)


def pad_lanes(array, lanes):
    missing = lanes - array.shape[1]
    return array if missing == 0 else jnp.concatenate([array, jnp.zeros((array.shape[0], missing), array.dtype)], axis=1)


def spread_head(head):
    rows = head.shape[0]

    def blank(count):
        return jnp.zeros((rows, count), head.dtype)

    return jnp.concatenate(
        [
            head[:, :BINS],
            blank(REWARD_AT - BINS),
            head[:, BINS : 2 * BINS],
            blank(CHANCE_AT - REWARD_AT - BINS),
            head[:, 2 * BINS + ACTIONS :],
            head[:, 2 * BINS : 2 * BINS + ACTIONS],
            blank(DEPTH - POLICY_AT - ACTIONS),
        ],
        axis=1,
    )


def gather_head(padded):
    return jnp.concatenate(
        [
            padded[:, VALUE_AT : VALUE_AT + BINS],
            padded[:, REWARD_AT : REWARD_AT + BINS],
            padded[:, POLICY_AT : POLICY_AT + ACTIONS],
            padded[:, CHANCE_AT : CHANCE_AT + CODES],
        ],
        axis=1,
    )


def send_kernel(packing, stem, up, down, head, table, norm, weight, near, far, block, send_sem, recv_sem):
    kinds = (near, far)
    partners = [(step, away) for step in packing.orders[0] for away in range(1, step[2])]
    barrier = pltpu.get_barrier_semaphore()
    for step, away in partners:
        pl.semaphore_signal(barrier, inc=1, device_id=partner_of(step, away)[0], device_id_type=MESH)

    block[...] = jnp.zeros_like(block)
    matrices = [stem[...]] + [up[layer] for layer in range(LAYERS)] + [down[layer] for layer in range(LAYERS)]
    for group in range(packing.groups):
        members = matrices[group * packing.per : (group + 1) * packing.per]
        block[group * packing.deep : (group + 1) * packing.deep, :] = pad_lanes(jnp.concatenate(members, axis=1), 128)
    padded = spread_head(head[...])
    for tile in range(DEPTH // 128):
        at = packing.head_at + packing.own * tile
        block[at : at + packing.own, :] = padded[:, tile * 128 : (tile + 1) * 128]
    at = packing.tail_at
    block[at : at + packing.own, 0:CODES] = table[...]
    for layer in range(LAYERS + 1):
        block[at + 2 * layer : at + 2 * layer + 2, NORM_LANE : NORM_LANE + packing.own] = norm[layer]
    amount = jnp.sum(jnp.sum(weight[...].astype(F32), axis=0, keepdims=True), axis=1, keepdims=True)
    amount = jnp.broadcast_to(amount, (1, 128))
    for row in range(SUM_ROW, SUM_ROW + 3):
        part = amount.astype(BF).astype(F32)
        block[at + row : at + row + 1, SUM_LANE:128] = part[:, SUM_LANE:128]
        amount = amount - part
    data, model = lax.axis_index("dp"), lax.axis_index("mp")
    slots = [slot_of(order, data, model) for order in packing.orders]
    for side in range(2):
        kinds[side][slots[side]] = block[side * packing.half : (side + 1) * packing.half, :].astype(BF)

    pl.semaphore_wait(barrier, len(partners))

    def copies_of(side, number):
        step, size = packing.orders[side][number], packing.sizes[side][number]
        held = kinds[side].at[pl.ds((slots[side] // size) * size, size)]
        return [
            pltpu.make_async_remote_copy(
                src_ref=held,
                dst_ref=held,
                send_sem=send_sem.at[side, number, away],
                recv_sem=recv_sem.at[side, number, away],
                device_id=partner_of(step, away)[0],
                device_id_type=MESH,
            )
            for away in range(1, step[2])
        ]

    steps = len(packing.orders[0])
    copies = [[copies_of(side, number) for number in range(steps)] for side in range(2)]
    for number in range(steps + 1):
        for side in range(2):
            if number:
                for member in copies[side][number - 1]:
                    member.wait_recv()
            if number < steps:
                for member in copies[side][number]:
                    member.start()
    for side in range(2):
        for number in range(steps):
            for member in copies[side][number]:
                member.wait_send()


def send_weights(packing, stem, up, down, head, table, norm, weight):
    steps = len(packing.orders[0])
    shape = jax.ShapeDtypeStruct((packing.count, packing.half, 128), BF)
    return pl.pallas_call(
        functools.partial(send_kernel, packing),
        out_shape=[shape, shape],
        in_specs=[pl.BlockSpec()] * 7,
        out_specs=[pl.BlockSpec(memory_space=pltpu.VMEM)] * 2,
        scratch_shapes=[
            pltpu.VMEM((packing.rows, 128), F32),
            pltpu.SemaphoreType.DMA((2, steps, packing.most)),
            pltpu.SemaphoreType.DMA((2, steps, packing.most)),
        ],
        compiler_params=pltpu.CompilerParams(
            collective_id=0, has_side_effects=True, vmem_limit_bytes=48 * 1024 * 1024
        ),
        name="send_weights",
    )(stem, up, down, head, table, norm, weight)


def reduce_kernel(
    packing,
    near_in,
    far_in,
    own,
    squares,
    near,
    far,
    near_out,
    far_out,
    near_got,
    far_got,
    across,
    along,
    send_sem,
    recv_sem,
    part_send,
    part_recv,
):
    steps = len(packing.orders[0])
    data, model = lax.axis_index("dp"), lax.axis_index("mp")
    barrier = pltpu.get_barrier_semaphore()
    for away in range(1, packing.mp):
        pl.semaphore_signal(barrier, inc=1, device_id={"mp": (model + away) % packing.mp}, device_id_type=MESH)
    for away in range(1, packing.dp):
        pl.semaphore_signal(barrier, inc=1, device_id={"dp": (data + away) % packing.dp}, device_id_type=MESH)

    slots = [slot_of(order, data, model) for order in packing.orders]
    given, held, sent, got = (near_in, far_in), (near, far), (near_out, far_out), (near_got, far_got)

    def source_of(side, number):
        return given[side] if number == steps - 1 else held[side]

    def mine_of(side, number):
        size = packing.sizes[side][number]
        return (slots[side] // size) * size

    def place_of(side, number, away):
        size = packing.sizes[side][number]
        return pl.ds(size * away, size)

    def pack(side, number):
        step, size = packing.orders[side][number], packing.sizes[side][number]
        for away in range(1, step[2]):
            block = mine_of(side, number) + partner_of(step, away)[1] * size
            sent[side][place_of(side, number, away)] = source_of(side, number)[pl.ds(block, size)].astype(BF)

    def copies_of(side, number):
        step = packing.orders[side][number]
        return [
            pltpu.make_async_remote_copy(
                src_ref=sent[side].at[place_of(side, number, away)],
                dst_ref=got[side].at[place_of(side, number, away)],
                send_sem=send_sem.at[side, number, away],
                recv_sem=recv_sem.at[side, number, away],
                device_id=partner_of(step, away)[0],
                device_id_type=MESH,
            )
            for away in range(1, step[2])
        ]

    def take(side, number):
        rows = pl.ds(mine_of(side, number), packing.sizes[side][number])
        total = source_of(side, number)[rows]
        for away in range(1, packing.orders[side][number][2]):
            total = total + got[side][place_of(side, number, away)].astype(F32)
        held[side][rows] = total

    copies = [[copies_of(side, number) for number in range(steps)] for side in range(2)]
    for side in range(2):
        pack(side, steps - 1)
    pl.semaphore_wait(barrier, packing.mp + packing.dp - 2)
    for number in range(steps - 1, -1, -1):
        for side in range(2):
            if number < steps - 1:
                for member in copies[side][number + 1]:
                    member.wait_recv()
                take(side, number + 1)
                pack(side, number)
            for member in copies[side][number]:
                member.start()
    total = None
    for side in range(2):
        for member in copies[side][0]:
            member.wait_recv()
        take(side, 0)
        block = held[side][slots[side]]
        own[side * packing.half : (side + 1) * packing.half, :] = block
        total = fold_rows(total, block * block)

    def exchange(axis, index, count, buffer, value, first):
        buffer[index] = value
        going = []
        for away in range(1, count):
            going.append(
                pltpu.make_async_remote_copy(
                    src_ref=buffer.at[index],
                    dst_ref=buffer.at[index],
                    send_sem=part_send.at[first + away],
                    recv_sem=part_recv.at[first + away],
                    device_id={axis: (index + away) % count},
                    device_id_type=MESH,
                )
            )
            going[-1].start()
        for member in going:
            member.wait_recv()
        whole = buffer[0]
        for other in range(1, count):
            whole = whole + buffer[other]
        return whole, going

    total, going = exchange("mp", model, packing.mp, across, total, 0)
    total, more = exchange("dp", data, packing.dp, along, total, packing.mp)
    squares[...] = total
    for member in going + more:
        member.wait_send()
    for side in range(2):
        for number in range(steps):
            for member in copies[side][number]:
                member.wait_send()


def reduce_grads(packing, near, far):
    steps = len(packing.orders[0])
    vmem = pl.BlockSpec(memory_space=pltpu.VMEM)
    return pl.pallas_call(
        functools.partial(reduce_kernel, packing),
        out_shape=[jax.ShapeDtypeStruct((packing.rows, 128), F32), jax.ShapeDtypeStruct((8, 128), F32)],
        in_specs=[vmem] * 2,
        out_specs=[vmem] * 2,
        scratch_shapes=[pltpu.VMEM((packing.count, packing.half, 128), F32)] * 2
        + [pltpu.VMEM((packing.count, packing.half, 128), BF)] * 4
        + [
            pltpu.VMEM((packing.mp, 8, 128), F32),
            pltpu.VMEM((packing.dp, 8, 128), F32),
            pltpu.SemaphoreType.DMA((2, steps, packing.most)),
            pltpu.SemaphoreType.DMA((2, steps, packing.most)),
            pltpu.SemaphoreType.DMA((packing.mp + packing.dp,)),
            pltpu.SemaphoreType.DMA((packing.mp + packing.dp,)),
        ],
        compiler_params=pltpu.CompilerParams(
            collective_id=1, has_side_effects=True, vmem_limit_bytes=60 * 1024 * 1024
        ),
        name="reduce_grads",
    )(near, far)


def adam_rows(weight, moment, square, grad, rate, decay):
    first = beta_one * moment + (1.0 - beta_one) * grad
    second = beta_two * square + (1.0 - beta_two) * grad * grad
    first_hat = first / (1.0 - beta_one**STEP)
    second_hat = second / (1.0 - beta_two**STEP)
    updated = weight - rate * (first_hat / (jnp.sqrt(second_hat) + eps_adam) + decay * weight)
    return (updated, first, second)


def update_kernel(packing, rows_all, own, squares, *refs):
    ins, outs = refs[:18], refs[18:]
    grad_norm, outs = outs[0], outs[1:]
    whole = jnp.sum(jnp.sum(squares[...], axis=0, keepdims=True), axis=1, keepdims=True)
    norm = jnp.sqrt(whole)
    grad_norm[...] = norm
    ratio = jnp.minimum(1.0, clip_scale * math.sqrt(rows_all) / norm)

    def apply(which, index, grad, rate=matrix_rate, decay=decay_rate):
        weight, moment, square = (ins[3 * which + kind][index] for kind in range(3))
        base = 4 * which
        new, first, second = adam_rows(weight, moment, square, grad * ratio, rate, decay)
        outs[base][index] = new
        outs[base + 1][index] = first
        outs[base + 2][index] = second
        if which < 5:
            outs[base + 3][index] = new.astype(BF)

    def matrix(member):
        at = (member // packing.per) * packing.deep
        lane = (member % packing.per) * packing.wide
        return own[at : at + packing.deep, lane : lane + packing.wide]

    apply(0, ..., matrix(0))
    for layer in range(LAYERS):
        apply(1, layer, matrix(1 + layer))
        apply(2, layer, matrix(1 + LAYERS + layer))
    tiles = [
        own[packing.head_at + packing.own * tile : packing.head_at + packing.own * (tile + 1), :]
        for tile in range(DEPTH // 128)
    ]
    apply(3, ..., gather_head(jnp.concatenate(tiles, axis=1)))
    at = packing.tail_at
    apply(4, ..., own[at : at + packing.own, 0:CODES])
    for layer in range(LAYERS + 1):
        apply(
            5,
            layer,
            own[at + 2 * layer : at + 2 * layer + 2, NORM_LANE : NORM_LANE + packing.own],
            vector_rate,
            0.0,
        )


def update(packing, rows_all, own, squares, groups):
    ins = [member for group in groups for member in group]
    outs = [jax.ShapeDtypeStruct((1, 1), F32)]
    for which, group in enumerate(groups):
        outs += [jax.ShapeDtypeStruct(group[0].shape, F32)] * 3
        if which < 5:
            outs.append(jax.ShapeDtypeStruct(group[0].shape, BF))
    return pl.pallas_call(
        functools.partial(update_kernel, packing, rows_all),
        out_shape=outs,
        in_specs=[pl.BlockSpec()] * (2 + len(ins)),
        out_specs=[pl.BlockSpec()] * len(outs),
        compiler_params=pltpu.CompilerParams(vmem_limit_bytes=48 * 1024 * 1024),
        name="update",
    )(own, squares, *ins)


def train_kernel(
    packing,
    rows_all,
    chains,
    lat_ref,
    code_ref,
    weight_ref,
    value_ref,
    reward_ref,
    action_ref,
    target_ref,
    near_in,
    far_in,
    lat_grad,
    near_out,
    far_out,
    stem_acc,
    table_acc,
    up_acc,
    down_acc,
    head_acc,
    stem_t,
    table_t,
    up_t,
    up_n,
    down_t,
    down_n,
    head_t,
    head_n,
    scale_s,
    wide_s,
    head_wide,
    stream_s,
    centered_s,
    slope_s,
    inner_slope_s,
    rstd_s,
    act_s,
    gated_s,
    branch_s,
    inner_grad_s,
    logit_s,
    low_s,
    top_s,
    pre_s,
    hot_s,
    norm_s,
    norm_part,
):
    step = pl.program_id(0)
    devices = [(data, model) for data in range(packing.dp) for model in range(packing.mp)]

    @pl.when(step == 0)
    def _():
        held = (near_in, far_in)

        def rows_of(device, begin, end):
            side, rows = packing.split(begin, end)
            return held[side][slot_of(packing.orders[side], *device)].astype(F32)[rows]

        for data in range(packing.dp):
            for group in range(packing.groups):
                begin = group * packing.deep
                parts = [rows_of((data, model), begin, begin + packing.deep) for model in range(packing.mp)]
                for member in range(min(packing.per, MATRICES - group * packing.per)):
                    lane = member * packing.wide
                    wide_s[group * packing.per + member, data * packing.deep : (data + 1) * packing.deep, :] = (
                        jnp.concatenate([part[:, lane : lane + packing.wide] for part in parts], axis=1)
                    )
        stem_t[...] = wide_s[0].astype(BF)
        for layer in range(LAYERS):
            half_up = 0.5 * wide_s[1 + layer]
            half_down = 0.5 * wide_s[1 + LAYERS + layer]
            up_n[layer] = half_up.astype(BF)
            up_t[layer] = half_up.T.astype(BF)
            down_t[layer] = half_down.astype(BF)
            down_n[layer] = half_down.T.astype(BF)
        norm_parts = []
        total = None
        for device in devices:
            at = (device[0] * packing.mp + device[1]) * packing.own
            for tile in range(DEPTH // 128):
                begin = packing.head_at + packing.own * tile
                head_wide[at : at + packing.own, tile * 128 : (tile + 1) * 128] = rows_of(
                    device, begin, begin + packing.own
                )
            tail = rows_of(device, packing.tail_at, packing.tail_at + 16)
            table_acc[at : at + packing.own, :] = tail[0 : packing.own, 0:CODES]
            norm_parts.append(tail[:, NORM_LANE : NORM_LANE + packing.own])
            amount = tail[SUM_ROW : SUM_ROW + 1] + tail[SUM_ROW + 1 : SUM_ROW + 2] + tail[SUM_ROW + 2 : SUM_ROW + 3]
            total = amount if total is None else total + amount
        table_t[...] = table_acc[...].astype(BF)
        head_n[...] = head_wide[...].astype(BF)
        for at in range(0, DEPTH, D):
            turned = head_wide[:, at : at + D].T.astype(BF)
            end = min(D, ROWS - at)
            head_t[at : at + end, :] = turned[0:end]
        norms = jnp.concatenate(norm_parts, axis=1)
        columns = jnp.concatenate([norms, jnp.zeros((128 - norms.shape[0], D), F32)], axis=0).T
        for which in range(2 * (LAYERS + 1)):
            norm_s[which] = jnp.broadcast_to(columns[:, which : which + 1], (D, 128))
        scale_s[...] = jnp.broadcast_to(rows_all / total[:, SUM_LANE : SUM_LANE + 1], (1, LANES))

        stem_acc[...] = jnp.zeros_like(stem_acc)
        table_acc[...] = jnp.zeros_like(table_acc)
        up_acc[...] = jnp.zeros_like(up_acc)
        down_acc[...] = jnp.zeros_like(down_acc)
        head_acc[...] = jnp.zeros_like(head_acc)
        norm_part[...] = jnp.zeros_like(norm_part)
        low_s[...] = jnp.zeros_like(low_s)

    def norm_rows(which, at):
        half = norm_s[which, at : at + CHUNK, :]
        return jnp.concatenate([half] * (LANES // 128), axis=1)

    def add_norm(which, at, part):
        total = part[:, 0:128]
        for lane in range(128, LANES, 128):
            total = total + part[:, lane : lane + 128]
        norm_part[which, at : at + CHUNK, :] += total

    def chain(index):
        cols = slice(index * LANES, (index + 1) * LANES)

        def row_of(ref):
            return ref[cols].reshape(1, LANES)

        def norm_forward(layer, total, sink):
            mean = jnp.sum(total, axis=0, keepdims=True) * (1.0 / D)
            squares = None
            for at in range(0, D, CHUNK):
                rows = slice(at, at + CHUNK)
                centered = stream_s[rows, cols] - mean
                centered_s[layer, rows, cols] = centered
                squares = fold_rows(squares, centered * centered)
            spread = jnp.sum(squares, axis=0, keepdims=True) * (1.0 / D)
            rstd = lax.rsqrt(spread + eps_norm)
            rstd_s[layer, :, cols] = rstd
            total = None
            for at in range(0, D, CHUNK):
                rows = slice(at, at + CHUNK)
                scaled = centered_s[layer, rows, cols] * rstd
                value, slope = gelu_pair(scaled * norm_rows(2 * layer, at) + norm_rows(2 * layer + 1, at))
                if sink is None:
                    value = 0.5 * value
                    slope_s[layer, rows, cols] = 0.5 * slope
                    stream_s[rows, cols] = value
                    total = fold_rows(total, value)
                else:
                    slope_s[layer, rows, cols] = slope
                    sink[layer - 1, rows, cols] = value.astype(BF)
            return total

        def norm_backward(layer, grad_of, emit):
            rstd = rstd_s[layer, :, cols]
            first = second = None
            for at in range(0, D, CHUNK):
                rows = slice(at, at + CHUNK)
                grad = grad_of(rows) * slope_s[layer, rows, cols]
                centered = centered_s[layer, rows, cols]
                add_norm(2 * layer + 1, at, grad)
                grad = grad * rstd
                add_norm(2 * layer, at, grad * centered)
                wide = grad * norm_rows(2 * layer, at)
                slope_s[layer, rows, cols] = wide
                first = fold_rows(first, wide)
                second = fold_rows(second, wide * centered)
            shift = jnp.sum(first, axis=0, keepdims=True) * (1.0 / D)
            slant = jnp.sum(second, axis=0, keepdims=True) * (1.0 / D) * (rstd * rstd)
            for at in range(0, D, CHUNK):
                rows = slice(at, at + CHUNK)
                emit(rows, (slope_s[layer, rows, cols] - shift) - centered_s[layer, rows, cols] * slant)

        hot = (lax.broadcasted_iota(jnp.int32, (CODES, LANES), 0) == row_of(code_ref)).astype(F32).astype(BF)
        hot_s[:, cols] = hot
        pre = dot_nt(stem_t[...], lat_ref[cols, :]) + dot_nn(table_t[...], hot)
        yield
        total = None
        for at in range(0, D, CHUNK):
            rows = slice(at, at + CHUNK)
            stream_s[rows, cols] = pre[rows]
            total = fold_rows(total, pre[rows])
        total = norm_forward(0, total, None)
        yield
        for layer in range(1, LAYERS + 1):
            norm_forward(layer, total, act_s)
            yield
            inner = dot_nn(up_t[layer - 1], act_s[layer - 1, :, cols])
            yield
            for at in range(0, D, CHUNK):
                rows = slice(at, at + CHUNK)
                value, slope = gelu_pair(inner[rows])
                inner_slope_s[layer - 1, rows, cols] = slope
                gated_s[layer - 1, rows, cols] = value.astype(BF)
            yield
            branch = dot_nn(down_t[layer - 1], gated_s[layer - 1, :, cols])
            yield
            total = None
            for at in range(0, D, CHUNK):
                rows = slice(at, at + CHUNK)
                stream = stream_s[rows, cols] + branch[rows]
                if layer < LAYERS:
                    stream_s[rows, cols] = stream
                    total = fold_rows(total, stream)
                else:
                    top_s[rows, cols] = stream.astype(BF)
        yield
        logit_s[:, cols] = dot_nn(head_t[...], top_s[:, cols])
        yield
        coef = row_of(weight_ref).astype(F32) * scale_s[...]
        sections = (
            (VALUE_AT, BINS, value_ref),
            (REWARD_AT, BINS, reward_ref),
            (CHANCE_AT, CODES, target_ref),
            (POLICY_AT, ACTIONS, action_ref),
        )
        for begin, count, target_ref_of in sections:
            padded = -(-count // 8) * 8
            if padded != count:
                last = slice(begin + padded - 8, begin + padded)
                keep = lax.broadcasted_iota(jnp.int32, (8, LANES), 0) < count - (padded - 8)
                logit_s[last, cols] = jnp.where(keep, logit_s[last, cols], -1e30)
            peak = None
            for at in range(0, padded, CHUNK):
                rows = slice(begin + at, begin + min(at + CHUNK, padded))
                peak = peak_rows(peak, logit_s[rows, cols])
            peak = jnp.max(peak, axis=0, keepdims=True)
            mass = None
            for at in range(0, padded, CHUNK):
                rows = slice(begin + at, begin + min(at + CHUNK, padded))
                power = jnp.exp2((logit_s[rows, cols] - peak) * LOG2E)
                logit_s[rows, cols] = power
                mass = fold_rows(mass, power)
            scale = coef / jnp.sum(mass, axis=0, keepdims=True)
            target = row_of(target_ref_of)
            stored = -(-count // 16) * 16
            for at in range(0, padded, CHUNK):
                end = min(at + CHUNK, padded)
                rows = slice(begin + at, begin + end)
                soft = logit_s[rows, cols] * scale
                place = lax.broadcasted_iota(jnp.int32, soft.shape, 0) + at
                soft = jnp.where(place == target, soft - coef, soft)
                if end == padded and padded != stored:
                    soft = jnp.concatenate([soft, jnp.zeros((stored - padded, LANES), F32)], axis=0)
                    rows = slice(begin + at, begin + stored)
                low_s[rows, cols] = soft.astype(BF)
            yield
        grad = dot_nn(head_n[...], low_s[:, cols])
        yield
        if index == chains - 1:
            head_acc[...] += dot_nt(low_s[0:ROWS, :], top_s[...])
        for layer in range(LAYERS, 0, -1):
            if layer == LAYERS:
                for at in range(0, D, CHUNK):
                    rows = slice(at, at + CHUNK)
                    stream_s[rows, cols] = grad[rows]
                    branch_s[layer - 1, rows, cols] = grad[rows].astype(BF)
            yield
            gated_grad = dot_nn(down_n[layer - 1], branch_s[layer - 1, :, cols])
            yield
            for at in range(0, D, CHUNK):
                rows = slice(at, at + CHUNK)
                inner_grad_s[layer - 1, rows, cols] = (
                    gated_grad[rows] * inner_slope_s[layer - 1, rows, cols]
                ).astype(BF)
            yield
            active_grad = dot_nn(up_n[layer - 1], inner_grad_s[layer - 1, :, cols])
            if index == chains - 1:
                down_acc[layer - 1] += dot_nt(branch_s[layer - 1], gated_s[layer - 1])
                up_acc[layer - 1] += dot_nt(act_s[layer - 1], inner_grad_s[layer - 1])
            yield

            def emit(rows, change, layer=layer):
                stream = stream_s[rows, cols] + change
                stream_s[rows, cols] = stream
                if layer > 1:
                    branch_s[layer - 2, rows, cols] = stream.astype(BF)

            norm_backward(layer, lambda rows: active_grad[rows], emit)
            yield

        def emit_pre(rows, change):
            pre_s[rows, cols] = change.astype(BF)

        norm_backward(0, lambda rows: stream_s[rows, cols], emit_pre)
        yield
        lat_grad[cols, :] = dot_tn(pre_s[:, cols], stem_t[...])
        yield

    running = []
    waiting = [chain(index) for index in range(chains)]
    while running or waiting:
        if waiting:
            running.append(waiting.pop(0))
        for member in list(running):
            try:
                next(member)
            except StopIteration:
                running.remove(member)

    stem_acc[...] += dot_nn(pre_s[...], lat_ref[...])
    table_acc[...] += dot_nt(pre_s[...], hot_s[...])

    @pl.when(step == pl.num_programs(0) - 1)
    def _():
        outs = (near_out, far_out)
        near_out[...] = jnp.zeros_like(near_out)
        far_out[...] = jnp.zeros_like(far_out)
        for at in range(0, DEPTH, D):
            end = min(D, ROWS - at)
            turned = head_acc[at : at + end, :]
            if end < D:
                turned = jnp.concatenate([turned, jnp.zeros((D - end, D), F32)], axis=0)
            head_wide[:, at : at + D] = turned.T
        lane_at = lax.broadcasted_iota(jnp.int32, (D, 128), 1)
        columns = jnp.zeros((D, 128), F32)
        for which in range(2 * (LAYERS + 1)):
            columns = jnp.where(lane_at == which, jnp.sum(norm_part[which], axis=1, keepdims=True), columns)
        norms = columns.T[0:16]
        for device in devices:
            data, model = device
            at = (data * packing.mp + model) * packing.own
            slots = [slot_of(order, data, model) for order in packing.orders]

            def keep(begin, value, lanes=slice(0, 128)):
                side, rows = packing.split(begin, begin + value.shape[0])
                outs[side][slots[side], rows, lanes] = value

            deep = slice(data * packing.deep, (data + 1) * packing.deep)
            wide = slice(model * packing.wide, (model + 1) * packing.wide)
            pieces = [stem_acc[deep, wide]] + [0.5 * up_acc[layer, deep, wide] for layer in range(LAYERS)]
            pieces += [0.5 * down_acc[layer, deep, wide] for layer in range(LAYERS)]
            for group in range(packing.groups):
                members = pieces[group * packing.per : (group + 1) * packing.per]
                keep(group * packing.deep, pad_lanes(jnp.concatenate(members, axis=1), 128))
            for tile in range(DEPTH // 128):
                keep(
                    packing.head_at + packing.own * tile,
                    head_wide[at : at + packing.own, tile * 128 : (tile + 1) * 128],
                )
            keep(packing.tail_at, table_acc[at : at + packing.own, :], slice(0, CODES))
            keep(
                packing.tail_at,
                norms[0 : 2 * (LAYERS + 1), at : at + packing.own],
                slice(NORM_LANE, NORM_LANE + packing.own),
            )


def train(packing, rows_all, latent, code, weight, value, reward, action, target, near, far):
    count = latent.shape[0]
    chains = CHAINS
    block = chains * LANES

    def full(shape):
        return pl.BlockSpec(shape, lambda i: (0,) * len(shape), pipeline_mode=pl.Buffered(1))

    def row():
        return pl.BlockSpec((block,), lambda i: (i,))

    packed = (packing.count, packing.half, 128)
    return pl.pallas_call(
        functools.partial(train_kernel, packing, rows_all, chains),
        grid=(count // block,),
        out_shape=[
            jax.ShapeDtypeStruct((count, D), F32),
            jax.ShapeDtypeStruct(packed, F32),
            jax.ShapeDtypeStruct(packed, F32),
        ],
        in_specs=[pl.BlockSpec((block, D), lambda i: (i, 0))] + [row() for _ in range(6)] + [full(packed)] * 2,
        out_specs=[pl.BlockSpec((block, D), lambda i: (i, 0))] + [full(packed)] * 2,
        scratch_shapes=[
            pltpu.VMEM((D, D), F32),
            pltpu.VMEM((D, CODES), F32),
            pltpu.VMEM((LAYERS, D, D), F32),
            pltpu.VMEM((LAYERS, D, D), F32),
            pltpu.VMEM((ROWS, D), F32),
            pltpu.VMEM((D, D), BF),
            pltpu.VMEM((D, CODES), BF),
            pltpu.VMEM((LAYERS, D, D), BF),
            pltpu.VMEM((LAYERS, D, D), BF),
            pltpu.VMEM((LAYERS, D, D), BF),
            pltpu.VMEM((LAYERS, D, D), BF),
            pltpu.VMEM((ROWS, D), BF),
            pltpu.VMEM((D, DEPTH), BF),
            pltpu.VMEM((1, LANES), F32),
            pltpu.VMEM((MATRICES, D, D), F32),
            pltpu.VMEM((D, DEPTH), F32),
            pltpu.VMEM((D, block), F32),
            pltpu.VMEM((LAYERS + 1, D, block), F32),
            pltpu.VMEM((LAYERS + 1, D, block), F32),
            pltpu.VMEM((LAYERS, D, block), F32),
            pltpu.VMEM((LAYERS + 1, 1, block), F32),
            pltpu.VMEM((LAYERS, D, block), BF),
            pltpu.VMEM((LAYERS, D, block), BF),
            pltpu.VMEM((LAYERS, D, block), BF),
            pltpu.VMEM((LAYERS, D, block), BF),
            pltpu.VMEM((ROWS, block), F32),
            pltpu.VMEM((DEPTH, block), BF),
            pltpu.VMEM((D, block), BF),
            pltpu.VMEM((D, block), BF),
            pltpu.VMEM((CODES, block), BF),
            pltpu.VMEM((2 * (LAYERS + 1), D, 128), F32),
            pltpu.VMEM((2 * (LAYERS + 1), D, 128), F32),
        ],
        compiler_params=pltpu.CompilerParams(
            dimension_semantics=("arbitrary",), vmem_limit_bytes=60 * 1024 * 1024
        ),
        name="train",
    )(latent, code, weight, value, reward, action, target, near, far)


def body(rows_all, packing, *args):
    latent, code, weight, value, reward, action, target = args[:7]
    groups = [args[7 + 3 * which : 10 + 3 * which] for which in range(6)]

    def turn(which, array):
        return jnp.swapaxes(array, -1, -2) if which in (0, 2, 4) else array

    groups = [tuple(turn(which, member) for member in group) for which, group in enumerate(groups)]
    stem, up, down, head, table, norm = (group[0] for group in groups)
    near, far = send_weights(packing, stem, up, down, head, table, norm, weight.reshape(-1, 128))
    lat_grad, near, far = train(packing, rows_all, latent, code, weight, value, reward, action, target, near, far)
    own, squares = reduce_grads(packing, near, far)
    outs = update(packing, rows_all, own, squares, groups)
    result = [outs[0].reshape(()), lat_grad]
    at = 1
    for which in range(6):
        for _ in range(4 if which < 5 else 3):
            result.append(turn(which, outs[at]))
            at += 1
    return tuple(result)


def solution(mesh):
    every = ("dp", "mp")
    states, flat = P(every, None), P(every)
    params = (P("mp", "dp"), P(None, "dp", "mp"), P(None, "mp", "dp"), P(every, None), P(None, every), P(None, None, every))
    in_specs = (states,) + (flat,) * 6 + tuple(spec for spec in params for _ in range(3))
    out_specs = (P(), states) + tuple(spec for which, spec in enumerate(params) for _ in range(4 if which < 5 else 3))
    packing = Packing(mesh.shape["dp"], mesh.shape["mp"])

    def run(*args):
        rows_all = args[0].shape[0] * packing.count
        return body(rows_all, packing, *args)

    return jax.shard_map(run, mesh=mesh, in_specs=in_specs, out_specs=out_specs, check_vma=False)
```

time: 946 us -> 223 us (0.24); the launches traced: 931 us -> 223 us
  blocking collectives: 311 us -> 0 us
  Pallas kernels: 0 us -> 213 us
  matrix products: 203 us -> 0 us
  other arithmetic: 171 us -> 0 us
  local copies, waits for them, and re-layouts: 145 us -> 8.97 us
  waiting for transfers between devices: 78.8 us -> 0 us
  between operations: 22.1 us -> 0.98 us
    all_gather x9 -> x0, blocking collectives: 229 us -> none  [the longest x1 40.6 us: body(): lax.all_gather(chance_table.astype(jnp.bfloat16), ('dp', 'mp'), axis=1, t...]
    pallas_call x0 -> x4, Pallas kernels: none -> 213 us  [the longest x1 153 us: train(): pl.pallas_call(functools.partial(train_kernel, packing, rows_all, chains)...]
    dot_general x41 -> x0, matrix products: 203 us -> none  [the longest x13 97.5 us: contract_cols(): lax.dot_general(left, right, (((1,), (1,)), ((), ())), preferred_element_...]
    concatenate x4 -> x0, local copies, waits for them, and re-layouts: 104 us -> none  [logit_grads(): return jnp.concatenate(pieces_out, axis=1)]
    psum x2 -> x0, blocking collectives: 82.3 us -> none  [the longest x1 42.2 us: body(): weight_total = lax.psum(jnp.sum(weight_values), ('dp', 'mp'))]
    reduce_sum x31 -> x0, other arithmetic: 78.9 us -> none  [the longest x6 36.8 us: layer_norm(): centered = stream - jnp.mean(stream, axis=-1, keepdims=True)]
    psum x1 -> x0, waiting for transfers between devices: 78.8 us -> none  [body(): lax.psum((stem_grad, up_grad, down_grad, head_grad, table_grad, norm_grad...]
    convert_element_type x15 -> x0, other arithmetic: 48.2 us -> none  [the longest x4 27.4 us: body(): active = normed(stream, norm_values[layer_idx + 1, 0], norm_values[layer_...]
  transfers between devices with their start and end apart: 1 -> 0, of which waited for: 1 -> 0; matrix products, arithmetic and copies ran while one was open for 2% -> 0% of each run, Pallas kernels for 0% -> 0%
where the time goes in v1:
time: 223 us
  Pallas kernels  213 us (96%)
  local copies, waits for them, and re-layouts  8.97 us (4%)
    pallas_call x1, Pallas kernels, train(): pl.pallas_call(functools.partial(train_kernel, packing, rows_all, chains)...  153 us
    pallas_call x1, Pallas kernels, reduce_grads(): pl.pallas_call(functools.partial(reduce_kernel, packing), out_shape=[jax....  33.9 us
    pallas_call x1, Pallas kernels, send_weights(): pl.pallas_call(functools.partial(send_kernel, packing), out_shape=[shape,...  25.2 us
    unnamed x58, local copies, waits for them, and re-layouts  8.97 us

profile of v1, /device:TPU:0, one launch (start us, length us, event | category | flops | bytes accessed | tf_op | source)
XLA Modules:
  0.0 222.8 jit_solution(11274351555303221521)
XLA Ops:
  0.7 0.0 copy-start.2
  0.7 0.8 copy-done.2
  1.5 0.8 copy-done.4
  2.4 0.8 copy-done.6
  3.1 0.8 copy-done.8
  3.9 0.7 copy-done.10
  4.6 0.7 copy-done.18
  5.3 0.7 copy-done.20
  6.0 25.2 %send_weights.1 = (bf16[32,128,128]{2,1,0:T(8,128)(2,1)S(1)}, bf16[32,128,128]{2,1,0:T(8,128)(2,1)S(1)}) custom-call(f32[32,64]{1,0:T(8,128)S(1)} %bitcast.26, f32[4,32,64]{2,1,0:T(8,128)S(1)} %copy-done.2, f32[4,32,64]{2,1,0:T(8,128)S(1)} %bitcast.23, f32[8,1238]{1,0:T(8,128)S(1)} %copy-done.6, f32[8,32]{1,0:T(8,128)S(1)} %bitcast.30, ...), custom_call_target="tpu_custom_call" | custom-call | tf_op jit(solution)/shard_map/send_weights/pallas_call | solution.py:247
  31.2 1.0 copy-done
  32.2 1.0 copy-done.1
  33.2 0.0 copy-start.12
  33.2 0.0 copy-start.13
  33.2 0.0 copy-start.14
  33.2 0.0 copy-start.15
  33.2 0.0 copy-start.16
  33.2 0.0 copy-start.17
  33.2 0.0 copy-start.19
  33.2 0.0 copy-start.21
  33.3 0.0 copy-start.22
  33.3 0.0 copy-start.23
  33.3 0.0 copy-start.24
  33.3 0.0 copy-start.25
  33.3 0.0 copy-start.26
  33.3 0.0 copy-start.27
  33.3 152.7 %train.1 = (f32[8192,256]{1,0:T(8,128)}, f32[32,128,128]{2,1,0:T(8,128)}, f32[32,128,128]{2,1,0:T(8,128)}) custom-call(bf16[8192,256]{1,0:T(8,128)(2,1)} %lat_ref.1, s32[8192]{0:T(1024)} %code_ref.1, s32[8192]{0:T(1024)} %weight_ref.1, s32[8192]{0:T(1024)} %value_ref.1, s32[8192]{0:T(1024)} %reward_ref.1, s32[8192]{0:T(1024)} %action_ref.1, ...), custom_call_target="tpu_custom_call" | custom-call | tf_op jit(solution)/shard_map/train/pallas_call | solution.py:842
  186.0 33.9 %reduce_grads.1 = (f32[256,128]{1,0:T(8,128)}, f32[8,128]{1,0:T(8,128)}) custom-call(f32[32,128,128]{2,1,0:T(8,128)} %get-tuple-element.58.near_in, f32[32,128,128]{2,1,0:T(8,128)} %get-tuple-element.59.far_in), custom_call_target="tpu_custom_call" | custom-call | tf_op jit(solution)/shard_map/reduce_grads/pallas_call | solution.py:390
  220.0 0.0 copy-done.3
  220.0 0.0 copy-done.5
  220.0 0.0 copy-done.7
  220.0 0.0 copy-done.11
  220.0 0.0 copy-done.12
  220.0 0.0 copy-done.13
  220.1 0.0 copy-done.14
  220.1 0.0 copy-done.15
  220.1 0.0 copy-done.16
  220.1 0.0 copy-done.17
  220.1 0.0 copy-done.19
  220.1 0.0 copy-done.21
  220.1 0.0 copy-done.22
  220.1 0.0 copy-done.23
  220.1 0.0 copy-done.24
  220.1 0.0 copy-done.25
  220.2 0.0 copy-done.26
  220.2 0.0 copy-done.27
  220.2 0.9 copy-done.9
  221.1 0.7 copy-done.28
  221.8 1.1 update.1
  (14 shorter events, 0.0 us)
Async XLA Ops:
  0.7 0.8 copy-start.2
  1.5 0.8 copy-start.4
  2.3 0.8 copy-start.6
  3.1 0.8 copy-start.8
  3.9 0.7 copy-start.10
  4.6 0.7 copy-start.18
  5.3 0.7 copy-start.20
  31.1 1.0 copy-start
  32.2 1.0 copy-start.1
  33.1 186.8 %copy-start.3 = (f32[4,32,64]{2,1,0:T(8,128)S(1)}, f32[4,32,64]{2,1,0:T(8,128)}, u32[]{:S(2)}) copy-start(f32[4,32,64]{2,1,0:T(8,128)} %refs_3_.1) | copy-start | bytes 98308
  33.2 186.9 %copy-start.5 = (f32[4,64,32]{1,2,0:T(8,128)S(1)}, f32[4,64,32]{1,2,0:T(8,128)}, u32[]{:S(2)}) copy-start(f32[4,64,32]{1,2,0:T(8,128)} %param.38) | copy-start | bytes 98308
  33.2 186.9 %copy-start.7 = (f32[8,1238]{1,0:T(8,128)S(1)}, f32[8,1238]{1,0:T(8,128)}, u32[]{:S(2)}) copy-start(f32[8,1238]{1,0:T(8,128)} %refs_9_.1) | copy-start | bytes 118852
  33.2 186.9 %copy-start.11 = (f32[64,32]{0,1:T(8,128)S(1)}, f32[64,32]{0,1:T(8,128)}, u32[]{:S(2)}) copy-start(f32[64,32]{0,1:T(8,128)} %param.32) | copy-start | bytes 24580
  33.2 186.9 %copy-start.12 = (f32[4,32,64]{2,1,0:T(8,128)S(1)}, f32[4,32,64]{2,1,0:T(8,128)}, u32[]{:S(2)}) copy-start(f32[4,32,64]{2,1,0:T(8,128)} %refs_4_.1) | copy-start | bytes 98308
  33.2 186.9 %copy-start.13 = (f32[4,32,64]{2,1,0:T(8,128)S(1)}, f32[4,32,64]{2,1,0:T(8,128)}, u32[]{:S(2)}) copy-start(f32[4,32,64]{2,1,0:T(8,128)} %refs_5_.1) | copy-start | bytes 98308
  33.2 186.9 %copy-start.14 = (f32[4,64,32]{1,2,0:T(8,128)S(1)}, f32[4,64,32]{1,2,0:T(8,128)}, u32[]{:S(2)}) copy-start(f32[4,64,32]{1,2,0:T(8,128)} %param.39) | copy-start | bytes 98308
  33.2 186.9 %copy-start.15 = (f32[4,64,32]{1,2,0:T(8,128)S(1)}, f32[4,64,32]{1,2,0:T(8,128)}, u32[]{:S(2)}) copy-start(f32[4,64,32]{1,2,0:T(8,128)} %param.40) | copy-start | bytes 98308
  33.2 186.9 %copy-start.16 = (f32[8,1238]{1,0:T(8,128)S(1)}, f32[8,1238]{1,0:T(8,128)}, u32[]{:S(2)}) copy-start(f32[8,1238]{1,0:T(8,128)} %refs_10_.1) | copy-start | bytes 118852
  33.2 186.9 %copy-start.17 = (f32[8,1238]{1,0:T(8,128)S(1)}, f32[8,1238]{1,0:T(8,128)}, u32[]{:S(2)}) copy-start(f32[8,1238]{1,0:T(8,128)} %refs_11_.1) | copy-start | bytes 118852
  33.2 186.9 %copy-start.19 = (f32[5,2,8]{2,1,0:T(2,128)S(1)}, f32[5,2,8]{2,1,0:T(2,128)}, u32[]{:S(2)}) copy-start(f32[5,2,8]{2,1,0:T(2,128)} %refs_15_.1) | copy-start | bytes 964
  33.2 186.9 %copy-start.21 = (f32[32,8]{0,1:T(8,128)S(1)}, f32[32,8]{0,1:T(8,128)}, u32[]{:S(2)}) copy-start(f32[32,8]{0,1:T(8,128)} %param.44) | copy-start | bytes 3076
  33.3 186.9 %copy-start.22 = (f32[64,32]{0,1:T(8,128)S(1)}, f32[64,32]{0,1:T(8,128)}, u32[]{:S(2)}) copy-start(f32[64,32]{0,1:T(8,128)} %param.33) | copy-start | bytes 24580
  33.3 186.9 %copy-start.23 = (f32[64,32]{0,1:T(8,128)S(1)}, f32[64,32]{0,1:T(8,128)}, u32[]{:S(2)}) copy-start(f32[64,32]{0,1:T(8,128)} %param.34) | copy-start | bytes 24580
  33.3 186.9 %copy-start.24 = (f32[5,2,8]{2,1,0:T(2,128)S(1)}, f32[5,2,8]{2,1,0:T(2,128)}, u32[]{:S(2)}) copy-start(f32[5,2,8]{2,1,0:T(2,128)} %refs_16_.1) | copy-start | bytes 964
  33.3 186.9 %copy-start.25 = (f32[5,2,8]{2,1,0:T(2,128)S(1)}, f32[5,2,8]{2,1,0:T(2,128)}, u32[]{:S(2)}) copy-start(f32[5,2,8]{2,1,0:T(2,128)} %refs_17_.1) | copy-start | bytes 964
  33.3 186.8 %copy-start.26 = (f32[32,8]{0,1:T(8,128)S(1)}, f32[32,8]{0,1:T(8,128)}, u32[]{:S(2)}) copy-start(f32[32,8]{0,1:T(8,128)} %param.45) | copy-start | bytes 3076
  33.3 186.8 %copy-start.27 = (f32[32,8]{0,1:T(8,128)S(1)}, f32[32,8]{0,1:T(8,128)}, u32[]{:S(2)}) copy-start(f32[32,8]{0,1:T(8,128)} %param.46) | copy-start | bytes 3076
  220.2 0.9 copy-start.9
  221.1 0.7 copy-start.28

commit v2 on v1

--- a/solution.py
+++ b/solution.py
@@ -35,8 +35,10 @@
 GELU_B = GELU_A * 0.044715
 LOG2E = 1.4426950408889634
 LANES = 256
-CHAINS = 2
-CHUNK = 16
+CHAINS = 4
+PARTS = 4
+UNIT, DELAY, STAGGER = 90, 250, 200
+CHUNK = 32
 BF = jnp.bfloat16
 F32 = jnp.float32
 MESH = pl.DeviceIdType.MESH
@@ -127,17 +129,23 @@
         self.per = 128 // self.wide
         self.groups = -(-MATRICES // self.per)
         self.head_at = self.groups * self.deep
-        self.tail_at = -(-(self.head_at + self.own * (DEPTH // 128)) // 8) * 8
-        self.rows = -(-(self.tail_at + 16) // 32) * 32
-        self.half = self.rows // 2
-        self.orders = orders_of(dp, mp)
+        self.tail_at = -(-(self.head_at + self.own * (DEPTH // 128)) // 16) * 16
+        self.rows = -(-(self.tail_at + 16) // (16 * PARTS)) * 16 * PARTS
+        self.part = self.rows // PARTS
+        self.orders = [orders_of(dp, mp)[number % 2] for number in range(PARTS)]
         self.sizes = [sizes_of(order) for order in self.orders]
         self.most = max(step[2] for step in self.orders[0])
 
     def split(self, begin, end):
-        side = 1 if begin >= self.half else 0
-        assert begin >= self.half or end <= self.half
-        return side, slice(begin - side * self.half, end - side * self.half)
+        side = begin // self.part
+        assert (end - 1) // self.part == side
+        return side, slice(begin - side * self.part, end - side * self.part)
+
+    def shapes(self, dtype):
+        return [jax.ShapeDtypeStruct((self.count, self.part, 128), dtype)] * PARTS
+
+    def scratch(self, dtype):
+        return [pltpu.VMEM((self.count, self.part, 128), dtype)] * PARTS
 
 
 def pad_lanes(array, lanes):
@@ -177,8 +185,10 @@
     )
 
 
-def send_kernel(packing, stem, up, down, head, table, norm, weight, near, far, block, send_sem, recv_sem):
-    kinds = (near, far)
+def send_kernel(packing, *refs):
+    stem, up, down, head, table, norm, weight = refs[:7]
+    outs, kinds = refs[7 : 7 + PARTS], refs[7 + PARTS : 7 + 2 * PARTS]
+    block, send_sem, recv_sem, keep_sem = refs[7 + 2 * PARTS :]
     partners = [(step, away) for step in packing.orders[0] for away in range(1, step[2])]
     barrier = pltpu.get_barrier_semaphore()
     for step, away in partners:
@@ -205,8 +215,8 @@
         amount = amount - part
     data, model = lax.axis_index("dp"), lax.axis_index("mp")
     slots = [slot_of(order, data, model) for order in packing.orders]
-    for side in range(2):
-        kinds[side][slots[side]] = block[side * packing.half : (side + 1) * packing.half, :].astype(BF)
+    for side in range(PARTS):
+        kinds[side][slots[side]] = block[side * packing.part : (side + 1) * packing.part, :].astype(BF)
 
     pl.semaphore_wait(barrier, len(partners))
 
@@ -225,17 +235,33 @@
             for away in range(1, step[2])
         ]
 
+    def kept(side, start, size, sem):
+        return pltpu.make_async_copy(
+            kinds[side].at[pl.ds(start, size)], outs[side].at[pl.ds(start, size)], keep_sem.at[side, sem]
+        )
+
     steps = len(packing.orders[0])
-    copies = [[copies_of(side, number) for number in range(steps)] for side in range(2)]
+    copies = [[copies_of(side, number) for number in range(steps)] for side in range(PARTS)]
+    local = [kept(side, slots[side], 1, 0) for side in range(PARTS)]
+    for member in local:
+        member.start()
     for number in range(steps + 1):
-        for side in range(2):
+        for side in range(PARTS):
             if number:
                 for member in copies[side][number - 1]:
                     member.wait_recv()
             if number < steps:
                 for member in copies[side][number]:
                     member.start()
-    for side in range(2):
+            if number:
+                step, size = packing.orders[side][number - 1], packing.sizes[side][number - 1]
+                for away in range(1, step[2]):
+                    start = (slots[side] // size) * size + partner_of(step, away)[1] * size
+                    local.append(kept(side, start, size, number * packing.most + away))
+                    local[-1].start()
+    for member in local:
+        member.wait()
+    for side in range(PARTS):
         for number in range(steps):
             for member in copies[side][number]:
                 member.wait_send()
@@ -243,43 +269,29 @@
 
 def send_weights(packing, stem, up, down, head, table, norm, weight):
     steps = len(packing.orders[0])
-    shape = jax.ShapeDtypeStruct((packing.count, packing.half, 128), BF)
     return pl.pallas_call(
         functools.partial(send_kernel, packing),
-        out_shape=[shape, shape],
+        out_shape=packing.shapes(BF),
         in_specs=[pl.BlockSpec()] * 7,
-        out_specs=[pl.BlockSpec(memory_space=pltpu.VMEM)] * 2,
-        scratch_shapes=[
+        out_specs=[pl.BlockSpec(memory_space=pl.ANY)] * PARTS,
+        scratch_shapes=packing.scratch(BF)
+        + [
             pltpu.VMEM((packing.rows, 128), F32),
-            pltpu.SemaphoreType.DMA((2, steps, packing.most)),
-            pltpu.SemaphoreType.DMA((2, steps, packing.most)),
+            pltpu.SemaphoreType.DMA((PARTS, steps, packing.most)),
+            pltpu.SemaphoreType.DMA((PARTS, steps, packing.most)),
+            pltpu.SemaphoreType.DMA((PARTS, (steps + 1) * packing.most)),
         ],
         compiler_params=pltpu.CompilerParams(
-            collective_id=0, has_side_effects=True, vmem_limit_bytes=48 * 1024 * 1024
+            collective_id=0, has_side_effects=True, vmem_limit_bytes=60 * 1024 * 1024
         ),
         name="send_weights",
     )(stem, up, down, head, table, norm, weight)
 
 
-def reduce_kernel(
-    packing,
-    near_in,
-    far_in,
-    own,
-    squares,
-    near,
-    far,
-    near_out,
-    far_out,
-    near_got,
-    far_got,
-    across,
-    along,
-    send_sem,
-    recv_sem,
-    part_send,
-    part_recv,
-):
+def reduce_kernel(packing, *refs):
+    given, own = refs[:PARTS], refs[PARTS]
+    held, sent, got = (refs[PARTS * kind + 1 : PARTS * (kind + 1) + 1] for kind in (1, 2, 3))
+    across, along, send_sem, recv_sem, part_send, part_recv = refs[4 * PARTS + 1 :]
     steps = len(packing.orders[0])
     data, model = lax.axis_index("dp"), lax.axis_index("mp")
     barrier = pltpu.get_barrier_semaphore()
@@ -289,7 +301,6 @@
         pl.semaphore_signal(barrier, inc=1, device_id={"dp": (data + away) % packing.dp}, device_id_type=MESH)
 
     slots = [slot_of(order, data, model) for order in packing.orders]
-    given, held, sent, got = (near_in, far_in), (near, far), (near_out, far_out), (near_got, far_got)
 
     def source_of(side, number):
         return given[side] if number == steps - 1 else held[side]
@@ -329,12 +340,12 @@
             total = total + got[side][place_of(side, number, away)].astype(F32)
         held[side][rows] = total
 
-    copies = [[copies_of(side, number) for number in range(steps)] for side in range(2)]
-    for side in range(2):
+    copies = [[copies_of(side, number) for number in range(steps)] for side in range(PARTS)]
+    for side in range(PARTS):
         pack(side, steps - 1)
     pl.semaphore_wait(barrier, packing.mp + packing.dp - 2)
     for number in range(steps - 1, -1, -1):
-        for side in range(2):
+        for side in range(PARTS):
             if number < steps - 1:
                 for member in copies[side][number + 1]:
                     member.wait_recv()
@@ -343,12 +354,12 @@
             for member in copies[side][number]:
                 member.start()
     total = None
-    for side in range(2):
+    for side in range(PARTS):
         for member in copies[side][0]:
             member.wait_recv()
         take(side, 0)
         block = held[side][slots[side]]
-        own[side * packing.half : (side + 1) * packing.half, :] = block
+        own[side * packing.part : (side + 1) * packing.part, :] = block
         total = fold_rows(total, block * block)
 
     def exchange(axis, index, count, buffer, value, first):
@@ -375,30 +386,30 @@
 
     total, going = exchange("mp", model, packing.mp, across, total, 0)
     total, more = exchange("dp", data, packing.dp, along, total, packing.mp)
-    squares[...] = total
+    own[packing.rows : packing.rows + 8, :] = total
     for member in going + more:
         member.wait_send()
-    for side in range(2):
+    for side in range(PARTS):
         for number in range(steps):
             for member in copies[side][number]:
                 member.wait_send()
 
 
-def reduce_grads(packing, near, far):
+def reduce_grads(packing, grads):
     steps = len(packing.orders[0])
     vmem = pl.BlockSpec(memory_space=pltpu.VMEM)
     return pl.pallas_call(
         functools.partial(reduce_kernel, packing),
-        out_shape=[jax.ShapeDtypeStruct((packing.rows, 128), F32), jax.ShapeDtypeStruct((8, 128), F32)],
-        in_specs=[vmem] * 2,
-        out_specs=[vmem] * 2,
-        scratch_shapes=[pltpu.VMEM((packing.count, packing.half, 128), F32)] * 2
-        + [pltpu.VMEM((packing.count, packing.half, 128), BF)] * 4
+        out_shape=jax.ShapeDtypeStruct((packing.rows + 8, 128), F32),
+        in_specs=[vmem] * PARTS,
+        out_specs=vmem,
+        scratch_shapes=packing.scratch(F32)
+        + packing.scratch(BF) * 2
         + [
             pltpu.VMEM((packing.mp, 8, 128), F32),
             pltpu.VMEM((packing.dp, 8, 128), F32),
-            pltpu.SemaphoreType.DMA((2, steps, packing.most)),
-            pltpu.SemaphoreType.DMA((2, steps, packing.most)),
+            pltpu.SemaphoreType.DMA((PARTS, steps, packing.most)),
+            pltpu.SemaphoreType.DMA((PARTS, steps, packing.most)),
             pltpu.SemaphoreType.DMA((packing.mp + packing.dp,)),
             pltpu.SemaphoreType.DMA((packing.mp + packing.dp,)),
         ],
@@ -406,7 +417,7 @@
             collective_id=1, has_side_effects=True, vmem_limit_bytes=60 * 1024 * 1024
         ),
         name="reduce_grads",
-    )(near, far)
+    )(*grads)
 
 
 def adam_rows(weight, moment, square, grad, rate, decay):
@@ -418,10 +429,11 @@
     return (updated, first, second)
 
 
-def update_kernel(packing, rows_all, own, squares, *refs):
+def update_kernel(packing, rows_all, own, *refs):
     ins, outs = refs[:18], refs[18:]
     grad_norm, outs = outs[0], outs[1:]
-    whole = jnp.sum(jnp.sum(squares[...], axis=0, keepdims=True), axis=1, keepdims=True)
+    squares = own[packing.rows : packing.rows + 8, :]
+    whole = jnp.sum(jnp.sum(squares, axis=0, keepdims=True), axis=1, keepdims=True)
     norm = jnp.sqrt(whole)
     grad_norm[...] = norm
     ratio = jnp.minimum(1.0, clip_scale * math.sqrt(rows_all) / norm)
@@ -462,7 +474,7 @@
         )
 
 
-def update(packing, rows_all, own, squares, groups):
+def update(packing, rows_all, own, groups):
     ins = [member for group in groups for member in group]
     outs = [jax.ShapeDtypeStruct((1, 1), F32)]
     for which, group in enumerate(groups):
@@ -472,11 +484,11 @@
     return pl.pallas_call(
         functools.partial(update_kernel, packing, rows_all),
         out_shape=outs,
-        in_specs=[pl.BlockSpec()] * (2 + len(ins)),
+        in_specs=[pl.BlockSpec()] * (1 + len(ins)),
         out_specs=[pl.BlockSpec()] * len(outs),
         compiler_params=pltpu.CompilerParams(vmem_limit_bytes=48 * 1024 * 1024),
         name="update",
-    )(own, squares, *ins)
+    )(own, *ins)
 
 
 def train_kernel(
@@ -490,11 +502,10 @@
     reward_ref,
     action_ref,
     target_ref,
-    near_in,
-    far_in,
-    lat_grad,
-    near_out,
-    far_out,
+    *refs,
+):
+    held, lat_grad, outs = refs[:PARTS], refs[PARTS], refs[PARTS + 1 : 2 * PARTS + 1]
+    (
     stem_acc,
     table_acc,
     up_acc,
@@ -509,8 +520,6 @@
     head_t,
     head_n,
     scale_s,
-    wide_s,
-    head_wide,
     stream_s,
     centered_s,
     slope_s,
@@ -527,31 +536,65 @@
     hot_s,
     norm_s,
     norm_part,
-):
+    ) = refs[2 * PARTS + 1 : -1]
     step = pl.program_id(0)
+    tiles_wide = logit_s.shape[1] // 128
+    chunks = packing.count * packing.part // D
+    copy_sem = refs[-1]
+
+    def chunk_at(buffers, chunk):
+        layers = buffers[0].shape[0]
+        which, chunk = divmod(chunk, layers * tiles_wide)
+        layer, tile = divmod(chunk, tiles_wide)
+        return buffers[which].at[layer, :, tile * 128 : (tile + 1) * 128]
+
+    def packed_at(buffers, side, slot):
+        chunk, row = divmod(slot * packing.part, D)
+        return chunk_at(buffers, side * chunks + chunk), row
+
+    def head_tile(tile):
+        return (
+            slice((tile // tiles_wide) * D, (tile // tiles_wide + 1) * D),
+            slice((tile % tiles_wide) * 128, (tile % tiles_wide + 1) * 128),
+        )
+
     devices = [(data, model) for data in range(packing.dp) for model in range(packing.mp)]
 
     @pl.when(step == 0)
     def _():
-        held = (near_in, far_in)
+        arrived = [
+            pltpu.make_async_copy(
+                held[side].at[chunk * D : (chunk + 1) * D],
+                chunk_at((act_s, gated_s), side * chunks + chunk),
+                copy_sem.at[side, chunk],
+            )
+            for side in range(PARTS)
+            for chunk in range(chunks)
+        ]
+        for member in arrived:
+            member.start()
+        for member in arrived:
+            member.wait()
 
         def rows_of(device, begin, end):
             side, rows = packing.split(begin, end)
-            return held[side][slot_of(packing.orders[side], *device)].astype(F32)[rows]
-
+            place, row = packed_at((act_s, gated_s), side, slot_of(packing.orders[side], *device))
+            return place[row : row + packing.part, :].astype(F32)[rows]
+
+        wide_s = [stem_acc] + [up_acc.at[layer] for layer in range(LAYERS)] + [down_acc.at[layer] for layer in range(LAYERS)]
         for data in range(packing.dp):
             for group in range(packing.groups):
                 begin = group * packing.deep
                 parts = [rows_of((data, model), begin, begin + packing.deep) for model in range(packing.mp)]
                 for member in range(min(packing.per, MATRICES - group * packing.per)):
                     lane = member * packing.wide
-                    wide_s[group * packing.per + member, data * packing.deep : (data + 1) * packing.deep, :] = (
+                    wide_s[group * packing.per + member][data * packing.deep : (data + 1) * packing.deep, :] = (
                         jnp.concatenate([part[:, lane : lane + packing.wide] for part in parts], axis=1)
                     )
-        stem_t[...] = wide_s[0].astype(BF)
+        stem_t[...] = wide_s[0][...].astype(BF)
         for layer in range(LAYERS):
-            half_up = 0.5 * wide_s[1 + layer]
-            half_down = 0.5 * wide_s[1 + LAYERS + layer]
+            half_up = 0.5 * wide_s[1 + layer][...]
+            half_down = 0.5 * wide_s[1 + LAYERS + layer][...]
             up_n[layer] = half_up.astype(BF)
             up_t[layer] = half_up.T.astype(BF)
             down_t[layer] = half_down.astype(BF)
@@ -562,7 +605,8 @@
             at = (device[0] * packing.mp + device[1]) * packing.own
             for tile in range(DEPTH // 128):
                 begin = packing.head_at + packing.own * tile
-                head_wide[at : at + packing.own, tile * 128 : (tile + 1) * 128] = rows_of(
+                rows, lanes = head_tile(tile)
+                logit_s[rows.start + at : rows.start + at + packing.own, lanes] = rows_of(
                     device, begin, begin + packing.own
                 )
             tail = rows_of(device, packing.tail_at, packing.tail_at + 16)
@@ -571,11 +615,12 @@
             amount = tail[SUM_ROW : SUM_ROW + 1] + tail[SUM_ROW + 1 : SUM_ROW + 2] + tail[SUM_ROW + 2 : SUM_ROW + 3]
             total = amount if total is None else total + amount
         table_t[...] = table_acc[...].astype(BF)
-        head_n[...] = head_wide[...].astype(BF)
-        for at in range(0, DEPTH, D):
-            turned = head_wide[:, at : at + D].T.astype(BF)
-            end = min(D, ROWS - at)
-            head_t[at : at + end, :] = turned[0:end]
+        for tile in range(DEPTH // 128):
+            at = tile * 128
+            whole = logit_s[head_tile(tile)]
+            head_n[:, at : at + 128] = whole.astype(BF)
+            end = min(128, ROWS - at)
+            head_t[at : at + end, :] = whole.T.astype(BF)[0:end]
         norms = jnp.concatenate(norm_parts, axis=1)
         columns = jnp.concatenate([norms, jnp.zeros((128 - norms.shape[0], D), F32)], axis=0).T
         for which in range(2 * (LAYERS + 1)):
@@ -600,6 +645,9 @@
             total = total + part[:, lane : lane + 128]
         norm_part[which, at : at + CHUNK, :] += total
 
+    def spans(count):
+        return [slice(at, min(at + CHUNK, count)) for at in range(0, count, CHUNK)]
+
     def chain(index):
         cols = slice(index * LANES, (index + 1) * LANES)
 
@@ -608,20 +656,23 @@
 
         def norm_forward(layer, total, sink):
             mean = jnp.sum(total, axis=0, keepdims=True) * (1.0 / D)
+            yield "wait", 40
             squares = None
-            for at in range(0, D, CHUNK):
-                rows = slice(at, at + CHUNK)
+            for rows in spans(D):
                 centered = stream_s[rows, cols] - mean
                 centered_s[layer, rows, cols] = centered
                 squares = fold_rows(squares, centered * centered)
+                yield "vector", 3
             spread = jnp.sum(squares, axis=0, keepdims=True) * (1.0 / D)
             rstd = lax.rsqrt(spread + eps_norm)
             rstd_s[layer, :, cols] = rstd
+            yield "wait", 60
             total = None
-            for at in range(0, D, CHUNK):
-                rows = slice(at, at + CHUNK)
+            for rows in spans(D):
                 scaled = centered_s[layer, rows, cols] * rstd
-                value, slope = gelu_pair(scaled * norm_rows(2 * layer, at) + norm_rows(2 * layer + 1, at))
+                value, slope = gelu_pair(
+                    scaled * norm_rows(2 * layer, rows.start) + norm_rows(2 * layer + 1, rows.start)
+                )
                 if sink is None:
                     value = 0.5 * value
                     slope_s[layer, rows, cols] = 0.5 * slope
@@ -630,64 +681,62 @@
                 else:
                     slope_s[layer, rows, cols] = slope
                     sink[layer - 1, rows, cols] = value.astype(BF)
+                yield "vector", 16
             return total
 
         def norm_backward(layer, grad_of, emit):
             rstd = rstd_s[layer, :, cols]
             first = second = None
-            for at in range(0, D, CHUNK):
-                rows = slice(at, at + CHUNK)
+            for rows in spans(D):
                 grad = grad_of(rows) * slope_s[layer, rows, cols]
                 centered = centered_s[layer, rows, cols]
-                add_norm(2 * layer + 1, at, grad)
+                add_norm(2 * layer + 1, rows.start, grad)
                 grad = grad * rstd
-                add_norm(2 * layer, at, grad * centered)
-                wide = grad * norm_rows(2 * layer, at)
+                add_norm(2 * layer, rows.start, grad * centered)
+                wide = grad * norm_rows(2 * layer, rows.start)
                 slope_s[layer, rows, cols] = wide
                 first = fold_rows(first, wide)
                 second = fold_rows(second, wide * centered)
+                yield "vector", 9
             shift = jnp.sum(first, axis=0, keepdims=True) * (1.0 / D)
             slant = jnp.sum(second, axis=0, keepdims=True) * (1.0 / D) * (rstd * rstd)
-            for at in range(0, D, CHUNK):
-                rows = slice(at, at + CHUNK)
+            yield "wait", 50
+            for rows in spans(D):
                 emit(rows, (slope_s[layer, rows, cols] - shift) - centered_s[layer, rows, cols] * slant)
+                yield "vector", 5
 
         hot = (lax.broadcasted_iota(jnp.int32, (CODES, LANES), 0) == row_of(code_ref)).astype(F32).astype(BF)
         hot_s[:, cols] = hot
         pre = dot_nt(stem_t[...], lat_ref[cols, :]) + dot_nn(table_t[...], hot)
-        yield
+        yield "product", 2
         total = None
-        for at in range(0, D, CHUNK):
-            rows = slice(at, at + CHUNK)
+        for rows in spans(D):
             stream_s[rows, cols] = pre[rows]
             total = fold_rows(total, pre[rows])
-        total = norm_forward(0, total, None)
-        yield
+            yield "vector", 2
+        total = yield from norm_forward(0, total, None)
         for layer in range(1, LAYERS + 1):
-            norm_forward(layer, total, act_s)
-            yield
+            yield from norm_forward(layer, total, act_s)
             inner = dot_nn(up_t[layer - 1], act_s[layer - 1, :, cols])
-            yield
-            for at in range(0, D, CHUNK):
-                rows = slice(at, at + CHUNK)
+            yield "product", 1
+            for rows in spans(D):
                 value, slope = gelu_pair(inner[rows])
                 inner_slope_s[layer - 1, rows, cols] = slope
                 gated_s[layer - 1, rows, cols] = value.astype(BF)
-            yield
+                yield "vector", 13
             branch = dot_nn(down_t[layer - 1], gated_s[layer - 1, :, cols])
-            yield
+            yield "product", 1
             total = None
-            for at in range(0, D, CHUNK):
-                rows = slice(at, at + CHUNK)
+            for rows in spans(D):
                 stream = stream_s[rows, cols] + branch[rows]
                 if layer < LAYERS:
                     stream_s[rows, cols] = stream
                     total = fold_rows(total, stream)
                 else:
                     top_s[rows, cols] = stream.astype(BF)
-        yield
+                yield "vector", 2
         logit_s[:, cols] = dot_nn(head_t[...], top_s[:, cols])
-        yield
+        yield "product", 5
         coef = row_of(weight_ref).astype(F32) * scale_s[...]
         sections = (
             (VALUE_AT, BINS, value_ref),
@@ -702,153 +751,202 @@
                 keep = lax.broadcasted_iota(jnp.int32, (8, LANES), 0) < count - (padded - 8)
                 logit_s[last, cols] = jnp.where(keep, logit_s[last, cols], -1e30)
             peak = None
-            for at in range(0, padded, CHUNK):
-                rows = slice(begin + at, begin + min(at + CHUNK, padded))
+            for part in spans(padded):
+                rows = slice(begin + part.start, begin + part.stop)
                 peak = peak_rows(peak, logit_s[rows, cols])
+                yield "vector", 1
             peak = jnp.max(peak, axis=0, keepdims=True)
+            yield "wait", 40
             mass = None
-            for at in range(0, padded, CHUNK):
-                rows = slice(begin + at, begin + min(at + CHUNK, padded))
+            for part in spans(padded):
+                rows = slice(begin + part.start, begin + part.stop)
                 power = jnp.exp2((logit_s[rows, cols] - peak) * LOG2E)
                 logit_s[rows, cols] = power
                 mass = fold_rows(mass, power)
+                yield "vector", 4
             scale = coef / jnp.sum(mass, axis=0, keepdims=True)
             target = row_of(target_ref_of)
+            yield "wait", 60
             stored = -(-count // 16) * 16
-            for at in range(0, padded, CHUNK):
-                end = min(at + CHUNK, padded)
-                rows = slice(begin + at, begin + end)
+            for part in spans(padded):
+                rows = slice(begin + part.start, begin + part.stop)
                 soft = logit_s[rows, cols] * scale
-                place = lax.broadcasted_iota(jnp.int32, soft.shape, 0) + at
+                place = lax.broadcasted_iota(jnp.int32, soft.shape, 0) + part.start
                 soft = jnp.where(place == target, soft - coef, soft)
-                if end == padded and padded != stored:
+                if part.stop == padded and padded != stored:
                     soft = jnp.concatenate([soft, jnp.zeros((stored - padded, LANES), F32)], axis=0)
-                    rows = slice(begin + at, begin + stored)
+                    rows = slice(begin + part.start, begin + stored)
                 low_s[rows, cols] = soft.astype(BF)
-            yield
+                yield "vector", 5
+        yield "ready", "head"
         grad = dot_nn(head_n[...], low_s[:, cols])
-        yield
-        if index == chains - 1:
-            head_acc[...] += dot_nt(low_s[0:ROWS, :], top_s[...])
+        yield "product", 5
+        for rows in spans(D):
+            stream_s[rows, cols] = grad[rows]
+            branch_s[LAYERS % 2, rows, cols] = grad[rows].astype(BF)
+            yield "vector", 1
         for layer in range(LAYERS, 0, -1):
-            if layer == LAYERS:
-                for at in range(0, D, CHUNK):
-                    rows = slice(at, at + CHUNK)
-                    stream_s[rows, cols] = grad[rows]
-                    branch_s[layer - 1, rows, cols] = grad[rows].astype(BF)
-            yield
-            gated_grad = dot_nn(down_n[layer - 1], branch_s[layer - 1, :, cols])
-            yield
-            for at in range(0, D, CHUNK):
-                rows = slice(at, at + CHUNK)
-                inner_grad_s[layer - 1, rows, cols] = (
+            gated_grad = dot_nn(down_n[layer - 1], branch_s[layer % 2, :, cols])
+            yield "product", 1
+            if layer + 2 <= LAYERS:
+                yield "until", ("block", layer + 2)
+            for rows in spans(D):
+                inner_grad_s[layer % 2, rows, cols] = (
                     gated_grad[rows] * inner_slope_s[layer - 1, rows, cols]
                 ).astype(BF)
-            yield
-            active_grad = dot_nn(up_n[layer - 1], inner_grad_s[layer - 1, :, cols])
-            if index == chains - 1:
-                down_acc[layer - 1] += dot_nt(branch_s[layer - 1], gated_s[layer - 1])
-                up_acc[layer - 1] += dot_nt(act_s[layer - 1], inner_grad_s[layer - 1])
-            yield
+                yield "vector", 2
+            active_grad = dot_nn(up_n[layer - 1], inner_grad_s[layer % 2, :, cols])
+            yield "product", 1
+            yield "ready", ("block", layer)
 
             def emit(rows, change, layer=layer):
                 stream = stream_s[rows, cols] + change
                 stream_s[rows, cols] = stream
                 if layer > 1:
-                    branch_s[layer - 2, rows, cols] = stream.astype(BF)
-
-            norm_backward(layer, lambda rows: active_grad[rows], emit)
-            yield
+                    branch_s[(layer - 1) % 2, rows, cols] = stream.astype(BF)
+
+            if layer + 1 <= LAYERS:
+                yield "until", ("block", layer + 1)
+            yield from norm_backward(layer, lambda rows: active_grad[rows], emit)
 
         def emit_pre(rows, change):
             pre_s[rows, cols] = change.astype(BF)
 
-        norm_backward(0, lambda rows: stream_s[rows, cols], emit_pre)
-        yield
+        yield from norm_backward(0, lambda rows: stream_s[rows, cols], emit_pre)
         lat_grad[cols, :] = dot_tn(pre_s[:, cols], stem_t[...])
-        yield
-
-    running = []
-    waiting = [chain(index) for index in range(chains)]
-    while running or waiting:
-        if waiting:
-            running.append(waiting.pop(0))
-        for member in list(running):
-            try:
-                next(member)
-            except StopIteration:
-                running.remove(member)
-
-    stem_acc[...] += dot_nn(pre_s[...], lat_ref[...])
-    table_acc[...] += dot_nt(pre_s[...], hot_s[...])
+        yield "product", 1
+        yield "ready", "stem"
+
+    def weight_grads(what):
+        if what == "head":
+            head_acc[...] += dot_nt(low_s[0:ROWS, :], top_s[...])
+        elif what == "stem":
+            stem_acc[...] += dot_nn(pre_s[...], lat_ref[...])
+            table_acc[...] += dot_nt(pre_s[...], hot_s[...])
+        else:
+            layer = what[1]
+            down_acc[layer - 1] += dot_nt(branch_s[layer % 2], gated_s[layer - 1])
+            up_acc[layer - 1] += dot_nt(act_s[layer - 1], inner_grad_s[layer % 2])
+
+    members = [chain(index) for index in range(chains)]
+    ready_at, progress = [0] * chains, [index * STAGGER for index in range(chains)]
+    now = product_free = 0
+    counts, done, until = {}, set(), [None] * chains
+    while members.count(None) < chains:
+        alive = [index for index in range(chains) if members[index] is not None]
+        alive = [index for index in alive if until[index] is None or until[index] in done]
+        able = [index for index in alive if ready_at[index] <= now]
+        if not able:
+            now = min(ready_at[index] for index in alive)
+            continue
+        index = min(able, key=lambda number: progress[number])
+        try:
+            kind, amount = next(members[index])
+        except StopIteration:
+            members[index] = None
+            continue
+        if kind == "vector":
+            cost = amount * (CHUNK // 8) * (LANES // 128) / 3
+            now += cost
+            progress[index] += cost
+        elif kind == "product":
+            product_free = max(now, product_free) + amount * UNIT
+            ready_at[index] = product_free + DELAY
+            progress[index] += amount * UNIT
+        elif kind == "wait":
+            ready_at[index] = now + amount
+        elif kind == "until":
+            until[index] = amount
+        else:
+            counts[amount] = counts.get(amount, 0) + 1
+            if counts[amount] == chains:
+                weight_grads(amount)
+                done.add(amount)
+                product_free = max(now, product_free) + UNIT * chains * (5 if amount == "head" else 2)
 
     @pl.when(step == pl.num_programs(0) - 1)
     def _():
-        outs = (near_out, far_out)
-        near_out[...] = jnp.zeros_like(near_out)
-        far_out[...] = jnp.zeros_like(far_out)
-        for at in range(0, DEPTH, D):
-            end = min(D, ROWS - at)
+        for tile in range(DEPTH // 128):
+            at = tile * 128
+            end = min(128, ROWS - at)
             turned = head_acc[at : at + end, :]
-            if end < D:
-                turned = jnp.concatenate([turned, jnp.zeros((D - end, D), F32)], axis=0)
-            head_wide[:, at : at + D] = turned.T
+            if end < 128:
+                turned = jnp.concatenate([turned, jnp.zeros((128 - end, D), F32)], axis=0)
+            logit_s[head_tile(tile)] = turned.T
         lane_at = lax.broadcasted_iota(jnp.int32, (D, 128), 1)
         columns = jnp.zeros((D, 128), F32)
         for which in range(2 * (LAYERS + 1)):
             columns = jnp.where(lane_at == which, jnp.sum(norm_part[which], axis=1, keepdims=True), columns)
         norms = columns.T[0:16]
-        for device in devices:
-            data, model = device
+        def pieces_of(data, model):
             at = (data * packing.mp + model) * packing.own
-            slots = [slot_of(order, data, model) for order in packing.orders]
-
-            def keep(begin, value, lanes=slice(0, 128)):
-                side, rows = packing.split(begin, begin + value.shape[0])
-                outs[side][slots[side], rows, lanes] = value
-
             deep = slice(data * packing.deep, (data + 1) * packing.deep)
             wide = slice(model * packing.wide, (model + 1) * packing.wide)
-            pieces = [stem_acc[deep, wide]] + [0.5 * up_acc[layer, deep, wide] for layer in range(LAYERS)]
-            pieces += [0.5 * down_acc[layer, deep, wide] for layer in range(LAYERS)]
+            squares = [lambda: stem_acc[deep, wide]]
+            squares += [lambda layer=layer: 0.5 * up_acc[layer, deep, wide] for layer in range(LAYERS)]
+            squares += [lambda layer=layer: 0.5 * down_acc[layer, deep, wide] for layer in range(LAYERS)]
             for group in range(packing.groups):
-                members = pieces[group * packing.per : (group + 1) * packing.per]
-                keep(group * packing.deep, pad_lanes(jnp.concatenate(members, axis=1), 128))
+                members = squares[group * packing.per : (group + 1) * packing.per]
+                yield (
+                    group * packing.deep,
+                    slice(0, packing.wide * len(members)),
+                    lambda members=members: jnp.concatenate([member() for member in members], axis=1),
+                )
             for tile in range(DEPTH // 128):
-                keep(
+                rows, lanes = head_tile(tile)
+                rows = slice(rows.start + at, rows.start + at + packing.own)
+                yield (
                     packing.head_at + packing.own * tile,
-                    head_wide[at : at + packing.own, tile * 128 : (tile + 1) * 128],
+                    slice(0, 128),
+                    lambda rows=rows, lanes=lanes: logit_s[rows, lanes],
                 )
-            keep(packing.tail_at, table_acc[at : at + packing.own, :], slice(0, CODES))
-            keep(
+            own = slice(at, at + packing.own)
+            yield packing.tail_at, slice(0, CODES), lambda: table_acc[own, :]
+            yield (
                 packing.tail_at,
-                norms[0 : 2 * (LAYERS + 1), at : at + packing.own],
                 slice(NORM_LANE, NORM_LANE + packing.own),
+                lambda: norms[0 : 2 * (LAYERS + 1), own],
             )
 
-
-def train(packing, rows_all, latent, code, weight, value, reward, action, target, near, far):
+        leaving = []
+        for side in range(PARTS):
+            owners = {slot_of(packing.orders[side], *device): device for device in devices}
+            for chunk in range(chunks):
+                place = chunk_at((centered_s, slope_s), side * chunks + chunk)
+                place[...] = jnp.zeros((D, 128), F32)
+                for row in range(0, D, packing.part):
+                    for begin, lanes, value in pieces_of(*owners[(chunk * D + row) // packing.part]):
+                        if begin // packing.part == side:
+                            rows = value()
+                            first = row + begin - side * packing.part
+                            place[first : first + rows.shape[0], lanes] = rows
+                leaving.append(
+                    pltpu.make_async_copy(
+                        place, outs[side].at[chunk * D : (chunk + 1) * D], copy_sem.at[side, chunk]
+                    )
+                )
+                leaving[-1].start()
+        for member in leaving:
+            member.wait()
+
+
+def train(packing, rows_all, latent, code, weight, value, reward, action, target, packed):
     count = latent.shape[0]
     chains = CHAINS
     block = chains * LANES
 
-    def full(shape):
-        return pl.BlockSpec(shape, lambda i: (0,) * len(shape), pipeline_mode=pl.Buffered(1))
-
     def row():
         return pl.BlockSpec((block,), lambda i: (i,))
 
-    packed = (packing.count, packing.half, 128)
+    parts = [pl.BlockSpec(memory_space=pl.ANY)] * PARTS
+    flat = jax.ShapeDtypeStruct((packing.count * packing.part, 128), F32)
+    packed = [member.reshape(-1, 128) for member in packed]
     return pl.pallas_call(
         functools.partial(train_kernel, packing, rows_all, chains),
         grid=(count // block,),
-        out_shape=[
-            jax.ShapeDtypeStruct((count, D), F32),
-            jax.ShapeDtypeStruct(packed, F32),
-            jax.ShapeDtypeStruct(packed, F32),
-        ],
-        in_specs=[pl.BlockSpec((block, D), lambda i: (i, 0))] + [row() for _ in range(6)] + [full(packed)] * 2,
-        out_specs=[pl.BlockSpec((block, D), lambda i: (i, 0))] + [full(packed)] * 2,
+        out_shape=[jax.ShapeDtypeStruct((count, D), F32)] + [flat] * PARTS,
+        in_specs=[pl.BlockSpec((block, D), lambda i: (i, 0))] + [row() for _ in range(6)] + parts,
+        out_specs=[pl.BlockSpec((block, D), lambda i: (i, 0))] + parts,
         scratch_shapes=[
             pltpu.VMEM((D, D), F32),
             pltpu.VMEM((D, CODES), F32),
@@ -864,8 +962,6 @@
             pltpu.VMEM((ROWS, D), BF),
             pltpu.VMEM((D, DEPTH), BF),
             pltpu.VMEM((1, LANES), F32),
-            pltpu.VMEM((MATRICES, D, D), F32),
-            pltpu.VMEM((D, DEPTH), F32),
             pltpu.VMEM((D, block), F32),
             pltpu.VMEM((LAYERS + 1, D, block), F32),
             pltpu.VMEM((LAYERS + 1, D, block), F32),
@@ -873,8 +969,8 @@
             pltpu.VMEM((LAYERS + 1, 1, block), F32),
             pltpu.VMEM((LAYERS, D, block), BF),
             pltpu.VMEM((LAYERS, D, block), BF),
-            pltpu.VMEM((LAYERS, D, block), BF),
-            pltpu.VMEM((LAYERS, D, block), BF),
+            pltpu.VMEM((2, D, block), BF),
+            pltpu.VMEM((2, D, block), BF),
             pltpu.VMEM((ROWS, block), F32),
             pltpu.VMEM((DEPTH, block), BF),
             pltpu.VMEM((D, block), BF),
@@ -882,12 +978,13 @@
             pltpu.VMEM((CODES, block), BF),
             pltpu.VMEM((2 * (LAYERS + 1), D, 128), F32),
             pltpu.VMEM((2 * (LAYERS + 1), D, 128), F32),
+            pltpu.SemaphoreType.DMA((PARTS, packing.count * packing.part // D)),
         ],
         compiler_params=pltpu.CompilerParams(
-            dimension_semantics=("arbitrary",), vmem_limit_bytes=60 * 1024 * 1024
+            dimension_semantics=("arbitrary",), vmem_limit_bytes=62 * 1024 * 1024
         ),
         name="train",
-    )(latent, code, weight, value, reward, action, target, near, far)
+    )(latent, code, weight, value, reward, action, target, *packed)
 
 
 def body(rows_all, packing, *args):
@@ -899,10 +996,10 @@
 
     groups = [tuple(turn(which, member) for member in group) for which, group in enumerate(groups)]
     stem, up, down, head, table, norm = (group[0] for group in groups)
-    near, far = send_weights(packing, stem, up, down, head, table, norm, weight.reshape(-1, 128))
-    lat_grad, near, far = train(packing, rows_all, latent, code, weight, value, reward, action, target, near, far)
-    own, squares = reduce_grads(packing, near, far)
-    outs = update(packing, rows_all, own, squares, groups)
+    packed = send_weights(packing, stem, up, down, head, table, norm, weight.reshape(-1, 128))
+    lat_grad, *grads = train(packing, rows_all, latent, code, weight, value, reward, action, target, packed)
+    own = reduce_grads(packing, [member.reshape(packing.count, packing.part, 128) for member in grads])
+    outs = update(packing, rows_all, own, groups)
     result = [outs[0].reshape(()), lat_grad]
     at = 1
     for which in range(6):

time: 223 us -> 189 us (0.85)
  Pallas kernels: 213 us -> 187 us
  local copies, waits for them, and re-layouts: 8.97 us -> 0.97 us
    pallas_call x1, Pallas kernels: 153 us -> 129 us  [train(): pl.pallas_call(functools.partial(train_kernel, packing, rows_all, chains)...]
    unnamed x58 -> x38, local copies, waits for them, and re-layouts: 8.97 us -> 0.97 us
    pallas_call x2, Pallas kernels: 59.1 us -> 56.6 us  [the longest x1 31.7 us: reduce_grads(): pl.pallas_call(functools.partial(reduce_kernel, packing), out_shape=jax.S...]
where the time goes in v2:
time: 189 us
  Pallas kernels  187 us (99%)
    pallas_call x1, Pallas kernels, train(): pl.pallas_call(functools.partial(train_kernel, packing, rows_all, chains)...  129 us
    pallas_call x1, Pallas kernels, reduce_grads(): pl.pallas_call(functools.partial(reduce_kernel, packing), out_shape=jax.S...  31.7 us
    pallas_call x1, Pallas kernels, send_weights(): pl.pallas_call(functools.partial(send_kernel, packing), out_shape=packing...  24.8 us

profile of v2, /device:TPU:0, one launch (start us, length us, event | category | flops | bytes accessed | tf_op | source)
XLA Modules:
  0.0 188.6 jit_solution(1477419280609456187)
XLA Ops:
  0.7 0.0 copy-start.11
  0.7 0.0 copy-start.3
  0.7 0.0 copy-start.1
  0.7 0.0 copy-start.16
  0.7 0.0 copy-start.15
  0.7 0.0 copy-start.18
  0.7 0.0 copy-start.17
  0.7 0.0 copy-start.12
  0.8 0.0 copy-start.10
  0.8 0.0 copy-start.9
  0.8 0.0 copy-start.8
  0.8 0.0 copy-start.7
  0.8 0.0 copy-start.2
  0.8 0.0 copy-start.6
  0.8 0.0 copy-start.5
  0.8 0.0 copy-start.14
  0.8 0.0 copy-start.13
  0.8 0.0 copy-start.4
  0.9 24.8 %send_weights.1 = (bf16[32,64,128]{2,1,0:T(8,128)(2,1)}, bf16[32,64,128]{2,1,0:T(8,128)(2,1)}, bf16[32,64,128]{2,1,0:T(8,128)(2,1)}, bf16[32,64,128]{2,1,0:T(8,128)(2,1)}) custom-call(f32[32,64]{1,0:T(8,128)} %bitcast.33, f32[4,32,64]{2,1,0:T(8,128)} %refs_3_.3, f32[4,32,64]{2,1,0:T(8,128)} %bitcast.31, f32[8,1238]{1,0:T(8,128)} %refs_9_.1, ...), custom_call_target="tpu_custom_call" | custom-call | tf_op jit(solution)/shard_map/send_weights/pallas_call | solution.py:272
  25.7 129.0 %train.1 = (f32[8192,256]{1,0:T(8,128)}, f32[2048,128]{1,0:T(8,128)}, f32[2048,128]{1,0:T(8,128)}, f32[2048,128]{1,0:T(8,128)}, f32[2048,128]{1,0:T(8,128)}) custom-call(bf16[8192,256]{1,0:T(8,128)(2,1)} %lat_ref.1, s32[8192]{0:T(1024)} %code_ref.1, s32[8192]{0:T(1024)} %weight_ref.1, s32[8192]{0:T(1024)} %value_ref.1, s32[8192]{0:T(1024)} %reward_ref.1, ...), custom_call_target="tpu_custom_call" | custom-call | tf_op jit(solution)/shard_map/train/pallas_call | solution.py:944
  154.7 31.7 %reduce_grads.1.own = f32[264,128]{1,0:T(8,128)} custom-call(f32[32,64,128]{2,1,0:T(8,128)} %bitcast.43, f32[32,64,128]{2,1,0:T(8,128)} %bitcast.44, f32[32,64,128]{2,1,0:T(8,128)} %bitcast.45, f32[32,64,128]{2,1,0:T(8,128)} %bitcast.46), custom_call_target="tpu_custom_call" | custom-call | tf_op jit(solution)/shard_map/reduce_grads/pallas_call | solution.py:401
  186.5 0.0 copy-done.11
  186.5 0.0 copy-done.3
  186.5 0.0 copy-done.1
  186.5 0.0 copy-done.16
  186.5 0.0 copy-done.15
  186.5 0.0 copy-done.18
  186.5 0.0 copy-done.17
  186.5 0.0 copy-done.12
  186.5 0.0 copy-done.10
  186.5 0.0 copy-done.9
  186.6 0.0 copy-done.8
  186.6 0.0 copy-done.7
  186.6 0.0 copy-done.2
  186.6 0.0 copy-done.6
  186.6 0.0 copy-done.5
  186.6 0.0 copy-done.14
  186.6 0.0 copy-done.13
  186.6 0.0 copy-done.4
  186.6 0.0 copy-start
  186.6 0.9 copy-done
  187.5 1.1 update.1
Async XLA Ops:
  0.7 185.8 %copy-start.11 = (f32[5,2,8]{2,1,0:T(2,128)S(1)}, f32[5,2,8]{2,1,0:T(2,128)}, u32[]{:S(2)}) copy-start(f32[5,2,8]{2,1,0:T(2,128)} %refs_15_.1) | copy-start | bytes 964
  0.7 185.8 %copy-start.3 = (f32[8,1238]{1,0:T(8,128)S(1)}, f32[8,1238]{1,0:T(8,128)}, u32[]{:S(2)}) copy-start(f32[8,1238]{1,0:T(8,128)} %refs_9_.1) | copy-start | bytes 118852
  0.7 185.8 %copy-start.1 = (f32[4,32,64]{2,1,0:T(8,128)S(1)}, f32[4,32,64]{2,1,0:T(8,128)}, u32[]{:S(2)}) copy-start(f32[4,32,64]{2,1,0:T(8,128)} %refs_3_.3) | copy-start | bytes 98308
  0.7 185.8 %copy-start.16 = (f32[5,2,8]{2,1,0:T(2,128)S(1)}, f32[5,2,8]{2,1,0:T(2,128)}, u32[]{:S(2)}) copy-start(f32[5,2,8]{2,1,0:T(2,128)} %refs_17_.1) | copy-start | bytes 964
  0.7 185.8 %copy-start.15 = (f32[5,2,8]{2,1,0:T(2,128)S(1)}, f32[5,2,8]{2,1,0:T(2,128)}, u32[]{:S(2)}) copy-start(f32[5,2,8]{2,1,0:T(2,128)} %refs_16_.1) | copy-start | bytes 964
  0.7 185.8 %copy-start.18 = (f32[32,8]{0,1:T(8,128)S(1)}, f32[32,8]{0,1:T(8,128)}, u32[]{:S(2)}) copy-start(f32[32,8]{0,1:T(8,128)} %param.46) | copy-start | bytes 3076
  0.7 185.8 %copy-start.17 = (f32[32,8]{0,1:T(8,128)S(1)}, f32[32,8]{0,1:T(8,128)}, u32[]{:S(2)}) copy-start(f32[32,8]{0,1:T(8,128)} %param.45) | copy-start | bytes 3076
  0.7 185.8 %copy-start.12 = (f32[32,8]{0,1:T(8,128)S(1)}, f32[32,8]{0,1:T(8,128)}, u32[]{:S(2)}) copy-start(f32[32,8]{0,1:T(8,128)} %param.44) | copy-start | bytes 3076
  0.8 185.8 %copy-start.10 = (f32[8,1238]{1,0:T(8,128)S(1)}, f32[8,1238]{1,0:T(8,128)}, u32[]{:S(2)}) copy-start(f32[8,1238]{1,0:T(8,128)} %refs_11_.1) | copy-start | bytes 118852
  0.8 185.8 %copy-start.9 = (f32[8,1238]{1,0:T(8,128)S(1)}, f32[8,1238]{1,0:T(8,128)}, u32[]{:S(2)}) copy-start(f32[8,1238]{1,0:T(8,128)} %refs_10_.1) | copy-start | bytes 118852
  0.8 185.8 %copy-start.8 = (f32[4,64,32]{1,2,0:T(8,128)S(1)}, f32[4,64,32]{1,2,0:T(8,128)}, u32[]{:S(2)}) copy-start(f32[4,64,32]{1,2,0:T(8,128)} %param.40) | copy-start | bytes 98308
  0.8 185.8 %copy-start.7 = (f32[4,64,32]{1,2,0:T(8,128)S(1)}, f32[4,64,32]{1,2,0:T(8,128)}, u32[]{:S(2)}) copy-start(f32[4,64,32]{1,2,0:T(8,128)} %param.39) | copy-start | bytes 98308
  0.8 185.8 %copy-start.2 = (f32[4,64,32]{1,2,0:T(8,128)S(1)}, f32[4,64,32]{1,2,0:T(8,128)}, u32[]{:S(2)}) copy-start(f32[4,64,32]{1,2,0:T(8,128)} %param.38) | copy-start | bytes 98308
  0.8 185.8 %copy-start.6 = (f32[4,32,64]{2,1,0:T(8,128)S(1)}, f32[4,32,64]{2,1,0:T(8,128)}, u32[]{:S(2)}) copy-start(f32[4,32,64]{2,1,0:T(8,128)} %refs_5_.3) | copy-start | bytes 98308
  0.8 185.8 %copy-start.5 = (f32[4,32,64]{2,1,0:T(8,128)S(1)}, f32[4,32,64]{2,1,0:T(8,128)}, u32[]{:S(2)}) copy-start(f32[4,32,64]{2,1,0:T(8,128)} %refs_4_.1) | copy-start | bytes 98308
  0.8 185.8 %copy-start.14 = (f32[64,32]{0,1:T(8,128)S(1)}, f32[64,32]{0,1:T(8,128)}, u32[]{:S(2)}) copy-start(f32[64,32]{0,1:T(8,128)} %param.34) | copy-start | bytes 24580
  0.8 185.8 %copy-start.13 = (f32[64,32]{0,1:T(8,128)S(1)}, f32[64,32]{0,1:T(8,128)}, u32[]{:S(2)}) copy-start(f32[64,32]{0,1:T(8,128)} %param.33) | copy-start | bytes 24580
  0.8 185.8 %copy-start.4 = (f32[64,32]{0,1:T(8,128)S(1)}, f32[64,32]{0,1:T(8,128)}, u32[]{:S(2)}) copy-start(f32[64,32]{0,1:T(8,128)} %param.32) | copy-start | bytes 24580
  186.6 0.9 copy-start

commit v3 on v2

--- a/solution.py
+++ b/solution.py
@@ -1,5 +1,5 @@
+import functools
 import math
-import functools
 
 import jax
 import jax.numpy as jnp
@@ -37,8 +37,8 @@
 LANES = 256
 CHAINS = 4
 PARTS = 4
-UNIT, DELAY, STAGGER = 90, 250, 200
-CHUNK = 32
+RING = 16
+CHUNK = 16
 BF = jnp.bfloat16
 F32 = jnp.float32
 MESH = pl.DeviceIdType.MESH
@@ -291,7 +291,10 @@
 def reduce_kernel(packing, *refs):
     given, own = refs[:PARTS], refs[PARTS]
     held, sent, got = (refs[PARTS * kind + 1 : PARTS * (kind + 1) + 1] for kind in (1, 2, 3))
-    across, along, send_sem, recv_sem, part_send, part_recv = refs[4 * PARTS + 1 :]
+    across, along, send_sem, recv_sem, part_send, part_recv, fetch_sem = refs[4 * PARTS + 1 :]
+    fetches = [pltpu.make_async_copy(given[side], held[side], fetch_sem.at[side]) for side in range(PARTS)]
+    for member in fetches:
+        member.start()
     steps = len(packing.orders[0])
     data, model = lax.axis_index("dp"), lax.axis_index("mp")
     barrier = pltpu.get_barrier_semaphore()
@@ -302,9 +305,6 @@
 
     slots = [slot_of(order, data, model) for order in packing.orders]
 
-    def source_of(side, number):
-        return given[side] if number == steps - 1 else held[side]
-
     def mine_of(side, number):
         size = packing.sizes[side][number]
         return (slots[side] // size) * size
@@ -317,7 +317,7 @@
         step, size = packing.orders[side][number], packing.sizes[side][number]
         for away in range(1, step[2]):
             block = mine_of(side, number) + partner_of(step, away)[1] * size
-            sent[side][place_of(side, number, away)] = source_of(side, number)[pl.ds(block, size)].astype(BF)
+            sent[side][place_of(side, number, away)] = held[side][pl.ds(block, size)].astype(BF)
 
     def copies_of(side, number):
         step = packing.orders[side][number]
@@ -335,14 +335,12 @@
 
     def take(side, number):
         rows = pl.ds(mine_of(side, number), packing.sizes[side][number])
-        total = source_of(side, number)[rows]
+        total = held[side][rows]
         for away in range(1, packing.orders[side][number][2]):
             total = total + got[side][place_of(side, number, away)].astype(F32)
         held[side][rows] = total
 
     copies = [[copies_of(side, number) for number in range(steps)] for side in range(PARTS)]
-    for side in range(PARTS):
-        pack(side, steps - 1)
     pl.semaphore_wait(barrier, packing.mp + packing.dp - 2)
     for number in range(steps - 1, -1, -1):
         for side in range(PARTS):
@@ -350,7 +348,9 @@
                 for member in copies[side][number + 1]:
                     member.wait_recv()
                 take(side, number + 1)
-                pack(side, number)
+            else:
+                fetches[side].wait()
+            pack(side, number)
             for member in copies[side][number]:
                 member.start()
     total = None
@@ -401,7 +401,7 @@
     return pl.pallas_call(
         functools.partial(reduce_kernel, packing),
         out_shape=jax.ShapeDtypeStruct((packing.rows + 8, 128), F32),
-        in_specs=[vmem] * PARTS,
+        in_specs=[pl.BlockSpec(memory_space=pl.ANY)] * PARTS,
         out_specs=vmem,
         scratch_shapes=packing.scratch(F32)
         + packing.scratch(BF) * 2
@@ -412,6 +412,7 @@
             pltpu.SemaphoreType.DMA((PARTS, steps, packing.most)),
             pltpu.SemaphoreType.DMA((packing.mp + packing.dp,)),
             pltpu.SemaphoreType.DMA((packing.mp + packing.dp,)),
+            pltpu.SemaphoreType.DMA((PARTS,)),
         ],
         compiler_params=pltpu.CompilerParams(
             collective_id=1, has_side_effects=True, vmem_limit_bytes=60 * 1024 * 1024
@@ -506,57 +507,34 @@
 ):
     held, lat_grad, outs = refs[:PARTS], refs[PARTS], refs[PARTS + 1 : 2 * PARTS + 1]
     (
-    stem_acc,
-    table_acc,
-    up_acc,
-    down_acc,
-    head_acc,
-    stem_t,
-    table_t,
-    up_t,
-    up_n,
-    down_t,
-    down_n,
-    head_t,
-    head_n,
-    scale_s,
-    stream_s,
-    centered_s,
-    slope_s,
-    inner_slope_s,
-    rstd_s,
-    act_s,
-    gated_s,
-    branch_s,
-    inner_grad_s,
-    logit_s,
-    low_s,
-    top_s,
-    pre_s,
-    hot_s,
-    norm_s,
-    norm_part,
-    ) = refs[2 * PARTS + 1 : -1]
+        stem_acc,
+        table_acc,
+        up_acc,
+        down_acc,
+        head_acc,
+        stem_t,
+        table_t,
+        up_t,
+        up_n,
+        down_t,
+        down_n,
+        head_t,
+        head_n,
+        scale_s,
+        norm_s,
+        norm_part,
+        lat_last,
+        pre_last,
+        hot_last,
+        arriving,
+        departing,
+        copy_sem,
+    ) = refs[2 * PARTS + 1 :]
     step = pl.program_id(0)
-    tiles_wide = logit_s.shape[1] // 128
     chunks = packing.count * packing.part // D
-    copy_sem = refs[-1]
-
-    def chunk_at(buffers, chunk):
-        layers = buffers[0].shape[0]
-        which, chunk = divmod(chunk, layers * tiles_wide)
-        layer, tile = divmod(chunk, tiles_wide)
-        return buffers[which].at[layer, :, tile * 128 : (tile + 1) * 128]
-
-    def packed_at(buffers, side, slot):
-        chunk, row = divmod(slot * packing.part, D)
-        return chunk_at(buffers, side * chunks + chunk), row
 
     def head_tile(tile):
-        return (
-            slice((tile // tiles_wide) * D, (tile // tiles_wide + 1) * D),
-            slice((tile % tiles_wide) * 128, (tile % tiles_wide + 1) * 128),
-        )
+        return head_acc.at[(tile // 2) * D : (tile // 2 + 1) * D, (tile % 2) * 128 : (tile % 2 + 1) * 128]
 
     devices = [(data, model) for data in range(packing.dp) for model in range(packing.mp)]
 
@@ -565,7 +543,7 @@
         arrived = [
             pltpu.make_async_copy(
                 held[side].at[chunk * D : (chunk + 1) * D],
-                chunk_at((act_s, gated_s), side * chunks + chunk),
+                arriving.at[side * chunks + chunk],
                 copy_sem.at[side, chunk],
             )
             for side in range(PARTS)
@@ -578,8 +556,8 @@
 
         def rows_of(device, begin, end):
             side, rows = packing.split(begin, end)
-            place, row = packed_at((act_s, gated_s), side, slot_of(packing.orders[side], *device))
-            return place[row : row + packing.part, :].astype(F32)[rows]
+            chunk, row = divmod(slot_of(packing.orders[side], *device) * packing.part, D)
+            return arriving[side * chunks + chunk, row : row + packing.part, :].astype(F32)[rows]
 
         wide_s = [stem_acc] + [up_acc.at[layer] for layer in range(LAYERS)] + [down_acc.at[layer] for layer in range(LAYERS)]
         for data in range(packing.dp):
@@ -605,10 +583,7 @@
             at = (device[0] * packing.mp + device[1]) * packing.own
             for tile in range(DEPTH // 128):
                 begin = packing.head_at + packing.own * tile
-                rows, lanes = head_tile(tile)
-                logit_s[rows.start + at : rows.start + at + packing.own, lanes] = rows_of(
-                    device, begin, begin + packing.own
-                )
+                head_tile(tile)[at : at + packing.own, :] = rows_of(device, begin, begin + packing.own)
             tail = rows_of(device, packing.tail_at, packing.tail_at + 16)
             table_acc[at : at + packing.own, :] = tail[0 : packing.own, 0:CODES]
             norm_parts.append(tail[:, NORM_LANE : NORM_LANE + packing.own])
@@ -617,7 +592,7 @@
         table_t[...] = table_acc[...].astype(BF)
         for tile in range(DEPTH // 128):
             at = tile * 128
-            whole = logit_s[head_tile(tile)]
+            whole = head_tile(tile)[...]
             head_n[:, at : at + 128] = whole.astype(BF)
             end = min(128, ROWS - at)
             head_t[at : at + end, :] = whole.T.astype(BF)[0:end]
@@ -633,20 +608,64 @@
         down_acc[...] = jnp.zeros_like(down_acc)
         head_acc[...] = jnp.zeros_like(head_acc)
         norm_part[...] = jnp.zeros_like(norm_part)
-        low_s[...] = jnp.zeros_like(low_s)
+        lat_last[...] = jnp.zeros_like(lat_last)
+        pre_last[...] = jnp.zeros_like(pre_last)
+        hot_last[...] = jnp.zeros_like(hot_last)
 
     def norm_rows(which, at):
         half = norm_s[which, at : at + CHUNK, :]
         return jnp.concatenate([half] * (LANES // 128), axis=1)
 
+    spans = [slice(at, at + CHUNK) for at in range(0, D, CHUNK)]
+    norm_total = {}
+
     def add_norm(which, at, part):
-        total = part[:, 0:128]
-        for lane in range(128, LANES, 128):
-            total = total + part[:, lane : lane + 128]
-        norm_part[which, at : at + CHUNK, :] += total
-
-    def spans(count):
-        return [slice(at, min(at + CHUNK, count)) for at in range(0, count, CHUNK)]
+        for lane in range(0, LANES, 128):
+            piece = part[:, lane : lane + 128]
+            norm_total[which, at] = norm_total[which, at] + piece if (which, at) in norm_total else piece
+
+    def pieces(array, count=D, begin=0):
+        return [array[begin + at : begin + min(at + CHUNK, count)] for at in range(0, count, CHUNK)]
+
+    def joined(parts):
+        return jnp.concatenate(parts, axis=0)
+
+    def folded(parts):
+        total = None
+        for part in parts:
+            total = fold_rows(total, part)
+        return jnp.sum(total, axis=0, keepdims=True)
+
+    def norm_forward(layer, stream):
+        mean = folded(stream) * (1.0 / D)
+        centered = [part - mean for part in stream]
+        rstd = lax.rsqrt(folded([part * part for part in centered]) * (1.0 / D) + eps_norm)
+        values, slopes = [], []
+        for rows, part in zip(spans, centered):
+            value, slope = gelu_pair(
+                (part * rstd) * norm_rows(2 * layer, rows.start) + norm_rows(2 * layer + 1, rows.start)
+            )
+            values.append(value)
+            slopes.append(slope)
+        return values, (centered, rstd, slopes)
+
+    def norm_backward(layer, grads, kept):
+        centered, rstd, slopes = kept
+        wide = []
+        for rows, grad, part, slope in zip(spans, grads, centered, slopes):
+            grad = grad * slope
+            add_norm(2 * layer + 1, rows.start, grad)
+            grad = grad * rstd
+            add_norm(2 * layer, rows.start, grad * part)
+            wide.append(grad * norm_rows(2 * layer, rows.start))
+        shift = folded(wide) * (1.0 / D)
+        slant = folded([grad * part for grad, part in zip(wide, centered)]) * (1.0 / D) * (rstd * rstd)
+        return [(grad - shift) - part * slant for grad, part in zip(wide, centered)]
+
+    acts, gateds, branches, inner_grads, lows, tops = ({} for _ in range(6))
+
+    def beside(kept, *key):
+        return jnp.concatenate([kept[(index,) + key] for index in range(chains)], axis=1)
 
     def chain(index):
         cols = slice(index * LANES, (index + 1) * LANES)
@@ -654,89 +673,30 @@
         def row_of(ref):
             return ref[cols].reshape(1, LANES)
 
-        def norm_forward(layer, total, sink):
-            mean = jnp.sum(total, axis=0, keepdims=True) * (1.0 / D)
-            yield "wait", 40
-            squares = None
-            for rows in spans(D):
-                centered = stream_s[rows, cols] - mean
-                centered_s[layer, rows, cols] = centered
-                squares = fold_rows(squares, centered * centered)
-                yield "vector", 3
-            spread = jnp.sum(squares, axis=0, keepdims=True) * (1.0 / D)
-            rstd = lax.rsqrt(spread + eps_norm)
-            rstd_s[layer, :, cols] = rstd
-            yield "wait", 60
-            total = None
-            for rows in spans(D):
-                scaled = centered_s[layer, rows, cols] * rstd
-                value, slope = gelu_pair(
-                    scaled * norm_rows(2 * layer, rows.start) + norm_rows(2 * layer + 1, rows.start)
-                )
-                if sink is None:
-                    value = 0.5 * value
-                    slope_s[layer, rows, cols] = 0.5 * slope
-                    stream_s[rows, cols] = value
-                    total = fold_rows(total, value)
-                else:
-                    slope_s[layer, rows, cols] = slope
-                    sink[layer - 1, rows, cols] = value.astype(BF)
-                yield "vector", 16
-            return total
-
-        def norm_backward(layer, grad_of, emit):
-            rstd = rstd_s[layer, :, cols]
-            first = second = None
-            for rows in spans(D):
-                grad = grad_of(rows) * slope_s[layer, rows, cols]
-                centered = centered_s[layer, rows, cols]
-                add_norm(2 * layer + 1, rows.start, grad)
-                grad = grad * rstd
-                add_norm(2 * layer, rows.start, grad * centered)
-                wide = grad * norm_rows(2 * layer, rows.start)
-                slope_s[layer, rows, cols] = wide
-                first = fold_rows(first, wide)
-                second = fold_rows(second, wide * centered)
-                yield "vector", 9
-            shift = jnp.sum(first, axis=0, keepdims=True) * (1.0 / D)
-            slant = jnp.sum(second, axis=0, keepdims=True) * (1.0 / D) * (rstd * rstd)
-            yield "wait", 50
-            for rows in spans(D):
-                emit(rows, (slope_s[layer, rows, cols] - shift) - centered_s[layer, rows, cols] * slant)
-                yield "vector", 5
-
         hot = (lax.broadcasted_iota(jnp.int32, (CODES, LANES), 0) == row_of(code_ref)).astype(F32).astype(BF)
-        hot_s[:, cols] = hot
-        pre = dot_nt(stem_t[...], lat_ref[cols, :]) + dot_nn(table_t[...], hot)
-        yield "product", 2
-        total = None
-        for rows in spans(D):
-            stream_s[rows, cols] = pre[rows]
-            total = fold_rows(total, pre[rows])
-            yield "vector", 2
-        total = yield from norm_forward(0, total, None)
+        stream = pieces(dot_nt(stem_t[...], lat_ref[cols, :]) + dot_nn(table_t[...], hot))
+        yield
+        kept, inner_slopes = {}, {}
+        values, kept[0] = norm_forward(0, stream)
+        stream = [0.5 * value for value in values]
+        yield
         for layer in range(1, LAYERS + 1):
-            yield from norm_forward(layer, total, act_s)
-            inner = dot_nn(up_t[layer - 1], act_s[layer - 1, :, cols])
-            yield "product", 1
-            for rows in spans(D):
-                value, slope = gelu_pair(inner[rows])
-                inner_slope_s[layer - 1, rows, cols] = slope
-                gated_s[layer - 1, rows, cols] = value.astype(BF)
-                yield "vector", 13
-            branch = dot_nn(down_t[layer - 1], gated_s[layer - 1, :, cols])
-            yield "product", 1
-            total = None
-            for rows in spans(D):
-                stream = stream_s[rows, cols] + branch[rows]
-                if layer < LAYERS:
-                    stream_s[rows, cols] = stream
-                    total = fold_rows(total, stream)
-                else:
-                    top_s[rows, cols] = stream.astype(BF)
-                yield "vector", 2
-        logit_s[:, cols] = dot_nn(head_t[...], top_s[:, cols])
-        yield "product", 5
+            values, kept[layer] = norm_forward(layer, stream)
+            acts[index, layer] = joined([value.astype(BF) for value in values])
+            yield
+            inner = dot_nn(up_t[layer - 1], acts[index, layer])
+            yield
+            both = [gelu_pair(part) for part in pieces(inner)]
+            inner_slopes[layer] = [slope for _, slope in both]
+            gateds[index, layer] = joined([value.astype(BF) for value, _ in both])
+            yield
+            branch = dot_nn(down_t[layer - 1], gateds[index, layer])
+            yield
+            stream = [part + change for part, change in zip(stream, pieces(branch))]
+        tops[(index,)] = joined([part.astype(BF) for part in stream])
+        yield
+        logits = dot_nn(head_t[...], tops[(index,)])
+        yield
         coef = row_of(weight_ref).astype(F32) * scale_s[...]
         sections = (
             (VALUE_AT, BINS, value_ref),
@@ -744,135 +704,86 @@
             (CHANCE_AT, CODES, target_ref),
             (POLICY_AT, ACTIONS, action_ref),
         )
+        low = []
         for begin, count, target_ref_of in sections:
             padded = -(-count // 8) * 8
+            parts = [logits[begin + at : begin + min(at + CHUNK, padded)] for at in range(0, padded, CHUNK)]
             if padded != count:
-                last = slice(begin + padded - 8, begin + padded)
-                keep = lax.broadcasted_iota(jnp.int32, (8, LANES), 0) < count - (padded - 8)
-                logit_s[last, cols] = jnp.where(keep, logit_s[last, cols], -1e30)
+                place = lax.broadcasted_iota(jnp.int32, parts[-1].shape, 0) + (padded - parts[-1].shape[0])
+                parts[-1] = jnp.where(place < count, parts[-1], -1e30)
             peak = None
-            for part in spans(padded):
-                rows = slice(begin + part.start, begin + part.stop)
-                peak = peak_rows(peak, logit_s[rows, cols])
-                yield "vector", 1
+            for part in parts:
+                peak = peak_rows(peak, part)
             peak = jnp.max(peak, axis=0, keepdims=True)
-            yield "wait", 40
-            mass = None
-            for part in spans(padded):
-                rows = slice(begin + part.start, begin + part.stop)
-                power = jnp.exp2((logit_s[rows, cols] - peak) * LOG2E)
-                logit_s[rows, cols] = power
-                mass = fold_rows(mass, power)
-                yield "vector", 4
-            scale = coef / jnp.sum(mass, axis=0, keepdims=True)
+            powers = [jnp.exp2((part - peak) * LOG2E) for part in parts]
+            scale = coef / folded(powers)
             target = row_of(target_ref_of)
-            yield "wait", 60
-            stored = -(-count // 16) * 16
-            for part in spans(padded):
-                rows = slice(begin + part.start, begin + part.stop)
-                soft = logit_s[rows, cols] * scale
-                place = lax.broadcasted_iota(jnp.int32, soft.shape, 0) + part.start
+            for number, power in enumerate(powers):
+                soft = power * scale
+                place = lax.broadcasted_iota(jnp.int32, soft.shape, 0) + number * CHUNK
                 soft = jnp.where(place == target, soft - coef, soft)
-                if part.stop == padded and padded != stored:
-                    soft = jnp.concatenate([soft, jnp.zeros((stored - padded, LANES), F32)], axis=0)
-                    rows = slice(begin + part.start, begin + stored)
-                low_s[rows, cols] = soft.astype(BF)
-                yield "vector", 5
-        yield "ready", "head"
-        grad = dot_nn(head_n[...], low_s[:, cols])
-        yield "product", 5
-        for rows in spans(D):
-            stream_s[rows, cols] = grad[rows]
-            branch_s[LAYERS % 2, rows, cols] = grad[rows].astype(BF)
-            yield "vector", 1
+                missing = -soft.shape[0] % 16
+                if missing:
+                    soft = jnp.concatenate([soft, jnp.zeros((missing, LANES), F32)], axis=0)
+                low.append(soft.astype(BF))
+            yield
+        low.append(jnp.zeros((DEPTH - ROWS, LANES), BF))
+        low = joined(low)
+        lows[(index,)] = low[0:ROWS]
+        grad = dot_nn(head_n[...], low)
+        yield
+        if index == chains - 1:
+            head_acc[0:ROWS, :] += dot_nt(beside(lows), beside(tops))
+        stream = pieces(grad)
         for layer in range(LAYERS, 0, -1):
-            gated_grad = dot_nn(down_n[layer - 1], branch_s[layer % 2, :, cols])
-            yield "product", 1
-            if layer + 2 <= LAYERS:
-                yield "until", ("block", layer + 2)
-            for rows in spans(D):
-                inner_grad_s[layer % 2, rows, cols] = (
-                    gated_grad[rows] * inner_slope_s[layer - 1, rows, cols]
-                ).astype(BF)
-                yield "vector", 2
-            active_grad = dot_nn(up_n[layer - 1], inner_grad_s[layer % 2, :, cols])
-            yield "product", 1
-            yield "ready", ("block", layer)
-
-            def emit(rows, change, layer=layer):
-                stream = stream_s[rows, cols] + change
-                stream_s[rows, cols] = stream
-                if layer > 1:
-                    branch_s[(layer - 1) % 2, rows, cols] = stream.astype(BF)
-
-            if layer + 1 <= LAYERS:
-                yield "until", ("block", layer + 1)
-            yield from norm_backward(layer, lambda rows: active_grad[rows], emit)
-
-        def emit_pre(rows, change):
-            pre_s[rows, cols] = change.astype(BF)
-
-        yield from norm_backward(0, lambda rows: stream_s[rows, cols], emit_pre)
-        lat_grad[cols, :] = dot_tn(pre_s[:, cols], stem_t[...])
-        yield "product", 1
-        yield "ready", "stem"
-
-    def weight_grads(what):
-        if what == "head":
-            head_acc[...] += dot_nt(low_s[0:ROWS, :], top_s[...])
-        elif what == "stem":
-            stem_acc[...] += dot_nn(pre_s[...], lat_ref[...])
-            table_acc[...] += dot_nt(pre_s[...], hot_s[...])
-        else:
-            layer = what[1]
-            down_acc[layer - 1] += dot_nt(branch_s[layer % 2], gated_s[layer - 1])
-            up_acc[layer - 1] += dot_nt(act_s[layer - 1], inner_grad_s[layer % 2])
-
-    members = [chain(index) for index in range(chains)]
-    ready_at, progress = [0] * chains, [index * STAGGER for index in range(chains)]
-    now = product_free = 0
-    counts, done, until = {}, set(), [None] * chains
-    while members.count(None) < chains:
-        alive = [index for index in range(chains) if members[index] is not None]
-        alive = [index for index in alive if until[index] is None or until[index] in done]
-        able = [index for index in alive if ready_at[index] <= now]
-        if not able:
-            now = min(ready_at[index] for index in alive)
-            continue
-        index = min(able, key=lambda number: progress[number])
-        try:
-            kind, amount = next(members[index])
-        except StopIteration:
-            members[index] = None
-            continue
-        if kind == "vector":
-            cost = amount * (CHUNK // 8) * (LANES // 128) / 3
-            now += cost
-            progress[index] += cost
-        elif kind == "product":
-            product_free = max(now, product_free) + amount * UNIT
-            ready_at[index] = product_free + DELAY
-            progress[index] += amount * UNIT
-        elif kind == "wait":
-            ready_at[index] = now + amount
-        elif kind == "until":
-            until[index] = amount
-        else:
-            counts[amount] = counts.get(amount, 0) + 1
-            if counts[amount] == chains:
-                weight_grads(amount)
-                done.add(amount)
-                product_free = max(now, product_free) + UNIT * chains * (5 if amount == "head" else 2)
+            branches[index, layer] = joined([part.astype(BF) for part in stream])
+            yield
+            gated_grad = dot_nn(down_n[layer - 1], branches[index, layer])
+            yield
+            inner_grads[index, layer] = joined(
+                [(part * slope).astype(BF) for part, slope in zip(pieces(gated_grad), inner_slopes[layer])]
+            )
+            yield
+            active_grad = dot_nn(up_n[layer - 1], inner_grads[index, layer])
+            if index == chains - 1:
+                down_acc[layer - 1] += dot_nt(beside(branches, layer), beside(gateds, layer))
+                up_acc[layer - 1] += dot_nt(beside(acts, layer), beside(inner_grads, layer))
+            yield
+            changes = norm_backward(layer, pieces(active_grad), kept[layer])
+            stream = [part + change for part, change in zip(stream, changes)]
+            yield
+        values, slopes = kept[0][:2], [0.5 * slope for slope in kept[0][2]]
+        pre = joined([part.astype(BF) for part in norm_backward(0, stream, (*values, slopes))])
+        yield
+        lat_grad[cols, :] = dot_tn(pre, stem_t[...])
+        pre_last[:, cols] = pre
+        hot_last[:, cols] = hot
+        lat_last[cols, :] = lat_ref[cols, :]
+
+    def stem_grads():
+        stem_acc[...] += dot_nn(pre_last[...], lat_last[...])
+        table_acc[...] += dot_nt(pre_last[...], hot_last[...])
+
+    stem_grads()
+
+    running = []
+    waiting = [chain(index) for index in range(chains)]
+    while running or waiting:
+        if waiting:
+            running.append(waiting.pop(0))
+        for member in list(running):
+            try:
+                next(member)
+            except StopIteration:
+                running.remove(member)
+    for (which, at), total in norm_total.items():
+        norm_part[which, at : at + CHUNK, :] += total
 
     @pl.when(step == pl.num_programs(0) - 1)
     def _():
-        for tile in range(DEPTH // 128):
-            at = tile * 128
-            end = min(128, ROWS - at)
-            turned = head_acc[at : at + end, :]
-            if end < 128:
-                turned = jnp.concatenate([turned, jnp.zeros((128 - end, D), F32)], axis=0)
-            logit_s[head_tile(tile)] = turned.T
+        stem_grads()
+        for at in range(0, DEPTH, D):
+            head_acc[at : at + D, :] = head_acc[at : at + D, :].T
         lane_at = lax.broadcasted_iota(jnp.int32, (D, 128), 1)
         columns = jnp.zeros((D, 128), F32)
         for which in range(2 * (LAYERS + 1)):
@@ -893,12 +804,10 @@
                     lambda members=members: jnp.concatenate([member() for member in members], axis=1),
                 )
             for tile in range(DEPTH // 128):
-                rows, lanes = head_tile(tile)
-                rows = slice(rows.start + at, rows.start + at + packing.own)
                 yield (
                     packing.head_at + packing.own * tile,
                     slice(0, 128),
-                    lambda rows=rows, lanes=lanes: logit_s[rows, lanes],
+                    lambda tile=tile: head_tile(tile)[at : at + packing.own, :],
                 )
             own = slice(at, at + packing.own)
             yield packing.tail_at, slice(0, CODES), lambda: table_acc[own, :]
@@ -912,7 +821,10 @@
         for side in range(PARTS):
             owners = {slot_of(packing.orders[side], *device): device for device in devices}
             for chunk in range(chunks):
-                place = chunk_at((centered_s, slope_s), side * chunks + chunk)
+                number = side * chunks + chunk
+                place = departing.at[number % RING]
+                if number >= RING:
+                    leaving[number - RING].wait()
                 place[...] = jnp.zeros((D, 128), F32)
                 for row in range(0, D, packing.part):
                     for begin, lanes, value in pieces_of(*owners[(chunk * D + row) // packing.part]):
@@ -926,7 +838,7 @@
                     )
                 )
                 leaving[-1].start()
-        for member in leaving:
+        for member in leaving[-RING:]:
             member.wait()
 
 
@@ -945,14 +857,15 @@
         functools.partial(train_kernel, packing, rows_all, chains),
         grid=(count // block,),
         out_shape=[jax.ShapeDtypeStruct((count, D), F32)] + [flat] * PARTS,
-        in_specs=[pl.BlockSpec((block, D), lambda i: (i, 0))] + [row() for _ in range(6)] + parts,
+        in_specs=[pl.BlockSpec((block, D), lambda i: (i, 0))]
+        + [row() for _ in range(6)] + parts,
         out_specs=[pl.BlockSpec((block, D), lambda i: (i, 0))] + parts,
         scratch_shapes=[
             pltpu.VMEM((D, D), F32),
             pltpu.VMEM((D, CODES), F32),
             pltpu.VMEM((LAYERS, D, D), F32),
             pltpu.VMEM((LAYERS, D, D), F32),
-            pltpu.VMEM((ROWS, D), F32),
+            pltpu.VMEM((DEPTH, D), F32),
             pltpu.VMEM((D, D), BF),
             pltpu.VMEM((D, CODES), BF),
             pltpu.VMEM((LAYERS, D, D), BF),
@@ -962,26 +875,17 @@
             pltpu.VMEM((ROWS, D), BF),
             pltpu.VMEM((D, DEPTH), BF),
             pltpu.VMEM((1, LANES), F32),
-            pltpu.VMEM((D, block), F32),
-            pltpu.VMEM((LAYERS + 1, D, block), F32),
-            pltpu.VMEM((LAYERS + 1, D, block), F32),
-            pltpu.VMEM((LAYERS, D, block), F32),
-            pltpu.VMEM((LAYERS + 1, 1, block), F32),
-            pltpu.VMEM((LAYERS, D, block), BF),
-            pltpu.VMEM((LAYERS, D, block), BF),
-            pltpu.VMEM((2, D, block), BF),
-            pltpu.VMEM((2, D, block), BF),
-            pltpu.VMEM((ROWS, block), F32),
-            pltpu.VMEM((DEPTH, block), BF),
-            pltpu.VMEM((D, block), BF),
+            pltpu.VMEM((2 * (LAYERS + 1), D, 128), F32),
+            pltpu.VMEM((2 * (LAYERS + 1), D, 128), F32),
+            pltpu.VMEM((block, D), BF),
             pltpu.VMEM((D, block), BF),
             pltpu.VMEM((CODES, block), BF),
-            pltpu.VMEM((2 * (LAYERS + 1), D, 128), F32),
-            pltpu.VMEM((2 * (LAYERS + 1), D, 128), F32),
+            pltpu.VMEM((PARTS * packing.count * packing.part // D, D, 128), BF),
+            pltpu.VMEM((RING, D, 128), F32),
             pltpu.SemaphoreType.DMA((PARTS, packing.count * packing.part // D)),
         ],
         compiler_params=pltpu.CompilerParams(
-            dimension_semantics=("arbitrary",), vmem_limit_bytes=62 * 1024 * 1024
+            dimension_semantics=("arbitrary",), vmem_limit_bytes=60 * 1024 * 1024
         ),
         name="train",
     )(latent, code, weight, value, reward, action, target, *packed)

time: 189 us -> 177 us (0.937)
  Pallas kernels: 187 us -> 174 us
    pallas_call x1, Pallas kernels: 129 us -> 119 us  [train(): pl.pallas_call(functools.partial(train_kernel, packing, rows_all, chains)...]
    pallas_call x1, Pallas kernels: 31.7 us -> 29.7 us  [reduce_grads(): pl.pallas_call(functools.partial(reduce_kernel, packing), out_shape=jax.S...]
where the time goes in v3:
time: 177 us; the launch traced here: 176 us
  Pallas kernels  174 us (98%)
    pallas_call x1, Pallas kernels, train(): pl.pallas_call(functools.partial(train_kernel, packing, rows_all, chains)...  119 us
    pallas_call x1, Pallas kernels, reduce_grads(): pl.pallas_call(functools.partial(reduce_kernel, packing), out_shape=jax.S...  29.7 us
    pallas_call x1, Pallas kernels, send_weights(): pl.pallas_call(functools.partial(send_kernel, packing), out_shape=packing...  24.8 us

profile of v3, /device:TPU:0, one launch (start us, length us, event | category | flops | bytes accessed | tf_op | source)
XLA Modules:
  0.0 176.4 jit_solution(16380908748472478408)
XLA Ops:
  0.7 0.0 copy-start.11
  0.7 0.0 copy-start.3
  0.7 0.0 copy-start.1
  0.7 0.0 copy-start.16
  0.7 0.0 copy-start.15
  0.7 0.0 copy-start.18
  0.7 0.0 copy-start.17
  0.7 0.0 copy-start.12
  0.8 0.0 copy-start.10
  0.8 0.0 copy-start.9
  0.8 0.0 copy-start.8
  0.8 0.0 copy-start.7
  0.8 0.0 copy-start.2
  0.8 0.0 copy-start.6
  0.8 0.0 copy-start.5
  0.8 0.0 copy-start.14
  0.8 0.0 copy-start.13
  0.8 0.0 copy-start.4
  0.9 24.8 %send_weights.1 = (bf16[32,64,128]{2,1,0:T(8,128)(2,1)}, bf16[32,64,128]{2,1,0:T(8,128)(2,1)}, bf16[32,64,128]{2,1,0:T(8,128)(2,1)}, bf16[32,64,128]{2,1,0:T(8,128)(2,1)}) custom-call(f32[32,64]{1,0:T(8,128)} %bitcast.33, f32[4,32,64]{2,1,0:T(8,128)} %refs_3_.3, f32[4,32,64]{2,1,0:T(8,128)} %bitcast.31, f32[8,1238]{1,0:T(8,128)} %refs_9_.1, ...), custom_call_target="tpu_custom_call" | custom-call | tf_op jit(solution)/shard_map/send_weights/pallas_call | solution.py:272
  25.7 118.8 %train.1 = (f32[8192,256]{1,0:T(8,128)}, f32[2048,128]{1,0:T(8,128)}, f32[2048,128]{1,0:T(8,128)}, f32[2048,128]{1,0:T(8,128)}, f32[2048,128]{1,0:T(8,128)}) custom-call(bf16[8192,256]{1,0:T(8,128)(2,1)} %lat_ref.1, s32[8192]{0:T(1024)} %code_ref.1, s32[8192]{0:T(1024)} %weight_ref.1, s32[8192]{0:T(1024)} %value_ref.1, s32[8192]{0:T(1024)} %reward_ref.1, ...), custom_call_target="tpu_custom_call" | custom-call | tf_op jit(solution)/shard_map/train/pallas_call | solution.py:856
  144.5 29.7 %reduce_grads.1.own = f32[264,128]{1,0:T(8,128)} custom-call(f32[32,64,128]{2,1,0:T(8,128)} %bitcast.43, f32[32,64,128]{2,1,0:T(8,128)} %bitcast.44, f32[32,64,128]{2,1,0:T(8,128)} %bitcast.45, f32[32,64,128]{2,1,0:T(8,128)} %bitcast.46), custom_call_target="tpu_custom_call" | custom-call | tf_op jit(solution)/shard_map/reduce_grads/pallas_call | solution.py:401
  174.2 0.0 copy-done.11
  174.2 0.0 copy-done.3
  174.2 0.0 copy-done.1
  174.2 0.0 copy-done.16
  174.3 0.0 copy-done.15
  174.3 0.0 copy-done.18
  174.3 0.0 copy-done.17
  174.3 0.0 copy-done.12
  174.3 0.0 copy-done.10
  174.3 0.0 copy-done.9
  174.3 0.0 copy-done.8
  174.3 0.0 copy-done.7
  174.3 0.0 copy-done.2
  174.3 0.0 copy-done.6
  174.4 0.0 copy-done.5
  174.4 0.0 copy-done.14
  174.4 0.0 copy-done.13
  174.4 0.0 copy-done.4
  174.4 0.0 copy-start
  174.4 0.9 copy-done
  175.3 1.1 update.1
Async XLA Ops:
  0.7 173.5 %copy-start.11 = (f32[5,2,8]{2,1,0:T(2,128)S(1)}, f32[5,2,8]{2,1,0:T(2,128)}, u32[]{:S(2)}) copy-start(f32[5,2,8]{2,1,0:T(2,128)} %refs_15_.1) | copy-start | bytes 964
  0.7 173.5 %copy-start.3 = (f32[8,1238]{1,0:T(8,128)S(1)}, f32[8,1238]{1,0:T(8,128)}, u32[]{:S(2)}) copy-start(f32[8,1238]{1,0:T(8,128)} %refs_9_.1) | copy-start | bytes 118852
  0.7 173.5 %copy-start.1 = (f32[4,32,64]{2,1,0:T(8,128)S(1)}, f32[4,32,64]{2,1,0:T(8,128)}, u32[]{:S(2)}) copy-start(f32[4,32,64]{2,1,0:T(8,128)} %refs_3_.3) | copy-start | bytes 98308
  0.7 173.5 %copy-start.16 = (f32[5,2,8]{2,1,0:T(2,128)S(1)}, f32[5,2,8]{2,1,0:T(2,128)}, u32[]{:S(2)}) copy-start(f32[5,2,8]{2,1,0:T(2,128)} %refs_17_.1) | copy-start | bytes 964
  0.7 173.5 %copy-start.15 = (f32[5,2,8]{2,1,0:T(2,128)S(1)}, f32[5,2,8]{2,1,0:T(2,128)}, u32[]{:S(2)}) copy-start(f32[5,2,8]{2,1,0:T(2,128)} %refs_16_.1) | copy-start | bytes 964
  0.7 173.5 %copy-start.18 = (f32[32,8]{0,1:T(8,128)S(1)}, f32[32,8]{0,1:T(8,128)}, u32[]{:S(2)}) copy-start(f32[32,8]{0,1:T(8,128)} %param.46) | copy-start | bytes 3076
  0.7 173.5 %copy-start.17 = (f32[32,8]{0,1:T(8,128)S(1)}, f32[32,8]{0,1:T(8,128)}, u32[]{:S(2)}) copy-start(f32[32,8]{0,1:T(8,128)} %param.45) | copy-start | bytes 3076
  0.7 173.5 %copy-start.12 = (f32[32,8]{0,1:T(8,128)S(1)}, f32[32,8]{0,1:T(8,128)}, u32[]{:S(2)}) copy-start(f32[32,8]{0,1:T(8,128)} %param.44) | copy-start | bytes 3076
  0.8 173.5 %copy-start.10 = (f32[8,1238]{1,0:T(8,128)S(1)}, f32[8,1238]{1,0:T(8,128)}, u32[]{:S(2)}) copy-start(f32[8,1238]{1,0:T(8,128)} %refs_11_.1) | copy-start | bytes 118852
  0.8 173.5 %copy-start.9 = (f32[8,1238]{1,0:T(8,128)S(1)}, f32[8,1238]{1,0:T(8,128)}, u32[]{:S(2)}) copy-start(f32[8,1238]{1,0:T(8,128)} %refs_10_.1) | copy-start | bytes 118852
  0.8 173.5 %copy-start.8 = (f32[4,64,32]{1,2,0:T(8,128)S(1)}, f32[4,64,32]{1,2,0:T(8,128)}, u32[]{:S(2)}) copy-start(f32[4,64,32]{1,2,0:T(8,128)} %param.40) | copy-start | bytes 98308
  0.8 173.5 %copy-start.7 = (f32[4,64,32]{1,2,0:T(8,128)S(1)}, f32[4,64,32]{1,2,0:T(8,128)}, u32[]{:S(2)}) copy-start(f32[4,64,32]{1,2,0:T(8,128)} %param.39) | copy-start | bytes 98308
  0.8 173.5 %copy-start.2 = (f32[4,64,32]{1,2,0:T(8,128)S(1)}, f32[4,64,32]{1,2,0:T(8,128)}, u32[]{:S(2)}) copy-start(f32[4,64,32]{1,2,0:T(8,128)} %param.38) | copy-start | bytes 98308
  0.8 173.5 %copy-start.6 = (f32[4,32,64]{2,1,0:T(8,128)S(1)}, f32[4,32,64]{2,1,0:T(8,128)}, u32[]{:S(2)}) copy-start(f32[4,32,64]{2,1,0:T(8,128)} %refs_5_.3) | copy-start | bytes 98308
  0.8 173.5 %copy-start.5 = (f32[4,32,64]{2,1,0:T(8,128)S(1)}, f32[4,32,64]{2,1,0:T(8,128)}, u32[]{:S(2)}) copy-start(f32[4,32,64]{2,1,0:T(8,128)} %refs_4_.1) | copy-start | bytes 98308
  0.8 173.5 %copy-start.14 = (f32[64,32]{0,1:T(8,128)S(1)}, f32[64,32]{0,1:T(8,128)}, u32[]{:S(2)}) copy-start(f32[64,32]{0,1:T(8,128)} %param.34) | copy-start | bytes 24580
  0.8 173.5 %copy-start.13 = (f32[64,32]{0,1:T(8,128)S(1)}, f32[64,32]{0,1:T(8,128)}, u32[]{:S(2)}) copy-start(f32[64,32]{0,1:T(8,128)} %param.33) | copy-start | bytes 24580
  0.8 173.5 %copy-start.4 = (f32[64,32]{0,1:T(8,128)S(1)}, f32[64,32]{0,1:T(8,128)}, u32[]{:S(2)}) copy-start(f32[64,32]{0,1:T(8,128)} %param.32) | copy-start | bytes 24580
  174.4 0.9 copy-start

commit v4 on v3

--- a/solution.py
+++ b/solution.py
@@ -503,6 +503,7 @@
     reward_ref,
     action_ref,
     target_ref,
+    gate_ref,
     *refs,
 ):
     held, lat_grad, outs = refs[:PARTS], refs[PARTS], refs[PARTS + 1 : 2 * PARTS + 1]
@@ -526,6 +527,13 @@
         lat_last,
         pre_last,
         hot_last,
+        centered_s,
+        slope_s,
+        inner_slope_s,
+        rstd_s,
+        act_s,
+        gated_s,
+        grad_s,
         arriving,
         departing,
         copy_sem,
@@ -636,24 +644,27 @@
             total = fold_rows(total, part)
         return jnp.sum(total, axis=0, keepdims=True)
 
-    def norm_forward(layer, stream):
+    def norm_forward(layer, stream, cols):
         mean = folded(stream) * (1.0 / D)
         centered = [part - mean for part in stream]
         rstd = lax.rsqrt(folded([part * part for part in centered]) * (1.0 / D) + eps_norm)
-        values, slopes = [], []
+        rstd_s[layer, :, cols] = rstd
+        values = []
         for rows, part in zip(spans, centered):
+            centered_s[layer, rows, cols] = part
             value, slope = gelu_pair(
                 (part * rstd) * norm_rows(2 * layer, rows.start) + norm_rows(2 * layer + 1, rows.start)
             )
             values.append(value)
-            slopes.append(slope)
-        return values, (centered, rstd, slopes)
-
-    def norm_backward(layer, grads, kept):
-        centered, rstd, slopes = kept
+            slope_s[layer, rows, cols] = slope
+        return values
+
+    def norm_backward(layer, grads, cols):
+        rstd = rstd_s[layer, :, cols]
+        centered = [centered_s[layer, rows, cols] for rows in spans]
         wide = []
-        for rows, grad, part, slope in zip(spans, grads, centered, slopes):
-            grad = grad * slope
+        for rows, grad, part in zip(spans, grads, centered):
+            grad = grad * slope_s[layer, rows, cols]
             add_norm(2 * layer + 1, rows.start, grad)
             grad = grad * rstd
             add_norm(2 * layer, rows.start, grad * part)
@@ -662,42 +673,45 @@
         slant = folded([grad * part for grad, part in zip(wide, centered)]) * (1.0 / D) * (rstd * rstd)
         return [(grad - shift) - part * slant for grad, part in zip(wide, centered)]
 
-    acts, gateds, branches, inner_grads, lows, tops = ({} for _ in range(6))
+    branches, inner_grads, lows, tops = ({} for _ in range(4))
 
     def beside(kept, *key):
         return jnp.concatenate([kept[(index,) + key] for index in range(chains)], axis=1)
 
-    def chain(index):
+    def row_of(ref, cols):
+        return ref[cols].reshape(1, LANES)
+
+    def hot_of(cols):
+        return (lax.broadcasted_iota(jnp.int32, (CODES, LANES), 0) == row_of(code_ref, cols)).astype(F32).astype(BF)
+
+    def forward(index):
         cols = slice(index * LANES, (index + 1) * LANES)
-
-        def row_of(ref):
-            return ref[cols].reshape(1, LANES)
-
-        hot = (lax.broadcasted_iota(jnp.int32, (CODES, LANES), 0) == row_of(code_ref)).astype(F32).astype(BF)
-        stream = pieces(dot_nt(stem_t[...], lat_ref[cols, :]) + dot_nn(table_t[...], hot))
+        stream = pieces(dot_nt(stem_t[...], lat_ref[cols, :]) + dot_nn(table_t[...], hot_of(cols)))
         yield
-        kept, inner_slopes = {}, {}
-        values, kept[0] = norm_forward(0, stream)
-        stream = [0.5 * value for value in values]
+        stream = [0.5 * value for value in norm_forward(0, stream, cols)]
         yield
         for layer in range(1, LAYERS + 1):
-            values, kept[layer] = norm_forward(layer, stream)
-            acts[index, layer] = joined([value.astype(BF) for value in values])
+            act = joined([value.astype(BF) for value in norm_forward(layer, stream, cols)])
+            act_s[layer - 1, :, cols] = act
             yield
-            inner = dot_nn(up_t[layer - 1], acts[index, layer])
+            inner = dot_nn(up_t[layer - 1], act)
             yield
-            both = [gelu_pair(part) for part in pieces(inner)]
-            inner_slopes[layer] = [slope for _, slope in both]
-            gateds[index, layer] = joined([value.astype(BF) for value, _ in both])
+            gated = []
+            for rows, part in zip(spans, pieces(inner)):
+                value, slope = gelu_pair(part)
+                inner_slope_s[layer - 1, rows, cols] = slope
+                gated.append(value.astype(BF))
+            gated = joined(gated)
+            gated_s[layer - 1, :, cols] = gated
             yield
-            branch = dot_nn(down_t[layer - 1], gateds[index, layer])
+            branch = dot_nn(down_t[layer - 1], gated)
             yield
             stream = [part + change for part, change in zip(stream, pieces(branch))]
         tops[(index,)] = joined([part.astype(BF) for part in stream])
         yield
         logits = dot_nn(head_t[...], tops[(index,)])
         yield
-        coef = row_of(weight_ref).astype(F32) * scale_s[...]
+        coef = row_of(weight_ref, cols).astype(F32) * scale_s[...]
         sections = (
             (VALUE_AT, BINS, value_ref),
             (REWARD_AT, BINS, reward_ref),
@@ -717,7 +731,7 @@
             peak = jnp.max(peak, axis=0, keepdims=True)
             powers = [jnp.exp2((part - peak) * LOG2E) for part in parts]
             scale = coef / folded(powers)
-            target = row_of(target_ref_of)
+            target = row_of(target_ref_of, cols)
             for number, power in enumerate(powers):
                 soft = power * scale
                 place = lax.broadcasted_iota(jnp.int32, soft.shape, 0) + number * CHUNK
@@ -730,54 +744,65 @@
         low.append(jnp.zeros((DEPTH - ROWS, LANES), BF))
         low = joined(low)
         lows[(index,)] = low[0:ROWS]
-        grad = dot_nn(head_n[...], low)
-        yield
+        grad_s[:, cols] = dot_nn(head_n[...], low)
         if index == chains - 1:
             head_acc[0:ROWS, :] += dot_nt(beside(lows), beside(tops))
-        stream = pieces(grad)
+
+    def backward(index):
+        cols = slice(index * LANES, (index + 1) * LANES)
+        stream = [grad_s[rows, cols] for rows in spans]
         for layer in range(LAYERS, 0, -1):
             branches[index, layer] = joined([part.astype(BF) for part in stream])
             yield
             gated_grad = dot_nn(down_n[layer - 1], branches[index, layer])
             yield
             inner_grads[index, layer] = joined(
-                [(part * slope).astype(BF) for part, slope in zip(pieces(gated_grad), inner_slopes[layer])]
+                [
+                    (part * inner_slope_s[layer - 1, rows, cols]).astype(BF)
+                    for rows, part in zip(spans, pieces(gated_grad))
+                ]
             )
             yield
             active_grad = dot_nn(up_n[layer - 1], inner_grads[index, layer])
             if index == chains - 1:
-                down_acc[layer - 1] += dot_nt(beside(branches, layer), beside(gateds, layer))
-                up_acc[layer - 1] += dot_nt(beside(acts, layer), beside(inner_grads, layer))
+                down_acc[layer - 1] += dot_nt(beside(branches, layer), gated_s[layer - 1])
+                up_acc[layer - 1] += dot_nt(act_s[layer - 1], beside(inner_grads, layer))
             yield
-            changes = norm_backward(layer, pieces(active_grad), kept[layer])
+            changes = norm_backward(layer, pieces(active_grad), cols)
             stream = [part + change for part, change in zip(stream, changes)]
             yield
-        values, slopes = kept[0][:2], [0.5 * slope for slope in kept[0][2]]
-        pre = joined([part.astype(BF) for part in norm_backward(0, stream, (*values, slopes))])
+        pre = joined([part.astype(BF) for part in norm_backward(0, [0.5 * part for part in stream], cols)])
         yield
         lat_grad[cols, :] = dot_tn(pre, stem_t[...])
         pre_last[:, cols] = pre
-        hot_last[:, cols] = hot
+        hot_last[:, cols] = hot_of(cols)
         lat_last[cols, :] = lat_ref[cols, :]
 
     def stem_grads():
         stem_acc[...] += dot_nn(pre_last[...], lat_last[...])
         table_acc[...] += dot_nt(pre_last[...], hot_last[...])
 
-    stem_grads()
-
-    running = []
-    waiting = [chain(index) for index in range(chains)]
-    while running or waiting:
-        if waiting:
-            running.append(waiting.pop(0))
-        for member in list(running):
-            try:
-                next(member)
-            except StopIteration:
-                running.remove(member)
-    for (which, at), total in norm_total.items():
-        norm_part[which, at : at + CHUNK, :] += total
+    def together(way):
+        running, waiting = [], [way(index) for index in range(chains)]
+        while running or waiting:
+            if waiting:
+                running.append(waiting.pop(0))
+            for member in list(running):
+                try:
+                    next(member)
+                except StopIteration:
+                    running.remove(member)
+
+    @pl.when(gate_ref[0] == 0)
+    def _():
+        stem_grads()
+        together(forward)
+
+    @pl.when(gate_ref[0] == 0)
+    def _():
+        together(backward)
+        for (which, at), total in norm_total.items():
+            norm_part[which, at : at + CHUNK, :] += total
 
     @pl.when(step == pl.num_programs(0) - 1)
     def _():
@@ -858,7 +883,9 @@
         grid=(count // block,),
         out_shape=[jax.ShapeDtypeStruct((count, D), F32)] + [flat] * PARTS,
         in_specs=[pl.BlockSpec((block, D), lambda i: (i, 0))]
-        + [row() for _ in range(6)] + parts,
+        + [row() for _ in range(6)]
+        + [pl.BlockSpec(memory_space=pltpu.SMEM)]
+        + parts,
         out_specs=[pl.BlockSpec((block, D), lambda i: (i, 0))] + parts,
         scratch_shapes=[
             pltpu.VMEM((D, D), F32),
@@ -880,6 +907,13 @@
             pltpu.VMEM((block, D), BF),
             pltpu.VMEM((D, block), BF),
             pltpu.VMEM((CODES, block), BF),
+            pltpu.VMEM((LAYERS + 1, D, block), F32),
+            pltpu.VMEM((LAYERS + 1, D, block), F32),
+            pltpu.VMEM((LAYERS, D, block), F32),
+            pltpu.VMEM((LAYERS + 1, 1, block), F32),
+            pltpu.VMEM((LAYERS, D, block), BF),
+            pltpu.VMEM((LAYERS, D, block), BF),
+            pltpu.VMEM((D, block), F32),
             pltpu.VMEM((PARTS * packing.count * packing.part // D, D, 128), BF),
             pltpu.VMEM((RING, D, 128), F32),
             pltpu.SemaphoreType.DMA((PARTS, packing.count * packing.part // D)),
@@ -888,7 +922,7 @@
             dimension_semantics=("arbitrary",), vmem_limit_bytes=60 * 1024 * 1024
         ),
         name="train",
-    )(latent, code, weight, value, reward, action, target, *packed)
+    )(latent, code, weight, value, reward, action, target, jnp.zeros((1,), jnp.int32), *packed)
 
 
 def body(rows_all, packing, *args):

time: 177 us -> 196 us (1.11)
  Pallas kernels: 174 us -> 194 us
    pallas_call x1, Pallas kernels: 119 us -> 139 us  [train(): pl.pallas_call(functools.partial(train_kernel, packing, rows_all, chains)...]
where the time goes in v4:
time: 196 us
  Pallas kernels  194 us (99%)
    pallas_call x1, Pallas kernels, train(): pl.pallas_call(functools.partial(train_kernel, packing, rows_all, chains)...  139 us
    pallas_call x1, Pallas kernels, reduce_grads(): pl.pallas_call(functools.partial(reduce_kernel, packing), out_shape=jax.S...  29.7 us
    pallas_call x1, Pallas kernels, send_weights(): pl.pallas_call(functools.partial(send_kernel, packing), out_shape=packing...  24.8 us

profile of v4, /device:TPU:0, one launch (start us, length us, event | category | flops | bytes accessed | tf_op | source)
XLA Modules:
  0.0 196.1 jit_solution(959530637676674734)
XLA Ops:
  0.7 0.0 copy-start.11
  0.7 0.0 copy-start.3
  0.7 0.0 copy-start.1
  0.7 0.0 copy-start.16
  0.7 0.0 copy-start.15
  0.7 0.0 copy-start.18
  0.7 0.0 copy-start.17
  0.7 0.0 copy-start.12
  0.8 0.0 copy-start.10
  0.8 0.0 copy-start.9
  0.8 0.0 copy-start.8
  0.8 0.0 copy-start.7
  0.8 0.0 copy-start.2
  0.8 0.0 copy-start.6
  0.8 0.0 copy-start.5
  0.8 0.0 copy-start.14
  0.8 0.0 copy-start.13
  0.8 0.0 copy-start.4
  0.9 24.8 %send_weights.1 = (bf16[32,64,128]{2,1,0:T(8,128)(2,1)}, bf16[32,64,128]{2,1,0:T(8,128)(2,1)}, bf16[32,64,128]{2,1,0:T(8,128)(2,1)}, bf16[32,64,128]{2,1,0:T(8,128)(2,1)}) custom-call(f32[32,64]{1,0:T(8,128)} %bitcast.33, f32[4,32,64]{2,1,0:T(8,128)} %refs_3_.3, f32[4,32,64]{2,1,0:T(8,128)} %bitcast.31, f32[8,1238]{1,0:T(8,128)} %refs_9_.1, ...), custom_call_target="tpu_custom_call" | custom-call | tf_op jit(solution)/shard_map/send_weights/pallas_call | solution.py:272
  25.7 138.5 %train.1 = (f32[8192,256]{1,0:T(8,128)}, f32[2048,128]{1,0:T(8,128)}, f32[2048,128]{1,0:T(8,128)}, f32[2048,128]{1,0:T(8,128)}, f32[2048,128]{1,0:T(8,128)}) custom-call(bf16[8192,256]{1,0:T(8,128)(2,1)} %lat_ref.1, s32[8192]{0:T(1024)} %code_ref.1, s32[8192]{0:T(1024)} %weight_ref.1, s32[8192]{0:T(1024)} %value_ref.1, s32[8192]{0:T(1024)} %reward_ref.1, ...), custom_call_target="tpu_custom_call" | custom-call | tf_op jit(solution)/shard_map/train/pallas_call | solution.py:881
  164.2 29.7 %reduce_grads.1.own = f32[264,128]{1,0:T(8,128)} custom-call(f32[32,64,128]{2,1,0:T(8,128)} %bitcast.43, f32[32,64,128]{2,1,0:T(8,128)} %bitcast.44, f32[32,64,128]{2,1,0:T(8,128)} %bitcast.45, f32[32,64,128]{2,1,0:T(8,128)} %bitcast.46), custom_call_target="tpu_custom_call" | custom-call | tf_op jit(solution)/shard_map/reduce_grads/pallas_call | solution.py:401
  193.9 0.0 copy-done.11
  193.9 0.0 copy-done.3
  193.9 0.0 copy-done.1
  193.9 0.0 copy-done.16
  193.9 0.0 copy-done.15
  193.9 0.0 copy-done.18
  194.0 0.0 copy-done.17
  194.0 0.0 copy-done.12
  194.0 0.0 copy-done.10
  194.0 0.0 copy-done.9
  194.0 0.0 copy-done.8
  194.0 0.0 copy-done.7
  194.0 0.0 copy-done.2
  194.0 0.0 copy-done.6
  194.0 0.0 copy-done.5
  194.0 0.0 copy-done.14
  194.1 0.0 copy-done.13
  194.1 0.0 copy-done.4
  194.1 0.0 copy-start
  194.1 0.9 copy-done
  195.0 1.1 update.1
Async XLA Ops:
  0.7 193.2 %copy-start.11 = (f32[5,2,8]{2,1,0:T(2,128)S(1)}, f32[5,2,8]{2,1,0:T(2,128)}, u32[]{:S(2)}) copy-start(f32[5,2,8]{2,1,0:T(2,128)} %refs_15_.1) | copy-start | bytes 964
  0.7 193.2 %copy-start.3 = (f32[8,1238]{1,0:T(8,128)S(1)}, f32[8,1238]{1,0:T(8,128)}, u32[]{:S(2)}) copy-start(f32[8,1238]{1,0:T(8,128)} %refs_9_.1) | copy-start | bytes 118852
  0.7 193.2 %copy-start.1 = (f32[4,32,64]{2,1,0:T(8,128)S(1)}, f32[4,32,64]{2,1,0:T(8,128)}, u32[]{:S(2)}) copy-start(f32[4,32,64]{2,1,0:T(8,128)} %refs_3_.3) | copy-start | bytes 98308
  0.7 193.2 %copy-start.16 = (f32[5,2,8]{2,1,0:T(2,128)S(1)}, f32[5,2,8]{2,1,0:T(2,128)}, u32[]{:S(2)}) copy-start(f32[5,2,8]{2,1,0:T(2,128)} %refs_17_.1) | copy-start | bytes 964
  0.7 193.2 %copy-start.15 = (f32[5,2,8]{2,1,0:T(2,128)S(1)}, f32[5,2,8]{2,1,0:T(2,128)}, u32[]{:S(2)}) copy-start(f32[5,2,8]{2,1,0:T(2,128)} %refs_16_.1) | copy-start | bytes 964
  0.7 193.2 %copy-start.18 = (f32[32,8]{0,1:T(8,128)S(1)}, f32[32,8]{0,1:T(8,128)}, u32[]{:S(2)}) copy-start(f32[32,8]{0,1:T(8,128)} %param.46) | copy-start | bytes 3076
  0.7 193.2 %copy-start.17 = (f32[32,8]{0,1:T(8,128)S(1)}, f32[32,8]{0,1:T(8,128)}, u32[]{:S(2)}) copy-start(f32[32,8]{0,1:T(8,128)} %param.45) | copy-start | bytes 3076
  0.7 193.2 %copy-start.12 = (f32[32,8]{0,1:T(8,128)S(1)}, f32[32,8]{0,1:T(8,128)}, u32[]{:S(2)}) copy-start(f32[32,8]{0,1:T(8,128)} %param.44) | copy-start | bytes 3076
  0.8 193.2 %copy-start.10 = (f32[8,1238]{1,0:T(8,128)S(1)}, f32[8,1238]{1,0:T(8,128)}, u32[]{:S(2)}) copy-start(f32[8,1238]{1,0:T(8,128)} %refs_11_.1) | copy-start | bytes 118852
  0.8 193.2 %copy-start.9 = (f32[8,1238]{1,0:T(8,128)S(1)}, f32[8,1238]{1,0:T(8,128)}, u32[]{:S(2)}) copy-start(f32[8,1238]{1,0:T(8,128)} %refs_10_.1) | copy-start | bytes 118852
  0.8 193.2 %copy-start.8 = (f32[4,64,32]{1,2,0:T(8,128)S(1)}, f32[4,64,32]{1,2,0:T(8,128)}, u32[]{:S(2)}) copy-start(f32[4,64,32]{1,2,0:T(8,128)} %param.40) | copy-start | bytes 98308
  0.8 193.2 %copy-start.7 = (f32[4,64,32]{1,2,0:T(8,128)S(1)}, f32[4,64,32]{1,2,0:T(8,128)}, u32[]{:S(2)}) copy-start(f32[4,64,32]{1,2,0:T(8,128)} %param.39) | copy-start | bytes 98308
  0.8 193.2 %copy-start.2 = (f32[4,64,32]{1,2,0:T(8,128)S(1)}, f32[4,64,32]{1,2,0:T(8,128)}, u32[]{:S(2)}) copy-start(f32[4,64,32]{1,2,0:T(8,128)} %param.38) | copy-start | bytes 98308
  0.8 193.2 %copy-start.6 = (f32[4,32,64]{2,1,0:T(8,128)S(1)}, f32[4,32,64]{2,1,0:T(8,128)}, u32[]{:S(2)}) copy-start(f32[4,32,64]{2,1,0:T(8,128)} %refs_5_.3) | copy-start | bytes 98308
  0.8 193.2 %copy-start.5 = (f32[4,32,64]{2,1,0:T(8,128)S(1)}, f32[4,32,64]{2,1,0:T(8,128)}, u32[]{:S(2)}) copy-start(f32[4,32,64]{2,1,0:T(8,128)} %refs_4_.1) | copy-start | bytes 98308
  0.8 193.2 %copy-start.14 = (f32[64,32]{0,1:T(8,128)S(1)}, f32[64,32]{0,1:T(8,128)}, u32[]{:S(2)}) copy-start(f32[64,32]{0,1:T(8,128)} %param.34) | copy-start | bytes 24580
  0.8 193.2 %copy-start.13 = (f32[64,32]{0,1:T(8,128)S(1)}, f32[64,32]{0,1:T(8,128)}, u32[]{:S(2)}) copy-start(f32[64,32]{0,1:T(8,128)} %param.33) | copy-start | bytes 24580
  0.8 193.2 %copy-start.4 = (f32[64,32]{0,1:T(8,128)S(1)}, f32[64,32]{0,1:T(8,128)}, u32[]{:S(2)}) copy-start(f32[64,32]{0,1:T(8,128)} %param.32) | copy-start | bytes 24580
  194.1 0.9 copy-start

commit v5 on v3

--- a/solution.py
+++ b/solution.py
@@ -636,8 +636,16 @@
             total = fold_rows(total, part)
         return jnp.sum(total, axis=0, keepdims=True)
 
-    def norm_forward(layer, stream):
-        mean = folded(stream) * (1.0 / D)
+    marks = {}
+
+    def mark(index, what, row):
+        marks[index, what] = jnp.minimum(jnp.abs(row), 0.0)
+
+    def after(index, what, row):
+        return row if index == 0 else row + marks[index - 1, what]
+
+    def norm_forward(index, layer, stream):
+        mean = after(index, ("norm", layer), folded(stream) * (1.0 / D))
         centered = [part - mean for part in stream]
         rstd = lax.rsqrt(folded([part * part for part in centered]) * (1.0 / D) + eps_norm)
         values, slopes = [], []
@@ -647,10 +655,12 @@
             )
             values.append(value)
             slopes.append(slope)
+        mark(index, ("norm", layer), values[-1][0:1])
         return values, (centered, rstd, slopes)
 
-    def norm_backward(layer, grads, kept):
+    def norm_backward(index, layer, grads, kept):
         centered, rstd, slopes = kept
+        rstd = after(index, ("back", layer), rstd)
         wide = []
         for rows, grad, part, slope in zip(spans, grads, centered, slopes):
             grad = grad * slope
@@ -660,7 +670,9 @@
             wide.append(grad * norm_rows(2 * layer, rows.start))
         shift = folded(wide) * (1.0 / D)
         slant = folded([grad * part for grad, part in zip(wide, centered)]) * (1.0 / D) * (rstd * rstd)
-        return [(grad - shift) - part * slant for grad, part in zip(wide, centered)]
+        changes = [(grad - shift) - part * slant for grad, part in zip(wide, centered)]
+        mark(index, ("back", layer), changes[-1][0:1])
+        return changes
 
     acts, gateds, branches, inner_grads, lows, tops = ({} for _ in range(6))
 
@@ -677,11 +689,11 @@
         stream = pieces(dot_nt(stem_t[...], lat_ref[cols, :]) + dot_nn(table_t[...], hot))
         yield
         kept, inner_slopes = {}, {}
-        values, kept[0] = norm_forward(0, stream)
+        values, kept[0] = norm_forward(index, 0, stream)
         stream = [0.5 * value for value in values]
         yield
         for layer in range(1, LAYERS + 1):
-            values, kept[layer] = norm_forward(layer, stream)
+            values, kept[layer] = norm_forward(index, layer, stream)
             acts[index, layer] = joined([value.astype(BF) for value in values])
             yield
             inner = dot_nn(up_t[layer - 1], acts[index, layer])
@@ -714,7 +726,7 @@
             peak = None
             for part in parts:
                 peak = peak_rows(peak, part)
-            peak = jnp.max(peak, axis=0, keepdims=True)
+            peak = after(index, ("head", begin), jnp.max(peak, axis=0, keepdims=True))
             powers = [jnp.exp2((part - peak) * LOG2E) for part in parts]
             scale = coef / folded(powers)
             target = row_of(target_ref_of)
@@ -726,6 +738,7 @@
                 if missing:
                     soft = jnp.concatenate([soft, jnp.zeros((missing, LANES), F32)], axis=0)
                 low.append(soft.astype(BF))
+            mark(index, ("head", begin), scale)
             yield
         low.append(jnp.zeros((DEPTH - ROWS, LANES), BF))
         low = joined(low)
@@ -749,11 +762,11 @@
                 down_acc[layer - 1] += dot_nt(beside(branches, layer), beside(gateds, layer))
                 up_acc[layer - 1] += dot_nt(beside(acts, layer), beside(inner_grads, layer))
             yield
-            changes = norm_backward(layer, pieces(active_grad), kept[layer])
+            changes = norm_backward(index, layer, pieces(active_grad), kept[layer])
             stream = [part + change for part, change in zip(stream, changes)]
             yield
         values, slopes = kept[0][:2], [0.5 * slope for slope in kept[0][2]]
-        pre = joined([part.astype(BF) for part in norm_backward(0, stream, (*values, slopes))])
+        pre = joined([part.astype(BF) for part in norm_backward(index, 0, stream, (*values, slopes))])
         yield
         lat_grad[cols, :] = dot_tn(pre, stem_t[...])
         pre_last[:, cols] = pre
@@ -885,7 +898,7 @@
             pltpu.SemaphoreType.DMA((PARTS, packing.count * packing.part // D)),
         ],
         compiler_params=pltpu.CompilerParams(
-            dimension_semantics=("arbitrary",), vmem_limit_bytes=60 * 1024 * 1024
+            dimension_semantics=("arbitrary",), vmem_limit_bytes=62 * 1024 * 1024
         ),
         name="train",
     )(latent, code, weight, value, reward, action, target, *packed)

time: 177 us -> 177 us (level)
  no operation moved by 1% of the time
where the time goes in v5:
time: 177 us
  Pallas kernels  175 us (99%)
    pallas_call x1, Pallas kernels, train(): pl.pallas_call(functools.partial(train_kernel, packing, rows_all, chains)...  119 us
    pallas_call x1, Pallas kernels, reduce_grads(): pl.pallas_call(functools.partial(reduce_kernel, packing), out_shape=jax.S...  29.7 us
    pallas_call x1, Pallas kernels, send_weights(): pl.pallas_call(functools.partial(send_kernel, packing), out_shape=packing...  24.8 us

profile of v5, /device:TPU:0, one launch (start us, length us, event | category | flops | bytes accessed | tf_op | source)
XLA Modules:
  0.0 176.9 jit_solution(2696990495125464734)
XLA Ops:
  0.7 0.0 copy-start.11
  0.7 0.0 copy-start.3
  0.7 0.0 copy-start.1
  0.7 0.0 copy-start.16
  0.7 0.0 copy-start.15
  0.7 0.0 copy-start.18
  0.7 0.0 copy-start.17
  0.7 0.0 copy-start.12
  0.8 0.0 copy-start.10
  0.8 0.0 copy-start.9
  0.8 0.0 copy-start.8
  0.8 0.0 copy-start.7
  0.8 0.0 copy-start.2
  0.8 0.0 copy-start.6
  0.8 0.0 copy-start.5
  0.8 0.0 copy-start.14
  0.8 0.0 copy-start.13
  0.8 0.0 copy-start.4
  0.9 24.8 %send_weights.1 = (bf16[32,64,128]{2,1,0:T(8,128)(2,1)}, bf16[32,64,128]{2,1,0:T(8,128)(2,1)}, bf16[32,64,128]{2,1,0:T(8,128)(2,1)}, bf16[32,64,128]{2,1,0:T(8,128)(2,1)}) custom-call(f32[32,64]{1,0:T(8,128)} %bitcast.33, f32[4,32,64]{2,1,0:T(8,128)} %refs_3_.3, f32[4,32,64]{2,1,0:T(8,128)} %bitcast.31, f32[8,1238]{1,0:T(8,128)} %refs_9_.1, ...), custom_call_target="tpu_custom_call" | custom-call | tf_op jit(solution)/shard_map/send_weights/pallas_call | solution.py:272
  25.7 119.4 %train.1 = (f32[8192,256]{1,0:T(8,128)}, f32[2048,128]{1,0:T(8,128)}, f32[2048,128]{1,0:T(8,128)}, f32[2048,128]{1,0:T(8,128)}, f32[2048,128]{1,0:T(8,128)}) custom-call(bf16[8192,256]{1,0:T(8,128)(2,1)} %lat_ref.1, s32[8192]{0:T(1024)} %code_ref.1, s32[8192]{0:T(1024)} %weight_ref.1, s32[8192]{0:T(1024)} %value_ref.1, s32[8192]{0:T(1024)} %reward_ref.1, ...), custom_call_target="tpu_custom_call" | custom-call | tf_op jit(solution)/shard_map/train/pallas_call | solution.py:869
  145.1 29.7 %reduce_grads.1.own = f32[264,128]{1,0:T(8,128)} custom-call(f32[32,64,128]{2,1,0:T(8,128)} %bitcast.43, f32[32,64,128]{2,1,0:T(8,128)} %bitcast.44, f32[32,64,128]{2,1,0:T(8,128)} %bitcast.45, f32[32,64,128]{2,1,0:T(8,128)} %bitcast.46), custom_call_target="tpu_custom_call" | custom-call | tf_op jit(solution)/shard_map/reduce_grads/pallas_call | solution.py:401
  174.7 0.0 copy-done.11
  174.7 0.0 copy-done.3
  174.8 0.0 copy-done.1
  174.8 0.0 copy-done.16
  174.8 0.0 copy-done.15
  174.8 0.0 copy-done.18
  174.8 0.0 copy-done.17
  174.8 0.0 copy-done.12
  174.8 0.0 copy-done.10
  174.8 0.0 copy-done.9
  174.8 0.0 copy-done.8
  174.8 0.0 copy-done.7
  174.9 0.0 copy-done.2
  174.9 0.0 copy-done.6
  174.9 0.0 copy-done.5
  174.9 0.0 copy-done.14
  174.9 0.0 copy-done.13
  174.9 0.0 copy-done.4
  174.9 0.0 copy-start
  174.9 0.9 copy-done
  175.8 1.1 update.1
Async XLA Ops:
  0.7 174.1 %copy-start.11 = (f32[5,2,8]{2,1,0:T(2,128)S(1)}, f32[5,2,8]{2,1,0:T(2,128)}, u32[]{:S(2)}) copy-start(f32[5,2,8]{2,1,0:T(2,128)} %refs_15_.1) | copy-start | bytes 964
  0.7 174.1 %copy-start.3 = (f32[8,1238]{1,0:T(8,128)S(1)}, f32[8,1238]{1,0:T(8,128)}, u32[]{:S(2)}) copy-start(f32[8,1238]{1,0:T(8,128)} %refs_9_.1) | copy-start | bytes 118852
  0.7 174.1 %copy-start.1 = (f32[4,32,64]{2,1,0:T(8,128)S(1)}, f32[4,32,64]{2,1,0:T(8,128)}, u32[]{:S(2)}) copy-start(f32[4,32,64]{2,1,0:T(8,128)} %refs_3_.3) | copy-start | bytes 98308
  0.7 174.1 %copy-start.16 = (f32[5,2,8]{2,1,0:T(2,128)S(1)}, f32[5,2,8]{2,1,0:T(2,128)}, u32[]{:S(2)}) copy-start(f32[5,2,8]{2,1,0:T(2,128)} %refs_17_.1) | copy-start | bytes 964
  0.7 174.1 %copy-start.15 = (f32[5,2,8]{2,1,0:T(2,128)S(1)}, f32[5,2,8]{2,1,0:T(2,128)}, u32[]{:S(2)}) copy-start(f32[5,2,8]{2,1,0:T(2,128)} %refs_16_.1) | copy-start | bytes 964
  0.7 174.1 %copy-start.18 = (f32[32,8]{0,1:T(8,128)S(1)}, f32[32,8]{0,1:T(8,128)}, u32[]{:S(2)}) copy-start(f32[32,8]{0,1:T(8,128)} %param.46) | copy-start | bytes 3076
  0.7 174.1 %copy-start.17 = (f32[32,8]{0,1:T(8,128)S(1)}, f32[32,8]{0,1:T(8,128)}, u32[]{:S(2)}) copy-start(f32[32,8]{0,1:T(8,128)} %param.45) | copy-start | bytes 3076
  0.7 174.1 %copy-start.12 = (f32[32,8]{0,1:T(8,128)S(1)}, f32[32,8]{0,1:T(8,128)}, u32[]{:S(2)}) copy-start(f32[32,8]{0,1:T(8,128)} %param.44) | copy-start | bytes 3076
  0.8 174.1 %copy-start.10 = (f32[8,1238]{1,0:T(8,128)S(1)}, f32[8,1238]{1,0:T(8,128)}, u32[]{:S(2)}) copy-start(f32[8,1238]{1,0:T(8,128)} %refs_11_.1) | copy-start | bytes 118852
  0.8 174.1 %copy-start.9 = (f32[8,1238]{1,0:T(8,128)S(1)}, f32[8,1238]{1,0:T(8,128)}, u32[]{:S(2)}) copy-start(f32[8,1238]{1,0:T(8,128)} %refs_10_.1) | copy-start | bytes 118852
  0.8 174.1 %copy-start.8 = (f32[4,64,32]{1,2,0:T(8,128)S(1)}, f32[4,64,32]{1,2,0:T(8,128)}, u32[]{:S(2)}) copy-start(f32[4,64,32]{1,2,0:T(8,128)} %param.40) | copy-start | bytes 98308
  0.8 174.1 %copy-start.7 = (f32[4,64,32]{1,2,0:T(8,128)S(1)}, f32[4,64,32]{1,2,0:T(8,128)}, u32[]{:S(2)}) copy-start(f32[4,64,32]{1,2,0:T(8,128)} %param.39) | copy-start | bytes 98308
  0.8 174.1 %copy-start.2 = (f32[4,64,32]{1,2,0:T(8,128)S(1)}, f32[4,64,32]{1,2,0:T(8,128)}, u32[]{:S(2)}) copy-start(f32[4,64,32]{1,2,0:T(8,128)} %param.38) | copy-start | bytes 98308
  0.8 174.1 %copy-start.6 = (f32[4,32,64]{2,1,0:T(8,128)S(1)}, f32[4,32,64]{2,1,0:T(8,128)}, u32[]{:S(2)}) copy-start(f32[4,32,64]{2,1,0:T(8,128)} %refs_5_.3) | copy-start | bytes 98308
  0.8 174.1 %copy-start.5 = (f32[4,32,64]{2,1,0:T(8,128)S(1)}, f32[4,32,64]{2,1,0:T(8,128)}, u32[]{:S(2)}) copy-start(f32[4,32,64]{2,1,0:T(8,128)} %refs_4_.1) | copy-start | bytes 98308
  0.8 174.1 %copy-start.14 = (f32[64,32]{0,1:T(8,128)S(1)}, f32[64,32]{0,1:T(8,128)}, u32[]{:S(2)}) copy-start(f32[64,32]{0,1:T(8,128)} %param.34) | copy-start | bytes 24580
  0.8 174.1 %copy-start.13 = (f32[64,32]{0,1:T(8,128)S(1)}, f32[64,32]{0,1:T(8,128)}, u32[]{:S(2)}) copy-start(f32[64,32]{0,1:T(8,128)} %param.33) | copy-start | bytes 24580
  0.8 174.1 %copy-start.4 = (f32[64,32]{0,1:T(8,128)S(1)}, f32[64,32]{0,1:T(8,128)}, u32[]{:S(2)}) copy-start(f32[64,32]{0,1:T(8,128)} %param.32) | copy-start | bytes 24580
  174.9 0.9 copy-start
